TPU v7x, 256 devices: a whole 4x4x8 slice. The times are simulated.
256 devices in a mesh: dp: 8 (over x, z_hi), ctx: 32 (over z_lo, y, core).
Axes of the slice: x: 4, y: 4, z: 8 (z_hi: 2, z_lo: 4; z = z_hi * 4 + z_lo), core: 2. Of those that a mesh axis runs over, the one named last changes fastest.
Arguments:
- proj: bfloat16 [8, 4096, 12288], P('dp', 'ctx'), may hold values from -6 to 6
- filters: float32 [4096, 4096], P('ctx'), may hold values from -0.09375 to 0.09375
- cotangent: bfloat16 [8, 4096, 4096], P('dp', 'ctx'), may hold values from -6 to 6
Outputs:
- gated: bfloat16 [8, 4096, 4096], P('dp', 'ctx')
- grad_proj: bfloat16 [8, 4096, 12288], P('dp', 'ctx')
- filter_grad: float32 [4096, 4096], P('ctx')
All inputs are finite; a program needn't handle non-finite values.
Results may differ from a plain program's by a relative error of at most 0.017.
Values may be sent and summed in bfloat16 or wider, within the bound.
No kernel may reach another device: no remote copies, remote signals or barrier semaphores. Data moves between devices by JAX's collectives and lax.ppermute only.
A program may use at most 192 MiB of HBM per device.

v0:
```python
import math

import jax
import jax.numpy as jnp
from jax import lax
from jax.sharding import PartitionSpec as P

HIGHEST_PRECISION = lax.Precision.HIGHEST


def dft_tables(row_count, col_count, period):
    products = lax.broadcasted_iota(jnp.int32, (row_count, col_count), 0) * lax.broadcasted_iota(
        jnp.int32, (row_count, col_count), 1
    )
    phases = (products % period).astype(jnp.float32) * (2.0 * math.pi / period)
    return (jnp.cos(phases), jnp.sin(phases))


def split_parts(packed):
    return (packed[..., :128], packed[..., 128:])


def pack_parts(real_part, imag_part):
    return jnp.concatenate([real_part, imag_part], axis=-1)


def spectrum(signal):
    channels, length = signal.shape
    half_rows = length // 128
    row_count = 2 * half_rows
    blocks = signal.reshape(channels, half_rows, 128)
    first_cos, first_sin = dft_tables(row_count, half_rows, row_count)
    first_table = jnp.stack([first_cos, -first_sin], axis=0)
    stacked = jnp.einsum("tnk,ckm->ctnm", first_table, blocks, precision=HIGHEST_PRECISION)
    real_part = stacked[:, 0]
    imag_part = stacked[:, 1]
    spin_cos, spin_sin = dft_tables(row_count, 128, 2 * length)
    turned = pack_parts(
        real_part * spin_cos + imag_part * spin_sin, imag_part * spin_cos - real_part * spin_sin
    )
    last_cos, last_sin = dft_tables(128, 128, 128)
    last_table = jnp.concatenate(
        [
            jnp.concatenate([last_cos, -last_sin], axis=1),
            jnp.concatenate([last_sin, last_cos], axis=1),
        ],
        axis=0,
    )
    return jnp.einsum("cnm,mj->cnj", turned, last_table, precision=HIGHEST_PRECISION)


def signal_of(packed, both_parts):
    channels, row_count, _ = packed.shape
    half_rows = row_count // 2
    period = row_count * 128
    last_cos, last_sin = dft_tables(128, 128, 128)
    inner_table = jnp.concatenate(
        [
            jnp.concatenate([last_cos, last_sin], axis=1),
            jnp.concatenate([-last_sin, last_cos], axis=1),
        ],
        axis=0,
    )
    inner = jnp.einsum("cnm,mj->cnj", packed, inner_table, precision=HIGHEST_PRECISION)
    inner_real, inner_imag = split_parts(inner)
    spin_cos, spin_sin = dft_tables(row_count, 128, period)
    turned = jnp.stack(
        [
            inner_real * spin_cos - inner_imag * spin_sin,
            inner_imag * spin_cos + inner_real * spin_sin,
        ],
        axis=1,
    )
    back_cos, back_sin = dft_tables(half_rows, row_count, row_count)
    if both_parts:
        back_table = jnp.stack(
            [jnp.stack([back_cos, -back_sin], axis=1), jnp.stack([back_sin, back_cos], axis=1)],
            axis=0,
        )
        output = (
            jnp.einsum("ohtr,ctrm->cohm", back_table, turned, precision=HIGHEST_PRECISION) / period
        )
        return (
            output[:, 0].reshape(channels, half_rows * 128),
            output[:, 1].reshape(channels, half_rows * 128),
        )
    back_table = jnp.stack([back_cos, -back_sin], axis=1)
    output = jnp.einsum("htr,ctrm->chm", back_table, turned, precision=HIGHEST_PRECISION) / period
    return output.reshape(channels, half_rows * 128)


def convolve_lanes(filter_spec, mixed_lanes):
    mixed_spec = spectrum(mixed_lanes.astype(jnp.float32))
    mixed_real, mixed_imag = split_parts(mixed_spec)
    filter_real, filter_imag = split_parts(filter_spec)
    product = pack_parts(
        mixed_real * filter_real - mixed_imag * filter_imag,
        mixed_real * filter_imag + mixed_imag * filter_real,
    )
    conv_lanes = signal_of(product, False).astype(jnp.bfloat16)
    return (conv_lanes, mixed_spec)


def backward_lanes(filter_spec, mixed_spec, grad_lanes):
    grad_spec = spectrum(grad_lanes.astype(jnp.float32))
    grad_real, grad_imag = split_parts(grad_spec)
    filter_real, filter_imag = split_parts(filter_spec)
    mixed_real, mixed_imag = split_parts(mixed_spec)
    first_real = filter_real * grad_real + filter_imag * grad_imag
    first_imag = filter_real * grad_imag - filter_imag * grad_real
    second_real = mixed_real * grad_real + mixed_imag * grad_imag
    second_imag = mixed_real * grad_imag - mixed_imag * grad_real
    joined = pack_parts(first_real - second_imag, first_imag + second_real)
    grad_mixed_wide, filter_local = signal_of(joined, True)
    return (grad_mixed_wide.astype(jnp.bfloat16), filter_local)


def body(proj, filters, cotangent):
    seq_proj = proj[0]
    seq_grad = cotangent[0]
    local_rows = seq_proj.shape[0]
    channel_count = seq_grad.shape[1]
    ctx_count = lax.axis_size("ctx")
    replica_count = lax.axis_size("dp")
    seq_length = local_rows * ctx_count
    grad_scale = 1.0 / math.sqrt(replica_count * seq_length)
    filter_spec = spectrum(filters)
    query_part = seq_proj[:, :channel_count].astype(jnp.float32)
    key_part = seq_proj[:, channel_count : 2 * channel_count].astype(jnp.float32)
    value_part = seq_proj[:, 2 * channel_count :].astype(jnp.float32)
    mixed = (key_part * value_part).astype(jnp.bfloat16)
    mixed_lanes = lax.all_to_all(mixed, "ctx", split_axis=1, concat_axis=0, tiled=True).T
    conv_lanes, mixed_spec = convolve_lanes(filter_spec, mixed_lanes)
    conv_wide = lax.all_to_all(conv_lanes.T, "ctx", split_axis=0, concat_axis=1, tiled=True).astype(
        jnp.float32
    )
    gated = (query_part * conv_wide).astype(jnp.bfloat16)
    grad_wide = seq_grad.astype(jnp.float32)
    grad_conv = (grad_wide * query_part).astype(jnp.bfloat16)
    grad_query = grad_wide * conv_wide
    grad_lanes = lax.all_to_all(grad_conv, "ctx", split_axis=1, concat_axis=0, tiled=True).T
    grad_mixed_lanes, filter_local = backward_lanes(filter_spec, mixed_spec, grad_lanes)
    grad_mixed = lax.all_to_all(
        grad_mixed_lanes.T, "ctx", split_axis=0, concat_axis=1, tiled=True
    ).astype(jnp.float32)
    grad_out = jnp.concatenate(
        [grad_query, grad_mixed * value_part, grad_mixed * key_part], axis=1
    ).astype(jnp.bfloat16)
    filter_grad = lax.psum(filter_local.astype(jnp.bfloat16), "dp").astype(jnp.float32) * grad_scale
    return (gated[None], grad_out[None], filter_grad)


def solution(mesh):
    return jax.shard_map(
        body,
        mesh=mesh,
        in_specs=(P("dp", "ctx", None), P("ctx", None), P("dp", "ctx", None)),
        out_specs=(P("dp", "ctx", None), P("dp", "ctx", None), P("ctx", None)),
        check_vma=False,
    )
```

profile of v0, /device:TPU:1, one launch (start us, length us, event | category | flops | bytes accessed | tf_op | source)
XLA Modules:
  0.0 436.3 jit_solution(11887351191809282192)
XLA Ops:
  7.2 3.5 copy.36
  10.7 2.3 copy.46
  12.9 3.1 fusion.20
  16.0 2.3 copy.47
  18.3 10.2 %all-to-all-start.2 = ((bf16[128,32,128]{2,0,1:T(8,128)(2,1)}), bf16[128,32,128]{2,0,1:T(8,128)(2,1)}, u32[]{:S(2)}, u32[]{:S(2)}) async-start(bf16[128,32,128]{2,0,1:T(8,128)(2,1)} %copy.47), calls=%async_computation.2 | async-start | bytes 2097152 | tf_op jit(solution)/shard_map/all_to_all | solution.py:141
  28.5 2.3 copy.37
  30.8 24.4 %all-to-all-done.2 = bf16[128,32,128]{2,0,1:T(8,128)(2,1)} async-done(((bf16[128,32,128]{2,0,1:T(8,128)(2,1)}), bf16[128,32,128]{2,0,1:T(8,128)(2,1)}, u32[]{:S(2)}, u32[]{:S(2)}) %all-to-all-start.2) | async-done | bytes 1048608 | tf_op jit(solution)/shard_map/all_to_all | solution.py:141
  55.2 5.6 %all-to-all-start = ((bf16[128,32,128]{2,0,1:T(8,128)(2,1)}), bf16[128,32,128]{2,0,1:T(8,128)(2,1)}, u32[]{:S(2)}, u32[]{:S(2)}) async-start(bf16[128,32,128]{2,0,1:T(8,128)(2,1)} %copy.37), calls=%async_computation | async-start | bytes 2097152 | tf_op jit(solution)/shard_map/all_to_all | solution.py:132
  60.8 2.0 copy.72
  62.8 0.1 fusion.80
  62.9 0.1 sine_negate_fusion
  63.0 0.1 fusion.77
  63.1 0.1 fusion.71
  63.2 0.3 fusion.61
  63.5 0.3 fusion.56
  63.7 9.0 %convolution_bitcast_fusion.1 = f32[128,2,64,128]{3,2,0,1:T(8,128)} fusion(f32[128,32,128,1]{2,1,0,3:T(8,128)S(1)} %bitcast.172, f32[1,64,32]{1,2,0:T(8,128)S(1)} %get-tuple-element.34, f32[1,64,32]{1,2,0:T(8,128)S(1)} %get-tuple-element.35), kind=kOutput, calls=%fused_computation.45 | convolution fusion | flops 805310464 | bytes 10502144 | tf_op jit(solution)/shard_map/tnk,ckm->ctnm/dot_general | solution.py:34
  72.8 2.3 copy.48
  75.0 1.5 copy.74
  76.5 5.7 %convolution_bitcast_fusion = f32[128,2,64,128]{3,2,0,1:T(8,128)} fusion(bf16[128,32,128,1]{2,1,0,3:T(8,128)(2,1)S(1)} %bitcast.176, f32[1,64,32]{1,2,0:T(8,128)S(1)} %get-tuple-element.34, f32[1,64,32]{1,2,0:T(8,128)S(1)} %get-tuple-element.35), kind=kOutput, calls=%fused_computation.44 | convolution fusion | flops 805310464 | bytes 9453568 | tf_op jit(solution)/shard_map/tnk,ckm->ctnm/dot_general | solution.py:34
  82.1 5.1 %all-to-all-done = bf16[128,32,128]{2,0,1:T(8,128)(2,1)} async-done(((bf16[128,32,128]{2,0,1:T(8,128)(2,1)}), bf16[128,32,128]{2,0,1:T(8,128)(2,1)}, u32[]{:S(2)}, u32[]{:S(2)}) %all-to-all-start) | async-done | bytes 1048608 | tf_op jit(solution)/shard_map/all_to_all | solution.py:132
  87.3 2.3 copy.38
  89.5 1.5 copy.71
  91.0 5.7 %convolution_bitcast_fusion.2 = f32[128,2,64,128]{3,2,1,0:T(8,128)} fusion(bf16[128,32,128,1]{2,1,0,3:T(8,128)(2,1)S(1)} %bitcast.174, f32[1,64,32]{1,2,0:T(8,128)S(1)} %get-tuple-element.34, f32[1,64,32]{1,2,0:T(8,128)S(1)} %get-tuple-element.35), kind=kOutput, calls=%fused_computation.46 | convolution fusion | flops 805310464 | bytes 9453568 | tf_op jit(solution)/shard_map/tnk,ckm->ctnm/dot_general | solution.py:34
  96.7 16.4 %multiply_add_fusion = (f32[128,64,128]{2,1,0:T(8,128)}, f32[128,64,128]{2,1,0:T(8,128)}, f32[128,64,128]{2,1,0:T(8,128)}, f32[128,64,128]{2,1,0:T(8,128)}, f32[128,64,128]{2,1,0:T(8,128)}, /*index=5*/f32[128,64,128]{2,1,0:T(8,128)}) fusion(f32[128,2,64,128]{3,2,0,1:T(8,128)} %convolution_bitcast_fusion, f32[64,128]{1,0:T(8,128)S(1)} %get-tuple-element.36, ...), kind=kLoop, calls=%fused_computation.35 | loop fusion | flops 18874368 | bytes 50397184 | tf_op jit(solution)/shard_map/add | solution.py:39
  113.2 7.9 %pad_maximum_fusion = f32[128,64,256]{2,1,0:T(8,128)} fusion(f32[128,64,128]{2,1,0:T(8,128)} %get-tuple-element.30, f32[128,64,128]{2,1,0:T(8,128)} %get-tuple-element.31), kind=kLoop, calls=%fused_computation | loop fusion | flops 2097152 | bytes 16777216 | tf_op jit(solution)/shard_map/concatenate | solution.py:24
  121.1 0.0 copy-done.2
  121.1 4.2 pad_maximum_fusion.1
  125.3 14.0 %fusion.14 = f32[128,64,256]{2,0,1:T(8,128)S(1)} fusion(f32[128,64,256]{2,1,0:T(8,128)} %pad_maximum_fusion, f32[128,128]{1,0:T(8,128)S(1)} %get-tuple-element.39, f32[128,128]{1,0:T(8,128)S(1)} %get-tuple-element.38, f32[128,128]{1,0:T(8,128)S(1)} %fusion.61), kind=kOutput, calls=%fused_computation.20 | convolution fusion | flops 6442647552 | bytes 16973824 | tf_op jit(solution)/shard_map/cnm,mj->cnj/dot_general | solution.py:49
  139.3 0.0 copy-done
  139.3 0.0 copy-start.1
  139.3 11.8 %fusion.12 = f32[128,64,256]{2,0,1:T(8,128)} fusion(f32[128,64,256]{2,1,0:T(8,128)S(1)} %copy-done, f32[128,128]{1,0:T(8,128)S(1)} %get-tuple-element.39, f32[128,128]{1,0:T(8,128)S(1)} %get-tuple-element.38, f32[128,128]{1,0:T(8,128)S(1)} %fusion.61), kind=kOutput, calls=%fused_computation.18 | convolution fusion | flops 6442647552 | bytes 16973824 | tf_op jit(solution)/shard_map/cnm,mj->cnj/dot_general | solution.py:49
  151.1 6.4 %pad_maximum_fusion.3 = f32[128,64,256]{2,1,0:T(8,128)} fusion(f32[128,64,128]{2,1,0:T(8,128)} %get-tuple-element.12, f32[128,64,128]{2,1,0:T(8,128)S(1)} %copy-done.1), kind=kLoop, calls=%fused_computation.7 | loop fusion | flops 2097152 | bytes 16777216 | tf_op jit(solution)/shard_map/concatenate | solution.py:24
  157.5 16.3 %fusion.10 = f32[128,64,256]{2,0,1:T(8,128)} fusion(f32[128,64,256]{2,1,0:T(8,128)} %pad_maximum_fusion.3, f32[128,128]{1,0:T(8,128)S(1)} %get-tuple-element.39, f32[128,128]{1,0:T(8,128)S(1)} %get-tuple-element.38, f32[128,128]{1,0:T(8,128)S(1)} %fusion.61), kind=kOutput, calls=%fused_computation.16 | convolution fusion | flops 6442647552 | bytes 16973824 | tf_op jit(solution)/shard_map/cnm,mj->cnj/dot_general | solution.py:49
  173.8 6.9 %multiply_add_fusion.1 = f32[128,64,128]{2,0,1:T(8,128)} fusion(f32[128,64,256]{2,0,1:T(8,128)} %fusion.12, f32[128,64,256]{2,0,1:T(8,128)S(1)} %fusion.14), kind=kLoop, calls=%fused_computation.38 | loop fusion | flops 3145728 | bytes 20971520 | tf_op jit(solution)/shard_map/add | solution.py:98
  180.7 11.2 %subtract_subtract_fusion = (f32[128,64,128]{2,0,1:T(8,128)}, f32[128,64,128]{2,0,1:T(8,128)}, f32[128,64,128]{2,0,1:T(8,128)}) fusion(f32[128,64,256]{2,0,1:T(8,128)} %fusion.10, f32[128,64,256]{2,0,1:T(8,128)} %fusion.12, f32[128,64,256]{2,0,1:T(8,128)S(1)} %fusion.14), kind=kLoop, calls=%fused_computation.33 | loop fusion | flops 17825792 | bytes 37748736 | tf_op jit(solution)/shard_map/sub | solution.py:113
  191.9 4.2 pad_maximum_fusion.2
  196.1 11.6 %fusion.8 = f32[128,64,256]{2,1,0:T(8,128)S(1)} fusion(f32[128,64,256]{2,0,1:T(8,128)S(1)} %pad_maximum_fusion.2, f32[128,128]{1,0:T(8,128)S(1)} %get-tuple-element.39, f32[128,128]{1,0:T(8,128)S(1)} %fusion.61, f32[128,128]{1,0:T(8,128)S(1)} %get-tuple-element.38), kind=kOutput, calls=%fused_computation.14 | convolution fusion | flops 6442647552 | bytes 16973824 | tf_op jit(solution)/shard_map/cnm,mj->cnj/dot_general | solution.py:64
  207.6 4.2 pad_maximum_fusion.4
  211.8 11.7 %fusion.6 = f32[128,64,256]{2,1,0:T(8,128)} fusion(f32[128,64,256]{2,0,1:T(8,128)S(1)} %pad_maximum_fusion.4, f32[128,128]{1,0:T(8,128)S(1)} %get-tuple-element.39, f32[128,128]{1,0:T(8,128)S(1)} %fusion.61, f32[128,128]{1,0:T(8,128)S(1)} %get-tuple-element.38), kind=kOutput, calls=%fused_computation.12 | convolution fusion | flops 6442647552 | bytes 16973824 | tf_op jit(solution)/shard_map/cnm,mj->cnj/dot_general | solution.py:64
  223.5 6.5 %subtract_bitcast_fusion = (f32[128,1,64,128]{3,2,0,1:T(8,128)}, f32[128,1,64,128]{3,2,0,1:T(8,128)}, f32[128,1,64,128]{3,2,0,1:T(8,128)S(1)}, f32[128,1,64,128]{3,2,0,1:T(8,128)S(1)}) fusion(f32[128,64,256]{2,1,0:T(8,128)} %fusion.6, f32[64,128]{1,0:T(8,128)S(1)} %get-tuple-element.36, f32[64,128]{1,0:T(8,128)S(1)} %get-tuple-element.37, ...), kind=kLoop, calls=%fused_computation.31 | loop fusion | flops 12582912 | bytes 33619968 | tf_op jit(solution)/shard_map/stack | solution.py:67
  230.1 4.7 %fusion.25 = bf16[128,128,32]{1,2,0:T(8,128)(2,1)S(1)} fusion(f32[128,1,64,128]{3,2,0,1:T(8,128)S(1)} %get-tuple-element.26, f32[128,1,64,128]{3,2,0,1:T(8,128)S(1)} %get-tuple-element.27, f32[32,1,64]{2,0,1:T(8,128)S(1)} %fusion.80, f32[32,1,64]{2,0,1:T(8,128)S(1)} %get-tuple-element.41), kind=kOutput, calls=%fused_computation.62 | convolution fusion | flops 808456192 | bytes 9453568 | tf_op jit(solution)/shard_map/htr,ctrm->chm/dot_general | solution.py:88
  234.8 1.4 copy.98
  236.2 2.4 copy.44
  238.6 5.3 %all-to-all-start.1 = ((bf16[32,128,128]{2,1,0:T(8,128)(2,1)}), bf16[32,128,128]{2,1,0:T(8,128)(2,1)}, u32[]{:S(2)}, u32[]{:S(2)}) async-start(bf16[32,128,128]{2,1,0:T(8,128)(2,1)} %bitcast.177), calls=%async_computation.1 | async-start | bytes 2097152 | tf_op jit(solution)/shard_map/all_to_all | solution.py:134
  243.9 0.0 all-reduce.2.cloned.1.call-start
  244.0 7.3 %fusion.26 = bf16[128,2,32,128]{3,2,1,0:T(8,128)(2,1)S(1)} fusion(f32[1,32,2,64]{3,1,2,0:T(8,128)S(1)} %get-tuple-element.33, f32[1,32,2,64]{3,1,2,0:T(8,128)S(1)} %get-tuple-element.32, f32[128,1,64,128]{3,2,0,1:T(8,128)} %get-tuple-element.10, f32[128,1,64,128]{3,2,0,1:T(8,128)} %get-tuple-element.9), kind=kOutput, calls=%fused_computation.64 | convolution fusion | flops 1614815232 | bytes 10518528 | tf_op jit(solution)/shard_map/ohtr,ctrm->cohm/dot_general | solution.py:81
  251.2 1.3 fusion.91
  252.6 1.5 copy.96
  254.0 0.0 all-reduce.2.cloned.1.call-update
  254.1 2.6 copy.97
  256.7 2.3 copy.54
  259.0 11.5 %all-to-all-done.1 = bf16[32,128,128]{2,1,0:T(8,128)(2,1)} async-done(((bf16[32,128,128]{2,1,0:T(8,128)(2,1)}), bf16[32,128,128]{2,1,0:T(8,128)(2,1)}, u32[]{:S(2)}, u32[]{:S(2)}) %all-to-all-start.1) | async-done | bytes 1048608 | tf_op jit(solution)/shard_map/all_to_all | solution.py:134
  270.5 9.2 %all-to-all-start.3 = ((bf16[32,128,128]{2,1,0:T(8,128)(2,1)}), bf16[32,128,128]{2,1,0:T(8,128)(2,1)}, u32[]{:S(2)}, u32[]{:S(2)}) async-start(bf16[32,128,128]{2,1,0:T(8,128)(2,1)} %bitcast.179), calls=%async_computation.3 | async-start | bytes 2097152 | tf_op jit(solution)/shard_map/all_to_all | solution.py:143
  279.8 114.7 %all-reduce.2.cloned.1.call-done = bf16[128,4096]{1,0:T(8,128)(2,1)} async-done(((bf16[128,4096]{1,0:T(8,128)(2,1)}), bf16[128,4096]{1,0:T(8,128)(2,1)}) %all-reduce.2.cloned.1.call-update) | async-done | bytes 1048592 | tf_op jit(solution)/shard_map/psum | solution.py:149
  394.5 2.8 convert_multiply_fusion.6
  397.2 2.3 copy.45
  399.5 1.5 convert_element_type.233
  400.9 2.4 fusion.24
  403.4 0.0 all-to-all-done.3
  403.4 2.3 copy.55
  405.6 3.3 fusion.23
  409.0 15.3 %pad_maximum_fusion.5 = bf16[1,128,12288]{1,2,0:T(8,128)(2,1)S(1)} fusion(bf16[1,128,4096]{1,2,0:T(8,128)(2,1)S(1)} %bitcast.190, bf16[1,128,4096]{1,2,0:T(8,128)(2,1)S(1)} %bitcast.189, bf16[1,128,4096]{1,2,0:T(8,128)(2,1)S(1)} %copy-done.4), kind=kLoop, calls=%fused_computation.47 | loop fusion | flops 9437184 | bytes 6291456 | tf_op jit(solution)/shard_map/concatenate | solution.py:146
  424.3 2.8 copy.57
  427.0 2.3 copy.56
  (8 shorter events, 0.0 us)
Async XLA Ops:
  18.3 36.9 %all-to-all-start.2 = ((bf16[128,32,128]{2,0,1:T(8,128)(2,1)}), bf16[128,32,128]{2,0,1:T(8,128)(2,1)}, u32[]{:S(2)}, u32[]{:S(2)}) async-start(bf16[128,32,128]{2,0,1:T(8,128)(2,1)} %copy.47), calls=%async_computation.2 | async-start | bytes 2097152 | tf_op jit(solution)/shard_map/all_to_all | solution.py:141
  55.2 32.1 %all-to-all-start = ((bf16[128,32,128]{2,0,1:T(8,128)(2,1)}), bf16[128,32,128]{2,0,1:T(8,128)(2,1)}, u32[]{:S(2)}, u32[]{:S(2)}) async-start(bf16[128,32,128]{2,0,1:T(8,128)(2,1)} %copy.37), calls=%async_computation | async-start | bytes 2097152 | tf_op jit(solution)/shard_map/all_to_all | solution.py:132
  113.2 7.9 %copy-start.2 = (f32[128,64,128]{2,1,0:T(8,128)S(1)}, f32[128,64,128]{2,1,0:T(8,128)}, u32[]{:S(2)}) copy-start(f32[128,64,128]{2,1,0:T(8,128)} %get-tuple-element.28) | copy-start | bytes 12582916
  113.2 7.9 %copy-start.3 = (f32[128,64,128]{2,1,0:T(8,128)S(1)}, f32[128,64,128]{2,1,0:T(8,128)}, u32[]{:S(2)}) copy-start(f32[128,64,128]{2,1,0:T(8,128)} %get-tuple-element.29) | copy-start | bytes 12582916
  125.3 14.0 %copy-start = (f32[128,64,256]{2,1,0:T(8,128)S(1)}, f32[128,64,256]{2,1,0:T(8,128)}, u32[]{:S(2)}) copy-start(f32[128,64,256]{2,1,0:T(8,128)} %pad_maximum_fusion.1) | copy-start | bytes 25165828
  139.3 11.8 %copy-start.1 = (f32[128,64,128]{2,1,0:T(8,128)S(1)}, f32[128,64,128]{2,1,0:T(8,128)}, u32[]{:S(2)}) copy-start(f32[128,64,128]{2,1,0:T(8,128)} %get-tuple-element.11) | copy-start | bytes 12582916
  238.6 31.9 %all-to-all-start.1 = ((bf16[32,128,128]{2,1,0:T(8,128)(2,1)}), bf16[32,128,128]{2,1,0:T(8,128)(2,1)}, u32[]{:S(2)}, u32[]{:S(2)}) async-start(bf16[32,128,128]{2,1,0:T(8,128)(2,1)} %bitcast.177), calls=%async_computation.1 | async-start | bytes 2097152 | tf_op jit(solution)/shard_map/all_to_all | solution.py:134
  243.9 150.6 %all-reduce.2.cloned.1.call-start = ((), (), s32[]{:S(2)}) async-start(), calls=%async_computation.4 | async-start | bytes 2097152 | tf_op jit(solution)/shard_map/psum | solution.py:149
  270.5 132.9 %all-to-all-start.3 = ((bf16[32,128,128]{2,1,0:T(8,128)(2,1)}), bf16[32,128,128]{2,1,0:T(8,128)(2,1)}, u32[]{:S(2)}, u32[]{:S(2)}) async-start(bf16[32,128,128]{2,1,0:T(8,128)(2,1)} %bitcast.179), calls=%async_computation.3 | async-start | bytes 2097152 | tf_op jit(solution)/shard_map/all_to_all | solution.py:143
  405.6 3.3 copy-start.4
Sparse Core Ops, SparseCore 0:
  254.2 140.2 all-reduce.1
where the time goes:
time: 440 us; the launch traced here: 436 us
  waiting for transfers between devices  156 us (35%)
  matrix products  97.7 us (22%)
  other arithmetic  97.3 us (22%)
  local copies, waits for them, and re-layouts  40.8 us (9%)
  starting transfers between devices  30.4 us (7%)
  between operations  14.4 us (3%)
    psum x1, waiting for transfers between devices, body(): lax.psum(filter_local.astype(jnp.bfloat16), 'dp').astype(jnp.float32)  115 us
    dot_general x3, matrix products, spectrum(): jnp.einsum('cnm,mj->cnj', turned, last_table, precision=HIGHEST_PRECISION)  42 us
    concatenate x5, other arithmetic, pack_parts(): return jnp.concatenate([real_part, imag_part], axis=-1)  26.9 us
    all_to_all x1, waiting for transfers between devices, body(): lax.all_to_all(grad_conv, 'ctx', split_axis=1, concat_axis=0, tiled=True)  24.4 us
    dot_general x2, matrix products, signal_of(): jnp.einsum('cnm,mj->cnj', packed, inner_table, precision=HIGHEST_PRECISION)  23.3 us
    unnamed x20, local copies, waits for them, and re-layouts  21.2 us
    dot_general x3, matrix products, spectrum(): jnp.einsum('tnk,ckm->ctnm', first_table, blocks, precision=HIGHEST_PRECIS...  20.4 us
    add x1, other arithmetic, spectrum(): real_part * spin_cos + imag_part * spin_sin  16.4 us
  transfers between devices with their start and end apart: 5, of which 4 were waited for; matrix products, arithmetic and copies ran while one was open for 11% of the time, Pallas kernels for 0%

commit v1 on v0

v1 whole, which is shorter than its diff:
```python
import math

import jax
import jax.numpy as jnp
from jax import lax
from jax.experimental import pallas as pl
from jax.experimental.pallas import tpu as pltpu
from jax.sharding import PartitionSpec as P

F32 = jnp.float32
BF16 = jnp.bfloat16
LANES = 128
CHANS = 16
SEQS = 8
BLOCKS = 32
LENGTH = BLOCKS * LANES
ROWS = BLOCKS * SEQS
GROUPS = BLOCKS // 4
MIB = 1 << 20


def params(mib):
    return pltpu.CompilerParams(vmem_limit_bytes=mib * MIB)


def cost(flops, moved):
    return pl.CostEstimate(flops=flops, bytes_accessed=moved, transcendentals=0)


PRE_Q = 4


def pre_kernel(query_ref, key_ref, value_ref, grad_ref, out_ref):
    for q in range(PRE_Q):
        cols = pl.ds(q * LANES, LANES)
        mixed = key_ref[0, :, cols].astype(F32) * value_ref[0, :, cols].astype(F32)
        grad = grad_ref[0, :, cols].astype(F32) * query_ref[0, :, cols].astype(F32)
        out_ref[:, q, :, 0:LANES] = mixed.T.astype(BF16).reshape(SEQS, CHANS, LANES)
        out_ref[:, q, :, LANES:] = grad.T.astype(BF16).reshape(SEQS, CHANS, LANES)


def pre(proj, cotangent):
    wide = PRE_Q * LANES
    steps = BLOCKS // PRE_Q

    def col(first):
        return pl.BlockSpec((1, LANES, wide), lambda i: (0, 0, first * steps + i))

    return pl.pallas_call(
        pre_kernel,
        grid=(steps,),
        in_specs=[col(0), col(1), col(2), col(0)],
        out_specs=pl.BlockSpec((SEQS, PRE_Q, CHANS, 2 * LANES), lambda i: (0, i, 0, 0)),
        out_shape=jax.ShapeDtypeStruct((SEQS, BLOCKS, CHANS, 2 * LANES), BF16),
        compiler_params=params(32),
        cost_estimate=cost(2 * LANES * LENGTH, 6 * MIB),
        name="gate_products",
    )(proj, proj, proj, cotangent)


def tile_kernel(filter_ref, out_ref, shifted_ref):
    lane = lax.broadcasted_iota(jnp.int32, (8, LANES), 1)

    @pl.when(pl.program_id(0) == 0)
    def _():
        wide_lane = lax.broadcasted_iota(jnp.int32, (CHANS, LENGTH), 1)
        for s in range(8):
            rolled = filter_ref[...] if s == 0 else pltpu.roll(filter_ref[...], s, 1)
            rolled = jnp.where(wide_lane < s, 0.0, rolled)
            for c in range(CHANS):
                shifted_ref[c, s : s + 1, :] = rolled[c : c + 1, :]

    base = shifted_ref[pl.program_id(0)]
    for pair in range(8):
        halves = []
        for g in (2 * pair, 2 * pair + 1):
            rolled = base if g == 0 else pltpu.roll(base, 8 * g, 1)
            first = jnp.where(lane < 8 * g, 0.0, rolled[:, :LANES])
            halves.append(jnp.concatenate([first, rolled[:, LANES:]], axis=1))
        rows = jnp.concatenate(halves, axis=0).astype(BF16)
        for d in range(BLOCKS):
            e, p, h = d // 4, d % 2, (d % 4) // 2
            out_ref[0, e, pl.ds(p * LANES + 16 * pair, 16), pl.ds(h * LANES, LANES)] = rows[
                :, d * LANES : (d + 1) * LANES
            ]


def toeplitz_tiles(filters):
    return pl.pallas_call(
        tile_kernel,
        grid=(CHANS,),
        in_specs=[pl.BlockSpec((CHANS, LENGTH), lambda t: (0, 0))],
        out_specs=pl.BlockSpec((1, GROUPS, 2 * LANES, 2 * LANES), lambda t: (t, 0, 0, 0)),
        out_shape=jax.ShapeDtypeStruct((CHANS, GROUPS, 2 * LANES, 2 * LANES), BF16),
        scratch_shapes=[pltpu.VMEM((CHANS, 8, LENGTH), F32)],
        compiler_params=params(32),
        cost_estimate=cost(CHANS * LENGTH * LANES, 17 * MIB),
        name="toeplitz_tiles",
    )(filters)


NT = (((1,), (1,)), ((), ()))


def conv_kernel(lanes_ref, tile_ref, out_ref, x2_ref, g3_ref, mixed_ref, grad_ref, conv_ref, back_ref, acc_ref):
    t = pl.program_id(0)

    @pl.when(t == 0)
    def _():
        mixed_ref[...] = lanes_ref[:, 0:LANES].astype(F32)
        grad_ref[...] = lanes_ref[:, LANES:].astype(F32)

    def rows_of(ref):
        return jnp.concatenate(
            [ref[pl.ds(r * CHANS + t, SEQS, stride=BLOCKS * CHANS), :] for r in range(BLOCKS)], axis=0
        )

    mixed = rows_of(mixed_ref)
    grad = rows_of(grad_ref)
    none = jnp.zeros((SEQS, LANES), F32)
    x2_ref[0] = jnp.concatenate([mixed, jnp.concatenate([none, mixed[:-SEQS]], axis=0)], axis=1).astype(BF16)
    g3_ref[0] = jnp.concatenate([grad, jnp.concatenate([grad[2 * SEQS :], none, none], axis=0)], axis=1).astype(BF16)

    for e in range(GROUPS):
        skip = 4 * SEQS * e
        out = jnp.dot(x2_ref[0, : ROWS - skip, :], tile_ref[0, e], preferred_element_type=F32)
        if e == 0:
            acc_ref[...] = out[:, :LANES]
        else:
            acc_ref[skip:, :] += out[:, :LANES]
        acc_ref[skip + 2 * SEQS :, :] += out[: -2 * SEQS, LANES:]
    for r in range(BLOCKS):
        conv_ref[pl.ds(r * CHANS + t, SEQS, stride=BLOCKS * CHANS), :] = acc_ref[r * SEQS : (r + 1) * SEQS, :]

    for e in range(GROUPS):
        skip = 4 * SEQS * e
        out = lax.dot_general(g3_ref[0, skip:, :], tile_ref[0, e], NT, preferred_element_type=F32)
        if e == 0:
            acc_ref[...] = out[:, :LANES]
        else:
            acc_ref[: ROWS - skip, :] += out[:, :LANES]
        acc_ref[: ROWS - skip - SEQS, :] += out[SEQS:, LANES:]
    for r in range(BLOCKS):
        back_ref[pl.ds(r * CHANS + t, SEQS, stride=BLOCKS * CHANS), :] = acc_ref[r * SEQS : (r + 1) * SEQS, :]

    @pl.when(t == CHANS - 1)
    def _():
        out_ref[:, 0:LANES] = conv_ref[...].astype(BF16)
        out_ref[:, LANES:] = back_ref[...].astype(BF16)


def convolve(lanes, tiles):
    rows = ROWS * CHANS
    whole = pl.BlockSpec((rows, 2 * LANES), lambda t: (0, 0))
    chan = pl.BlockSpec((1, ROWS, 2 * LANES), lambda t: (t, 0, 0))
    return pl.pallas_call(
        conv_kernel,
        grid=(CHANS,),
        in_specs=[whole, pl.BlockSpec((1, GROUPS, 2 * LANES, 2 * LANES), lambda t: (t, 0, 0, 0))],
        out_specs=[whole, chan, chan],
        out_shape=[
            jax.ShapeDtypeStruct((rows, 2 * LANES), BF16),
            jax.ShapeDtypeStruct((CHANS, ROWS, 2 * LANES), BF16),
            jax.ShapeDtypeStruct((CHANS, ROWS, 2 * LANES), BF16),
        ],
        scratch_shapes=[pltpu.VMEM((rows, LANES), F32)] * 4 + [pltpu.VMEM((ROWS, LANES), F32)],
        compiler_params=params(48),
        cost_estimate=cost(2 * 2 * CHANS * 1152 * 65536, 24 * MIB),
        name="convolve",
    )(lanes, tiles)


def filter_kernel(scale, x2_ref, g3_ref, out_ref, part_ref, acc_ref):
    t = pl.program_id(0)
    turned = x2_ref[0].astype(F32).T.astype(BF16)
    row = lax.broadcasted_iota(jnp.int32, (LANES, LANES), 0)
    lane = lax.broadcasted_iota(jnp.int32, (LANES, LANES), 1)
    for e in range(GROUPS):
        skip = 4 * SEQS * e
        out = jnp.dot(turned[:, : ROWS - skip], g3_ref[0, skip:, :], preferred_element_type=F32)
        for p in range(2):
            for h in range(2):
                d = 4 * e + p + 2 * h
                block = out[p * LANES : (p + 1) * LANES, h * LANES : (h + 1) * LANES]
                if d == 0:
                    block = jnp.where(lane < row, 0.0, block)
                part_ref[:, d * LANES : (d + 1) * LANES] = block
    total = part_ref[0:8, :]
    for g in range(1, 16):
        total += pltpu.roll(part_ref[8 * g : 8 * g + 8, :], LENGTH - 8 * g, 1)
    acc_ref[t] = total

    @pl.when(t == CHANS - 1)
    def _():
        result = None
        for s in range(8):
            piece = jnp.concatenate([acc_ref[c, s : s + 1, :] for c in range(CHANS)], axis=0)
            piece = piece if s == 0 else pltpu.roll(piece, LENGTH - s, 1)
            result = piece if result is None else result + piece
        out_ref[...] = (result * scale).astype(BF16)


def filter_gradient(x2, g3, scale):
    chan = pl.BlockSpec((1, ROWS, 2 * LANES), lambda t: (t, 0, 0))
    return pl.pallas_call(
        lambda *refs: filter_kernel(scale, *refs),
        grid=(CHANS,),
        in_specs=[chan, chan],
        out_specs=pl.BlockSpec((CHANS, LENGTH), lambda t: (0, 0)),
        out_shape=jax.ShapeDtypeStruct((CHANS, LENGTH), BF16),
        scratch_shapes=[pltpu.VMEM((LANES, LENGTH), F32), pltpu.VMEM((CHANS, 8, LENGTH), F32)],
        compiler_params=params(32),
        cost_estimate=cost(2 * CHANS * 1152 * 65536, 5 * MIB),
        name="filter_gradient",
    )(x2, g3)


POST_Q = 8


def post_kernel(lanes_ref, query_ref, key_ref, value_ref, grad_ref, gated_ref, out_ref, back_ref):
    j = pl.program_id(1)

    @pl.when(j == 0)
    def _():
        for q in range(POST_Q):
            cols = pl.ds(q * LANES, LANES)
            both = lanes_ref[:, q].reshape(LANES, 2 * LANES).astype(F32)
            conv = both[:, :LANES].T
            gated_ref[0, :, cols] = (query_ref[0, :, cols].astype(F32) * conv).astype(BF16)
            out_ref[0, :, cols] = (grad_ref[0, :, cols].astype(F32) * conv).astype(BF16)
            back_ref[:, cols] = both[:, LANES:].T

    @pl.when(j == 1)
    def _():
        out_ref[0] = (back_ref[...] * value_ref[0].astype(F32)).astype(BF16)

    @pl.when(j == 2)
    def _():
        out_ref[0] = (back_ref[...] * key_ref[0].astype(F32)).astype(BF16)


def post(lanes, proj, cotangent):
    wide = POST_Q * LANES
    steps = BLOCKS // POST_Q

    def col(first):
        return pl.BlockSpec((1, LANES, wide), lambda i, j: (0, 0, first * steps + i))

    return pl.pallas_call(
        post_kernel,
        grid=(steps, 3),
        in_specs=[
            pl.BlockSpec((SEQS, POST_Q, CHANS, 2 * LANES), lambda i, j: (0, i, 0, 0)),
            col(0),
            col(1),
            col(2),
            col(0),
        ],
        out_specs=[col(0), pl.BlockSpec((1, LANES, wide), lambda i, j: (0, 0, j * steps + i))],
        out_shape=[
            jax.ShapeDtypeStruct((1, LANES, LENGTH), BF16),
            jax.ShapeDtypeStruct((1, LANES, 3 * LENGTH), BF16),
        ],
        scratch_shapes=[pltpu.VMEM((LANES, wide), F32)],
        compiler_params=params(32),
        cost_estimate=cost(4 * LANES * LENGTH, 10 * MIB),
        name="gate_results",
    )(lanes, proj, proj, proj, cotangent)


def gather_dp(piece):
    place = lax.axis_index("dp")
    upper = place // 2
    other = lax.ppermute(piece, "dp", [(i, i ^ 1) for i in range(8)])
    pair = jnp.where(place % 2 == 0, jnp.concatenate([piece, other]), jnp.concatenate([other, piece]))
    whole = jnp.zeros((8 * CHANS, LENGTH), F32)
    whole = lax.dynamic_update_slice(whole, pair.astype(F32), (upper * 2 * CHANS, 0))
    for k in range(1, 4):
        came = lax.ppermute(pair, "dp", [(i, (i + 2 * k) % 8) for i in range(8)])
        whole = lax.dynamic_update_slice(whole, came.astype(F32), (((upper + 4 - k) % 4) * 2 * CHANS, 0))
    return whole


def body(proj, filters, cotangent):
    place = lax.axis_index("dp")
    scale = 1.0 / math.sqrt(SEQS * LENGTH)
    send = pre(proj, cotangent).reshape(SEQS * BLOCKS, CHANS, 2 * LANES)
    lanes = lax.all_to_all(send, ("dp", "ctx"), split_axis=0, concat_axis=0, tiled=True)
    tiles = toeplitz_tiles(lax.dynamic_slice(filters, (place * CHANS, 0), (CHANS, LENGTH)))
    results, x2, g3 = convolve(lanes.reshape(ROWS * CHANS, 2 * LANES), tiles)
    back = lax.all_to_all(
        results.reshape(ROWS, CHANS, 2 * LANES), ("dp", "ctx"), split_axis=0, concat_axis=0, tiled=True
    )
    filter_grad = gather_dp(filter_gradient(x2, g3, scale))
    gated, grad_proj = post(back.reshape(SEQS, BLOCKS, CHANS, 2 * LANES), proj, cotangent)
    return (gated, grad_proj, filter_grad)


def solution(mesh):
    return jax.shard_map(
        body,
        mesh=mesh,
        in_specs=(P("dp", "ctx", None), P("ctx", None), P("dp", "ctx", None)),
        out_specs=(P("dp", "ctx", None), P("dp", "ctx", None), P("ctx", None)),
        check_vma=False,
    )
```

time: 440 us -> 192 us (0.44)
  matrix products: 97.7 us -> 0 us
  other arithmetic: 97.3 us -> 4.55 us
  waiting for transfers between devices: 156 us -> 79.3 us
  Pallas kernels: 0 us -> 50.6 us
  local copies, waits for them, and re-layouts: 40.8 us -> 20.2 us
  between operations: 14.4 us -> 0.78 us
  starting transfers between devices: 30.4 us -> 35.8 us
    psum x1 -> x0, waiting for transfers between devices: 115 us -> none  [body(): lax.psum(filter_local.astype(jnp.bfloat16), 'dp').astype(jnp.float32)]
    dot_general x10 -> x0, matrix products: 97.7 us -> none  [the longest x3 42 us: spectrum(): jnp.einsum('cnm,mj->cnj', turned, last_table, precision=HIGHEST_PRECISION)]
    pallas_call x0 -> x5, Pallas kernels: none -> 50.6 us  [the longest x1 19.3 us: convolve(): pl.pallas_call(conv_kernel, grid=(CHANS,), in_specs=[whole, pl.BlockSpec(...]
    concatenate x6 -> x0, other arithmetic: 42.1 us -> none  [the longest x5 26.9 us: pack_parts(): return jnp.concatenate([real_part, imag_part], axis=-1)]
    ppermute x0 -> x4, waiting for transfers between devices: none -> 38.9 us  [the longest x1 30.4 us: gather_dp(): other = lax.ppermute(piece, 'dp', [(i, i ^ 1) for i in range(8)])]
    add x2 -> x0, other arithmetic: 23.4 us -> none  [the longest x1 16.4 us: spectrum(): real_part * spin_cos + imag_part * spin_sin]
    all_to_all x6 -> x0, local copies, waits for them, and re-layouts: 13.6 us -> none  [the longest x2 4.55 us: body(): lax.all_to_all(grad_conv, 'ctx', split_axis=1, concat_axis=0, tiled=True)]
    another operation x4 -> x0, other arithmetic: 12.3 us -> none  [the longest x1 6.54 us: signal_of(): jnp.stack([inner_real * spin_cos - inner_imag * spin_sin, inner_imag * sp...]
  transfers between devices with their start and end apart: 5 -> 6, of which waited for: 4 -> 4; matrix products, arithmetic and copies ran while one was open for 11% -> 2% of each run, Pallas kernels for 0% -> 11%
where the time goes in v1:
time: 192 us; the launch traced here: 191 us
  waiting for transfers between devices  79.3 us (41%)
  Pallas kernels  50.6 us (26%)
  starting transfers between devices  35.8 us (19%)
  local copies, waits for them, and re-layouts  20.2 us (11%)
  other arithmetic  4.55 us (2%)
    all_to_all x1, waiting for transfers between devices, body(): lax.all_to_all(send, ('dp', 'ctx'), split_axis=0, concat_axis=0, tiled=True)  40.4 us
    ppermute x1, waiting for transfers between devices, gather_dp(): other = lax.ppermute(piece, 'dp', [(i, i ^ 1) for i in range(8)])  30.4 us
    unnamed x26, local copies, waits for them, and re-layouts  19.9 us
    pallas_call x1, Pallas kernels, convolve(): pl.pallas_call(conv_kernel, grid=(CHANS,), in_specs=[whole, pl.BlockSpec(...  19.3 us
    all_to_all x1, starting transfers between devices, body(): lax.all_to_all(send, ('dp', 'ctx'), split_axis=0, concat_axis=0, tiled=True)  16.7 us
    pallas_call x1, Pallas kernels, filter_gradient(): pl.pallas_call(lambda *refs: filter_kernel(scale, *refs), grid=(CHANS,),...  14.5 us
    pallas_call x1, Pallas kernels, post(): pl.pallas_call(post_kernel, grid=(steps, 3), in_specs=[pl.BlockSpec((SEQS...  8.71 us
    ppermute x3, waiting for transfers between devices, gather_dp(): came = lax.ppermute(pair, 'dp', [(i, (i + 2 * k) % 8) for i in range(8)])  8.45 us
  transfers between devices with their start and end apart: 6, of which 4 were waited for; matrix products, arithmetic and copies ran while one was open for 2% of the time, Pallas kernels for 11%

profile of v1, /device:TPU:1, one launch (start us, length us, event | category | flops | bytes accessed | tf_op | source)
XLA Modules:
  0.0 191.2 jit_solution(1142535222828272250)
XLA Ops:
  0.6 0.0 copy-start
  0.6 0.0 copy-start.1
  0.7 2.0 %copy-done.1 = bf16[1,128,12288]{2,1,0:T(8,128)(2,1)S(1)} copy-done((bf16[1,128,12288]{2,1,0:T(8,128)(2,1)S(1)}, bf16[1,128,12288]{2,1,0:T(8,128)(2,1)}, u32[]{:S(2)}) %copy-start.1) | copy-done | bytes 3145752
  2.7 0.0 copy-start.5
  2.7 1.2 copy-done.5
  3.9 1.7 gate_products.1
  5.7 0.0 copy-start.4
  5.7 1.3 copy-done.4
  7.0 16.7 %all-to-all-start = ((bf16[256,16,256]{2,1,0:T(8,128)(2,1)}), bf16[256,16,256]{2,1,0:T(8,128)(2,1)}, u32[]{:S(2)}, u32[]{:S(2)}) async-start(bf16[256,16,256]{2,1,0:T(8,128)(2,1)} %bitcast.4), calls=%async_computation | async-start | bytes 4194304 | tf_op jit(solution)/shard_map/all_to_all | solution.py:289
  23.7 0.0 copy-done
  23.7 6.3 %toeplitz_tiles.1.tile_ref = bf16[16,8,256,256]{3,2,1,0:T(8,128)(2,1)S(1)} custom-call(f32[16,4096]{1,0:T(8,128)S(1)} %constant_dynamic-slice_fusion.filter_ref), custom_call_target="tpu_custom_call" | custom-call | flops 8388608 | bytes 17825792 | tf_op jit(solution)/shard_map/toeplitz_tiles/pallas_call | solution.py:89
  30.0 0.0 copy-start.3
  30.0 5.7 %copy-done.3 = bf16[16,8,256,256]{3,2,1,0:T(8,128)(2,1)} copy-done((bf16[16,8,256,256]{3,2,1,0:T(8,128)(2,1)}, bf16[16,8,256,256]{3,2,1,0:T(8,128)(2,1)S(1)}, u32[]{:S(2)}) %copy-start.3) | copy-done | bytes 16777240
  35.7 40.4 %all-to-all-done = bf16[256,16,256]{2,1,0:T(8,128)(2,1)} async-done(((bf16[256,16,256]{2,1,0:T(8,128)(2,1)}), bf16[256,16,256]{2,1,0:T(8,128)(2,1)}, u32[]{:S(2)}, u32[]{:S(2)}) %all-to-all-start) | async-done | bytes 2097184 | tf_op jit(solution)/shard_map/all_to_all | solution.py:289
  76.2 19.3 %convolve.1 = (bf16[4096,256]{1,0:T(8,128)(2,1)S(1)}, bf16[16,256,256]{2,1,0:T(8,128)(2,1)S(1)}, bf16[16,256,256]{2,1,0:T(8,128)(2,1)}) custom-call(bf16[4096,256]{1,0:T(8,128)(2,1)} %bitcast.1.lanes_ref, bf16[16,8,256,256]{3,2,1,0:T(8,128)(2,1)} %copy-done.3), custom_call_target="tpu_custom_call" | custom-call | flops 4831838208 | bytes 25165824 | tf_op jit(solution)/shard_map/convolve/pallas_call | solution.py:156
  95.5 0.0 copy-start.7
  95.5 1.3 copy-done.7
  96.8 0.0 copy-start.8
  96.8 1.3 copy-done.8
  98.1 7.4 %all-to-all-start.1 = ((bf16[256,16,256]{2,1,0:T(8,128)(2,1)}), bf16[256,16,256]{2,1,0:T(8,128)(2,1)}, u32[]{:S(2)}, u32[]{:S(2)}) async-start(bf16[256,16,256]{2,1,0:T(8,128)(2,1)} %bitcast.5), calls=%async_computation.1 | async-start | bytes 4194304 | tf_op jit(solution)/shard_map/all_to_all | solution.py:292
  105.5 0.0 copy-start.9
  105.6 1.6 copy-done.9
  107.1 0.0 copy-start.10
  107.1 1.6 copy-done.10
  108.7 14.5 %filter_gradient.1 = bf16[16,4096]{1,0:T(8,128)(2,1)S(1)} custom-call(bf16[16,256,256]{2,1,0:T(8,128)(2,1)S(1)} %copy-done.9, bf16[16,256,256]{2,1,0:T(8,128)(2,1)S(1)} %copy-done.10), custom_call_target="tpu_custom_call" | custom-call | flops 2415919104 | bytes 5242880 | tf_op jit(solution)/shard_map/filter_gradient/pallas_call | solution.py:205
  123.3 6.4 %collective-permute-start = (bf16[16,4096]{1,0:T(8,128)(2,1)S(1)}, bf16[16,4096]{1,0:T(8,128)(2,1)S(1)}, u32[]{:S(2)}, u32[]{:S(2)}) collective-permute-start(bf16[16,4096]{1,0:T(8,128)(2,1)S(1)} %filter_gradient.1), channel_id=1, source_target_pairs={{0,32},{32,0},{64,96},{96,64},{128,160},{160,128},{192,224},{224,1... | collective-permute-start | bytes 393224 | tf_op jit(solution)/shard_map/ppermute | solution.py:275
  129.7 30.4 %collective-permute-done = bf16[16,4096]{1,0:T(8,128)(2,1)S(1)} collective-permute-done((bf16[16,4096]{1,0:T(8,128)(2,1)S(1)}, bf16[16,4096]{1,0:T(8,128)(2,1)S(1)}, u32[]{:S(2)}, u32[]{:S(2)}) %collective-permute-start) | collective-permute-done | bytes 131104 | tf_op jit(solution)/shard_map/ppermute | solution.py:275
  160.2 0.0 copy-start.12
  160.2 0.7 copy-done.12
  160.8 0.2 broadcast_in_dim.3
  161.0 0.0 copy-start.6
  161.0 1.1 convert_dynamic-update-slice_fusion.3
  162.1 0.0 copy-start.11
  162.2 1.3 copy-done.11
  163.5 1.7 collective-permute-start.1
  165.1 2.4 %collective-permute-start.2 = (bf16[32,4096]{1,0:T(8,128)(2,1)S(1)}, bf16[32,4096]{1,0:T(8,128)(2,1)S(1)}, u32[]{:S(2)}, u32[]{:S(2)}) collective-permute-start(bf16[32,4096]{1,0:T(8,128)(2,1)S(1)} %get-tuple-element.14), channel_id=1, source_target_pairs={{0,128},{32,160},{64,192},{96,224},{128,0},{160,32},{192,64},{224,... | collective-permute-start | bytes 786440 | tf_op jit(solution)/shard_map/ppermute | solution.py:280
  167.5 1.2 collective-permute-start.3
  168.7 3.3 %collective-permute-done.1 = bf16[32,4096]{1,0:T(8,128)(2,1)} collective-permute-done((bf16[32,4096]{1,0:T(8,128)(2,1)S(1)}, bf16[32,4096]{1,0:T(8,128)(2,1)}, u32[]{:S(2)}, u32[]{:S(2)}) %collective-permute-start.1) | collective-permute-done | bytes 262176 | tf_op jit(solution)/shard_map/ppermute | solution.py:280
  172.0 1.8 convert_dynamic-update-slice_fusion.2
  173.8 5.2 %collective-permute-done.2 = bf16[32,4096]{1,0:T(8,128)(2,1)S(1)} collective-permute-done((bf16[32,4096]{1,0:T(8,128)(2,1)S(1)}, bf16[32,4096]{1,0:T(8,128)(2,1)S(1)}, u32[]{:S(2)}, u32[]{:S(2)}) %collective-permute-start.2) | collective-permute-done | bytes 262176 | tf_op jit(solution)/shard_map/ppermute | solution.py:280
  178.9 0.8 convert_dynamic-update-slice_fusion.1
  179.8 0.0 collective-permute-done.3
  179.8 0.8 convert_dynamic-update-slice_fusion
  180.6 0.0 all-to-all-done.1
  180.6 0.0 copy-done.6
  180.6 0.0 copy-start.2
  180.6 1.9 copy-done.2
  182.5 8.7 %gate_results.1 = (bf16[1,128,4096]{2,1,0:T(8,128)(2,1)}, bf16[1,128,12288]{2,1,0:T(8,128)(2,1)}) custom-call(bf16[8,32,16,256]{3,2,1,0:T(8,128)(2,1)} %bitcast.3.lanes_ref, bf16[1,128,12288]{2,1,0:T(8,128)(2,1)S(1)} %copy-done.2, bf16[1,128,12288]{2,1,0:T(8,128)(2,1)S(1)} %copy-done.2, bf16[1,128,12288]{2,1,0:T(8,128)(2,1)S(1)} %copy-done.2, ...), custom_call_target="tpu_custom_call" | custom-call | flops 2097152 | bytes 10485760 | tf_op jit(solution)/shard_map/gate_results/pallas_call | solution.py:250
  (1 shorter events, 0.0 us)
Async XLA Ops:
  0.6 23.0 %copy-start = (f32[128,4096]{1,0:T(8,128)S(1)}, f32[128,4096]{1,0:T(8,128)}, u32[]{:S(2)}) copy-start(f32[128,4096]{1,0:T(8,128)} %param.4) | copy-start | bytes 6291460
  0.6 2.0 %copy-start.1 = (bf16[1,128,12288]{2,1,0:T(8,128)(2,1)S(1)}, bf16[1,128,12288]{2,1,0:T(8,128)(2,1)}, u32[]{:S(2)}) copy-start(bf16[1,128,12288]{2,1,0:T(8,128)(2,1)} %value_ref.3) | copy-start | bytes 9437188
  2.7 1.2 copy-start.5
  5.7 1.3 copy-start.4
  7.0 69.2 %all-to-all-start = ((bf16[256,16,256]{2,1,0:T(8,128)(2,1)}), bf16[256,16,256]{2,1,0:T(8,128)(2,1)}, u32[]{:S(2)}, u32[]{:S(2)}) async-start(bf16[256,16,256]{2,1,0:T(8,128)(2,1)} %bitcast.4), calls=%async_computation | async-start | bytes 4194304 | tf_op jit(solution)/shard_map/all_to_all | solution.py:289
  30.0 5.7 %copy-start.3 = (bf16[16,8,256,256]{3,2,1,0:T(8,128)(2,1)}, bf16[16,8,256,256]{3,2,1,0:T(8,128)(2,1)S(1)}, u32[]{:S(2)}) copy-start(bf16[16,8,256,256]{3,2,1,0:T(8,128)(2,1)S(1)} %toeplitz_tiles.1.tile_ref) | copy-start | bytes 50331652
  95.5 1.3 copy-start.7
  96.8 1.3 copy-start.8
  98.1 82.5 %all-to-all-start.1 = ((bf16[256,16,256]{2,1,0:T(8,128)(2,1)}), bf16[256,16,256]{2,1,0:T(8,128)(2,1)}, u32[]{:S(2)}, u32[]{:S(2)}) async-start(bf16[256,16,256]{2,1,0:T(8,128)(2,1)} %bitcast.5), calls=%async_computation.1 | async-start | bytes 4194304 | tf_op jit(solution)/shard_map/all_to_all | solution.py:292
  105.5 1.6 copy-start.9
  107.1 1.6 copy-start.10
  123.3 36.9 %collective-permute-start = (bf16[16,4096]{1,0:T(8,128)(2,1)S(1)}, bf16[16,4096]{1,0:T(8,128)(2,1)S(1)}, u32[]{:S(2)}, u32[]{:S(2)}) collective-permute-start(bf16[16,4096]{1,0:T(8,128)(2,1)S(1)} %filter_gradient.1), channel_id=1, source_target_pairs={{0,32},{32,0},{64,96},{96,64},{128,160},{160,128},{192,224},{224,1... | collective-permute-start | bytes 393224 | tf_op jit(solution)/shard_map/ppermute | solution.py:275
  160.2 0.7 copy-start.12
  161.0 19.6 %copy-start.6 = (bf16[1,128,4096]{2,1,0:T(8,128)(2,1)S(1)}, bf16[1,128,4096]{2,1,0:T(8,128)(2,1)}, u32[]{:S(2)}) copy-start(bf16[1,128,4096]{2,1,0:T(8,128)(2,1)} %grad_ref.3) | copy-start | bytes 3145732
  162.1 1.3 copy-start.11
  163.5 8.5 %collective-permute-start.1 = (bf16[32,4096]{1,0:T(8,128)(2,1)S(1)}, bf16[32,4096]{1,0:T(8,128)(2,1)}, u32[]{:S(2)}, u32[]{:S(2)}) collective-permute-start(bf16[32,4096]{1,0:T(8,128)(2,1)S(1)} %get-tuple-element.14), channel_id=1, source_target_pairs={{0,64},{32,96},{64,128},{96,160},{128,192},{160,224},{192,0},{224,... | collective-permute-start | bytes 786440 | tf_op jit(solution)/shard_map/ppermute | solution.py:280
  165.1 13.8 %collective-permute-start.2 = (bf16[32,4096]{1,0:T(8,128)(2,1)S(1)}, bf16[32,4096]{1,0:T(8,128)(2,1)S(1)}, u32[]{:S(2)}, u32[]{:S(2)}) collective-permute-start(bf16[32,4096]{1,0:T(8,128)(2,1)S(1)} %get-tuple-element.14), channel_id=1, source_target_pairs={{0,128},{32,160},{64,192},{96,224},{128,0},{160,32},{192,64},{224,... | collective-permute-start | bytes 786440 | tf_op jit(solution)/shard_map/ppermute | solution.py:280
  167.5 12.2 %collective-permute-start.3 = (bf16[32,4096]{1,0:T(8,128)(2,1)S(1)}, bf16[32,4096]{1,0:T(8,128)(2,1)S(1)}, u32[]{:S(2)}, u32[]{:S(2)}) collective-permute-start(bf16[32,4096]{1,0:T(8,128)(2,1)S(1)} %get-tuple-element.14), channel_id=1, source_target_pairs={{0,192},{32,224},{64,0},{96,32},{128,64},{160,96},{192,128},{224,1... | collective-permute-start | bytes 786440 | tf_op jit(solution)/shard_map/ppermute | solution.py:280
  180.6 1.9 copy-start.2

commit v2 on v1

v2 whole, which is shorter than its diff:
```python
import math

import jax
import jax.numpy as jnp
from jax import lax
from jax.experimental import pallas as pl
from jax.experimental.pallas import tpu as pltpu
from jax.sharding import PartitionSpec as P

F32 = jnp.float32
BF16 = jnp.bfloat16
LANES = 128
CHANS = 16
SEQS = 8
BLOCKS = 32
LENGTH = BLOCKS * LANES
ROWS = BLOCKS * SEQS
GROUPS = BLOCKS // 4
HALF = LANES // 2
STEPS = 4
TALL = 2 * ROWS
MIB = 1 << 20


def hbm(x):
    return pltpu.with_memory_space_constraint(x, pltpu.HBM)


def vmem(x):
    return pltpu.with_memory_space_constraint(x, pltpu.VMEM)


ANY = pl.BlockSpec(memory_space=pl.ANY)
RESIDENT = pl.BlockSpec(memory_space=pltpu.VMEM)


def params(mib):
    return pltpu.CompilerParams(vmem_limit_bytes=mib * MIB)


def cost(flops, moved):
    return pl.CostEstimate(flops=flops, bytes_accessed=moved, transcendentals=0)


CHUNKS = 8
PER = BLOCKS // CHUNKS
WIDE = PER * LANES


def pre_kernel(proj_hbm, grad_hbm, send_hbm, proj_ref, grad_ref, send_ref, in_sems, out_sems):
    def copies_in(i):
        found = []
        for part in range(3):
            cols = pl.ds(part * LENGTH + i * WIDE, WIDE)
            found.append(
                pltpu.make_async_copy(proj_hbm.at[0, :, cols], proj_ref.at[:, cols], in_sems.at[i, part])
            )
        cols = pl.ds(i * WIDE, WIDE)
        found.append(pltpu.make_async_copy(grad_hbm.at[0, :, cols], grad_ref.at[:, cols], in_sems.at[i, 3]))
        return found

    def copy_out(i):
        some = pl.ds(i * PER, PER)
        return pltpu.make_async_copy(send_ref.at[:, some], send_hbm.at[:, some], out_sems.at[i])

    for i in range(CHUNKS):
        for copy in copies_in(i):
            copy.start()
    for i in range(CHUNKS):
        for copy in copies_in(i):
            copy.wait()
        for q in range(i * PER, (i + 1) * PER):
            first = q * LANES
            query, key, value = (
                proj_ref[:, part * LENGTH + first : part * LENGTH + first + LANES].astype(F32) for part in range(3)
            )
            grad = grad_ref[:, first : first + LANES].astype(F32) * query
            send_ref[:, q, :, 0:LANES] = (key * value).T.astype(BF16).reshape(SEQS, CHANS, LANES)
            send_ref[:, q, :, LANES:] = grad.T.astype(BF16).reshape(SEQS, CHANS, LANES)
        copy_out(i).start()
    for i in range(CHUNKS):
        copy_out(i).wait()


def pre(proj, cotangent):
    shape = (SEQS, BLOCKS, CHANS, 2 * LANES)
    return pl.pallas_call(
        pre_kernel,
        in_specs=[ANY, ANY],
        out_specs=ANY,
        out_shape=pltpu.HBM(shape, BF16),
        scratch_shapes=[
            pltpu.VMEM((LANES, 3 * LENGTH), BF16),
            pltpu.VMEM((LANES, LENGTH), BF16),
            pltpu.VMEM(shape, BF16),
            pltpu.SemaphoreType.DMA((CHUNKS, 4)),
            pltpu.SemaphoreType.DMA((CHUNKS,)),
        ],
        compiler_params=params(16),
        cost_estimate=cost(2 * LANES * LENGTH, 6 * MIB),
        name="gate_products",
    )(hbm(proj), hbm(cotangent))


def tile_kernel(filter_ref, out_ref, shifted_ref):
    row = lax.broadcasted_iota(jnp.int32, (8, LANES), 0)
    lane = lax.broadcasted_iota(jnp.int32, (8, LANES), 1)
    t = pl.program_id(0)

    @pl.when(t == 0)
    def _():
        for s in range(8):
            rolled = filter_ref[...] if s == 0 else pltpu.roll(filter_ref[...], s, 1)
            for c in range(CHANS):
                shifted_ref[c, s : s + 1, :] = rolled[c : c + 1, :]

    base = shifted_ref[t]
    for pair in range(HALF // 16):
        halves = []
        for g in (2 * pair, 2 * pair + 1):
            rolled = base if g == 0 else pltpu.roll(base, 8 * g, 1)
            first = jnp.where(lane < row + 8 * g, 0.0, rolled[:, :LANES])
            halves.append(jnp.concatenate([first, rolled[:, LANES:]], axis=1))
        rows = jnp.concatenate(halves, axis=0).astype(BF16)
        for e in range(STEPS):
            for p in range(4):
                start = (4 * e + p) * 4 * HALF
                out_ref[0, e, pl.ds(p * HALF + 16 * pair, 16), :] = rows[:, start : start + 4 * HALF]


def toeplitz_tiles(filters):
    return pl.pallas_call(
        tile_kernel,
        grid=(CHANS,),
        in_specs=[pl.BlockSpec((CHANS, LENGTH), lambda t: (0, 0))],
        out_specs=pl.BlockSpec((1, STEPS, 4 * HALF, 4 * HALF), lambda t: (t, 0, 0, 0)),
        out_shape=pltpu.HBM((CHANS, STEPS, 4 * HALF, 4 * HALF), BF16),
        scratch_shapes=[pltpu.VMEM((CHANS, 8, LENGTH), F32)],
        compiler_params=params(32),
        cost_estimate=cost(CHANS * LENGTH * LANES, 9 * MIB),
        name="toeplitz_tiles",
    )(filters)


PAIRS = CHANS // 2
QUARTERS = 4
AHEAD = 4
NT = (((1,), (1,)), ((), ()))


def conv_kernel(
    lanes_hbm, tile_hbm, out_hbm,
    raw_ref, wide_ref, done_ref, send_ref, tile_ref, even_ref, odd_ref, even_acc, odd_acc,
    in_sems, out_sems, tile_sems,
):
    rows = ROWS * CHANS
    quarter = rows // QUARTERS

    def copy_in(h, c):
        place = (pl.ds(c * quarter, quarter), pl.ds(h * LANES, LANES))
        return pltpu.make_async_copy(lanes_hbm.at[place], raw_ref.at[place], in_sems.at[h, c])

    def copy_out(h, c):
        place = (pl.ds(c * quarter, quarter), pl.ds(h * LANES, LANES))
        return pltpu.make_async_copy(send_ref.at[place], out_hbm.at[place], out_sems.at[h, c])

    def copy_tile(t):
        return pltpu.make_async_copy(tile_hbm.at[t], tile_ref.at[t], tile_sems.at[t])

    left = lax.broadcasted_iota(jnp.int32, (SEQS, LANES), 1) < HALF
    none = jnp.zeros((SEQS, LANES), F32)
    tile = 2 * SEQS

    def turn(x):
        return pltpu.roll(x, HALF, 1)

    def rows_of(t):
        return [wide_ref[pl.ds(r * CHANS + t, SEQS, stride=BLOCKS * CHANS), :] for r in range(BLOCKS)]

    def gather_mixed(ref, t):
        own = rows_of(t)
        turned = [turn(x) for x in own]
        for r in range(BLOCKS):
            even = jnp.where(left, own[r], turned[r - 2] if r >= 2 else none)
            odd = jnp.where(left, turned[r], own[r - 2] if r >= 2 else none)
            both = jnp.concatenate([even, odd], axis=0).astype(BF16)
            ref[r * tile : (r + 1) * tile, :LANES] = both
            if r + 4 < BLOCKS:
                ref[(r + 4) * tile : (r + 5) * tile, LANES:] = both
        ref[: 4 * tile, LANES:] = jnp.zeros((4 * tile, LANES), BF16)

    def gather_grad(ref, t):
        own = rows_of(t) + [none]
        for r in range(BLOCKS):
            odd = turn(jnp.where(left, own[r + 1], own[r]))
            both = jnp.concatenate([own[r], odd], axis=0).astype(BF16)
            ref[r * tile : (r + 1) * tile, :LANES] = both
            if r >= 1:
                ref[(r - 1) * tile : r * tile, LANES:] = both
        ref[(BLOCKS - 1) * tile :, LANES:] = jnp.zeros((tile, LANES), BF16)

    def forward(ref, t, acc_ref):
        for e in range(STEPS):
            skip = 16 * SEQS * e
            out = jnp.dot(ref[: TALL - skip, :], tile_ref[t, e], preferred_element_type=F32)
            if e == 0:
                acc_ref[...] = out[:, :LANES]
            else:
                acc_ref[skip:, :] += out[:, :LANES]
            acc_ref[skip + tile :, :] += out[:-tile, LANES:]
        for r in range(BLOCKS):
            first = r * tile
            here = acc_ref[first : first + SEQS, :]
            before = acc_ref[first - SEQS : first, :] if r else none
            after = acc_ref[first + SEQS : first + tile, :]
            done_ref[pl.ds(r * CHANS + t, SEQS, stride=BLOCKS * CHANS), :] = here + turn(
                jnp.where(left, after, before)
            )

    def backward(ref, t, acc_ref):
        for e in range(STEPS):
            skip = 16 * SEQS * e
            out = lax.dot_general(ref[skip:, :], tile_ref[t, e], NT, preferred_element_type=F32)
            if e == 0:
                acc_ref[...] = out[:, :LANES]
            else:
                acc_ref[: TALL - skip, :] += out[:, :LANES]
            acc_ref[: TALL - skip - 4 * tile, :] += out[4 * tile :, LANES:]
        for r in range(BLOCKS):
            first = r * tile
            even = acc_ref[first : first + SEQS, :]
            odd = acc_ref[first + SEQS : first + tile, :]
            if r < BLOCKS - 2:
                far = first + 2 * tile
                even_far = acc_ref[far : far + SEQS, :]
                odd_far = acc_ref[far + SEQS : far + tile, :]
            else:
                even_far = odd_far = none
            done_ref[pl.ds(r * CHANS + t, SEQS, stride=BLOCKS * CHANS), :] = jnp.where(left, even, odd_far) + turn(
                jnp.where(left, odd, even_far)
            )

    for c in range(QUARTERS):
        copy_in(0, c).start()
    for t in range(AHEAD):
        copy_tile(t).start()
    for h, gather, product in ((0, gather_mixed, forward), (1, gather_grad, backward)):
        for c in range(QUARTERS):
            copy_in(h, c).wait()
            some = pl.ds(c * quarter, quarter)
            wide_ref[some, :] = raw_ref[some, pl.ds(h * LANES, LANES)].astype(F32)
        if h == 0:
            for c in range(QUARTERS):
                copy_in(1, c).start()
        gather(even_ref, 0)

        def step(i, carry, h=h, gather=gather, product=product):
            if h == 0:
                for k in range(2):
                    copy_tile(2 * i + k).wait()

                @pl.when(i < PAIRS - AHEAD // 2)
                def _():
                    for k in range(2):
                        copy_tile(2 * i + AHEAD + k).start()

            gather(odd_ref, 2 * i + 1)
            product(even_ref, 2 * i, even_acc)
            gather(even_ref, jnp.minimum(2 * i + 2, CHANS - 1))
            product(odd_ref, 2 * i + 1, odd_acc)
            return carry

        lax.fori_loop(0, PAIRS, step, 0)
        for c in range(QUARTERS):
            some = pl.ds(c * quarter, quarter)
            send_ref[some, pl.ds(h * LANES, LANES)] = done_ref[some, :].astype(BF16)
            copy_out(h, c).start()
    for h in range(2):
        for c in range(QUARTERS):
            copy_out(h, c).wait()


def convolve(lanes, tiles):
    rows = ROWS * CHANS
    weights = pltpu.VMEM((CHANS, STEPS, 4 * HALF, 4 * HALF), BF16)
    return pl.pallas_call(
        conv_kernel,
        in_specs=[ANY, ANY],
        out_specs=ANY,
        out_shape=pltpu.HBM((rows, 2 * LANES), BF16),
        scratch_shapes=[
            pltpu.VMEM((rows, 2 * LANES), BF16),
            pltpu.VMEM((rows, LANES), F32),
            pltpu.VMEM((rows, LANES), F32),
            pltpu.VMEM((rows, 2 * LANES), BF16),
            weights,
            pltpu.VMEM((TALL, 2 * LANES), BF16),
            pltpu.VMEM((TALL, 2 * LANES), BF16),
            pltpu.VMEM((TALL, LANES), F32),
            pltpu.VMEM((TALL, LANES), F32),
            pltpu.SemaphoreType.DMA((2, QUARTERS)),
            pltpu.SemaphoreType.DMA((2, QUARTERS)),
            pltpu.SemaphoreType.DMA((CHANS,)),
        ],
        compiler_params=params(40),
        cost_estimate=cost(2 * 2 * CHANS * 1280 * 65536, 20 * MIB),
        name="convolve",
    )(hbm(lanes), hbm(tiles))


def filter_kernel(scale, lanes_ref, out_ref, mixed_ref, grad_ref, x2_ref, g3_ref, part_ref, acc_ref):
    t = pl.program_id(0)

    @pl.when(t == 0)
    def _():
        mixed_ref[...] = lanes_ref[:, 0:LANES].astype(F32)
        grad_ref[...] = lanes_ref[:, LANES:].astype(F32)

    def rows_of(ref):
        return [ref[pl.ds(r * CHANS + t, SEQS, stride=BLOCKS * CHANS), :] for r in range(BLOCKS)]

    none = jnp.zeros((SEQS, LANES), F32)
    own = rows_of(mixed_ref)
    x2_ref[:, :LANES] = jnp.concatenate(own, axis=0)
    x2_ref[:, LANES:] = jnp.concatenate([none] + own[:-1], axis=0)
    grad = jnp.concatenate(rows_of(grad_ref), axis=0).astype(BF16)
    g3_ref[:, :LANES] = grad
    g3_ref[: ROWS - 2 * SEQS, LANES:] = grad[2 * SEQS :]
    g3_ref[ROWS - 2 * SEQS :, LANES:] = jnp.zeros((2 * SEQS, LANES), BF16)
    turned = x2_ref[...].T.astype(BF16)

    row = lax.broadcasted_iota(jnp.int32, (LANES, LANES), 0)
    lane = lax.broadcasted_iota(jnp.int32, (LANES, LANES), 1)
    for e in range(GROUPS):
        skip = 4 * SEQS * e
        out = jnp.dot(turned[:, : ROWS - skip], g3_ref[skip:, :], preferred_element_type=F32)
        for p in range(2):
            for h in range(2):
                d = 4 * e + p + 2 * h
                block = out[p * LANES : (p + 1) * LANES, h * LANES : (h + 1) * LANES]
                if d == 0:
                    block = jnp.where(lane < row, 0.0, block)
                part_ref[:, d * LANES : (d + 1) * LANES] = block
    total = part_ref[0:8, :]
    for g in range(1, 16):
        total += pltpu.roll(part_ref[8 * g : 8 * g + 8, :], LENGTH - 8 * g, 1)
    acc_ref[t] = total

    @pl.when(t == CHANS - 1)
    def _():
        result = None
        for s in range(8):
            piece = jnp.concatenate([acc_ref[c, s : s + 1, :] for c in range(CHANS)], axis=0)
            piece = piece if s == 0 else pltpu.roll(piece, LENGTH - s, 1)
            result = piece if result is None else result + piece
        out_ref[...] = (result * scale).astype(BF16)


def filter_gradient(lanes, scale):
    rows = ROWS * CHANS
    return pl.pallas_call(
        lambda *refs: filter_kernel(scale, *refs),
        grid=(CHANS,),
        in_specs=[pl.BlockSpec((rows, 2 * LANES), lambda t: (0, 0))],
        out_specs=pl.BlockSpec((CHANS, LENGTH), lambda t: (0, 0)),
        out_shape=jax.ShapeDtypeStruct((CHANS, LENGTH), BF16),
        scratch_shapes=[
            pltpu.VMEM((rows, LANES), F32),
            pltpu.VMEM((rows, LANES), F32),
            pltpu.VMEM((ROWS, 2 * LANES), F32),
            pltpu.VMEM((ROWS, 2 * LANES), BF16),
            pltpu.VMEM((LANES, LENGTH), F32),
            pltpu.VMEM((CHANS, 8, LENGTH), F32),
        ],
        compiler_params=params(32),
        cost_estimate=cost(2 * CHANS * 1152 * 65536, 5 * MIB),
        name="filter_gradient",
    )(lanes)


def place_pieces(rows_ref, pieces, out_hbm, wide_ref, sems):
    copies = []
    for k, piece in enumerate(pieces):
        wide_ref[k] = piece[...].astype(F32)
        first = pl.multiple_of(rows_ref[k], CHANS)
        copies.append(pltpu.make_async_copy(wide_ref.at[k], out_hbm.at[pl.ds(first, CHANS), :], sems.at[k]))
        copies[-1].start()
    return copies


def place_kernel(n, rows_ref, *refs):
    pieces, (out_hbm, wide_ref, sems) = refs[:n], refs[-3:]
    for copy in place_pieces(rows_ref, pieces, out_hbm, wide_ref, sems):
        copy.wait()


def place_rows(rows, pieces, whole):
    n = len(pieces)
    return pl.pallas_call(
        lambda *refs: place_kernel(n, *refs),
        in_specs=[pl.BlockSpec(memory_space=pltpu.SMEM)] + [RESIDENT] * n + [ANY],
        out_specs=ANY,
        out_shape=pltpu.HBM((SEQS * CHANS, LENGTH), F32),
        input_output_aliases={n + 1: 0},
        scratch_shapes=[pltpu.VMEM((n, CHANS, LENGTH), F32), pltpu.SemaphoreType.DMA((n,))],
        compiler_params=params(16),
        cost_estimate=cost(n * CHANS * LENGTH, n * 6 * CHANS * LENGTH),
        name="place_rows",
    )(jnp.stack(rows).astype(jnp.int32), *pieces, hbm(whole))


AT_HAND = 5


def post_kernel(rows_ref, lanes_hbm, proj_hbm, grad_hbm, *refs):
    pieces = refs[:AT_HAND]
    (
        gated_hbm, out_hbm, filter_hbm,
        lanes_ref, proj_ref, grad_ref, gated_ref, out_ref, wide_ref, in_sems, out_sems, row_sems,
    ) = refs[AT_HAND:]

    def copies_in(i):
        some = pl.ds(i * PER, PER)
        found = [pltpu.make_async_copy(lanes_hbm.at[:, some], lanes_ref.at[:, some], in_sems.at[i, 4])]
        for part in range(3):
            cols = pl.ds(part * LENGTH + i * WIDE, WIDE)
            found.append(
                pltpu.make_async_copy(proj_hbm.at[0, :, cols], proj_ref.at[:, cols], in_sems.at[i, part])
            )
        cols = pl.ds(i * WIDE, WIDE)
        found.append(pltpu.make_async_copy(grad_hbm.at[0, :, cols], grad_ref.at[:, cols], in_sems.at[i, 3]))
        return found

    def copies_out(i):
        cols = pl.ds(i * WIDE, WIDE)
        found = [pltpu.make_async_copy(gated_ref.at[:, cols], gated_hbm.at[0, :, cols], out_sems.at[i, 3])]
        for part in range(3):
            cols = pl.ds(part * LENGTH + i * WIDE, WIDE)
            found.append(pltpu.make_async_copy(out_ref.at[:, cols], out_hbm.at[0, :, cols], out_sems.at[i, part]))
        return found

    for i in range(CHUNKS):
        for copy in copies_in(i):
            copy.start()
    copies = place_pieces(rows_ref, pieces, filter_hbm, wide_ref, row_sems)
    for i in range(CHUNKS):
        for copy in copies_in(i):
            copy.wait()
        for q in range(i * PER, (i + 1) * PER):
            both = lanes_ref[:, q].reshape(LANES, 2 * LANES).astype(F32)
            conv = both[:, :LANES].T
            back = both[:, LANES:].T
            first = q * LANES
            cols = [slice(part * LENGTH + first, part * LENGTH + first + LANES) for part in range(3)]
            gated_ref[:, cols[0]] = (proj_ref[:, cols[0]].astype(F32) * conv).astype(BF16)
            out_ref[:, cols[0]] = (grad_ref[:, cols[0]].astype(F32) * conv).astype(BF16)
            out_ref[:, cols[1]] = (back * proj_ref[:, cols[2]].astype(F32)).astype(BF16)
            out_ref[:, cols[2]] = (back * proj_ref[:, cols[1]].astype(F32)).astype(BF16)
        for copy in copies_out(i):
            copy.start()
    for i in range(CHUNKS):
        for copy in copies_out(i):
            copy.wait()
    for copy in copies:
        copy.wait()


def post(lanes, proj, cotangent, rows, pieces):
    return pl.pallas_call(
        post_kernel,
        in_specs=[pl.BlockSpec(memory_space=pltpu.SMEM), ANY, ANY, ANY] + [RESIDENT] * AT_HAND,
        out_specs=[ANY, ANY, ANY],
        out_shape=[
            pltpu.HBM((1, LANES, LENGTH), BF16),
            pltpu.HBM((1, LANES, 3 * LENGTH), BF16),
            pltpu.HBM((SEQS * CHANS, LENGTH), F32),
        ],
        scratch_shapes=[
            pltpu.VMEM((SEQS, BLOCKS, CHANS, 2 * LANES), BF16),
            pltpu.VMEM((LANES, 3 * LENGTH), BF16),
            pltpu.VMEM((LANES, LENGTH), BF16),
            pltpu.VMEM((LANES, LENGTH), BF16),
            pltpu.VMEM((LANES, 3 * LENGTH), BF16),
            pltpu.VMEM((AT_HAND, CHANS, LENGTH), F32),
            pltpu.SemaphoreType.DMA((CHUNKS, 5)),
            pltpu.SemaphoreType.DMA((CHUNKS, 4)),
            pltpu.SemaphoreType.DMA((AT_HAND,)),
        ],
        compiler_params=params(32),
        cost_estimate=cost(4 * LANES * LENGTH, 14 * MIB),
        name="gate_results",
    )(jnp.stack(rows).astype(jnp.int32), hbm(lanes), hbm(proj), hbm(cotangent), *pieces)


def body(proj, filters, cotangent):
    place = lax.axis_index("dp")
    scale = 1.0 / math.sqrt(SEQS * LENGTH)
    send = pre(proj, cotangent)
    lanes = lax.all_to_all(
        send.reshape(ROWS, CHANS, 2 * LANES), ("dp", "ctx"), split_axis=0, concat_axis=0, tiled=True
    )
    tiles = toeplitz_tiles(lax.dynamic_slice(filters, (place * CHANS, 0), (CHANS, LENGTH)))
    lanes = lanes.reshape(ROWS * CHANS, 2 * LANES)
    results = convolve(lanes, tiles)
    back = lax.all_to_all(
        results.reshape(ROWS, CHANS, 2 * LANES), ("dp", "ctx"), split_axis=0, concat_axis=0, tiled=True
    )

    own = filter_gradient(lanes, scale)
    along_x = [[(i, (i + 2 * k) % 8) for i in range(8)] for k in range(1, 4)]
    before = [(place + 8 - 2 * k) % 8 for k in range(1, 4)]
    other = lax.ppermute(own, "dp", [(i, i ^ 1) for i in range(8)])
    first = [lax.ppermute(own, "dp", pairs) for pairs in along_x]
    rows = [place, place ^ 1] + before
    back, other = lax.optimization_barrier((back, other))
    second = [lax.ppermute(other, "dp", pairs) for pairs in along_x]
    gated, grad_proj, filter_grad = post(
        back.reshape(SEQS, BLOCKS, CHANS, 2 * LANES),
        proj,
        cotangent,
        [r * CHANS for r in rows],
        [own, other] + first,
    )
    filter_grad = place_rows([(r ^ 1) * CHANS for r in before], second, filter_grad)
    return (gated, grad_proj, filter_grad)


def solution(mesh):
    return jax.shard_map(
        body,
        mesh=mesh,
        in_specs=(P("dp", "ctx", None), P("ctx", None), P("dp", "ctx", None)),
        out_specs=(P("dp", "ctx", None), P("dp", "ctx", None), P("ctx", None)),
        check_vma=False,
    )
```

time: 192 us -> 165 us (0.86)
  local copies, waits for them, and re-layouts: 20.2 us -> 0.12 us
  waiting for transfers between devices: 79.3 us -> 68.4 us
  starting transfers between devices: 35.8 us -> 40.6 us
  other arithmetic: 4.55 us -> 0.08 us
  Pallas kernels: 50.6 us -> 54.7 us
    unnamed x26 -> x2, local copies, waits for them, and re-layouts: 19.9 us -> 0.01 us
    ppermute x4 -> x7, waiting for transfers between devices: 38.9 us -> 25.1 us  [the longest x1 25.1 us: body(): other = lax.ppermute(own, 'dp', [(i, i ^ 1) for i in range(8)])]
    ppermute x4 -> x7, starting transfers between devices: 11.7 us -> 16.5 us  [the longest x1 6.45 us: body(): other = lax.ppermute(own, 'dp', [(i, i ^ 1) for i in range(8)])]
    dynamic_update_slice x4 -> x0, other arithmetic: 4.55 us -> none  [the longest x3 3.43 us: gather_dp(): lax.dynamic_update_slice(whole, came.astype(F32), ((upper + 4 - k) % 4 *...]
    pallas_call x1, Pallas kernels: 14.5 us -> 18.3 us  [filter_gradient(): pl.pallas_call(lambda *refs: filter_kernel(scale, *refs), grid=(CHANS,),...]
    pallas_call x1, Pallas kernels: 6.32 us -> 9.22 us  [toeplitz_tiles(): pl.pallas_call(tile_kernel, grid=(CHANS,), in_specs=[pl.BlockSpec((CHANS,...]
    all_to_all x1, waiting for transfers between devices: 40.4 us -> 43.2 us  [body(): lax.all_to_all(send.reshape(ROWS, CHANS, 2 * LANES), ('dp', 'ctx'), split...]
    pallas_call x3 -> x4, Pallas kernels: 29.8 us -> 27.2 us  [the longest x1 15.5 us: convolve(): pl.pallas_call(conv_kernel, in_specs=[ANY, ANY], out_specs=ANY, out_shape...]
  transfers between devices with their start and end apart: 6 -> 9, of which waited for: 4 -> 2; matrix products, arithmetic and copies ran while one was open for 2% -> 0% of each run, Pallas kernels for 11% -> 21%
where the time goes in v2:
time: 165 us
  waiting for transfers between devices  68.4 us (41%)
  Pallas kernels  54.7 us (33%)
  starting transfers between devices  40.6 us (25%)
    all_to_all x1, waiting for transfers between devices, body(): lax.all_to_all(send.reshape(ROWS, CHANS, 2 * LANES), ('dp', 'ctx'), split...  43.2 us
    ppermute x1, waiting for transfers between devices, body(): other = lax.ppermute(own, 'dp', [(i, i ^ 1) for i in range(8)])  25.1 us
    pallas_call x1, Pallas kernels, filter_gradient(): pl.pallas_call(lambda *refs: filter_kernel(scale, *refs), grid=(CHANS,),...  18.3 us
    all_to_all x1, starting transfers between devices, body(): lax.all_to_all(send.reshape(ROWS, CHANS, 2 * LANES), ('dp', 'ctx'), split...  16.7 us
    pallas_call x1, Pallas kernels, convolve(): pl.pallas_call(conv_kernel, in_specs=[ANY, ANY], out_specs=ANY, out_shape...  15.5 us
    pallas_call x1, Pallas kernels, toeplitz_tiles(): pl.pallas_call(tile_kernel, grid=(CHANS,), in_specs=[pl.BlockSpec((CHANS,...  9.22 us
    all_to_all x1, starting transfers between devices, body(): lax.all_to_all(results.reshape(ROWS, CHANS, 2 * LANES), ('dp', 'ctx'), sp...  7.43 us
    pallas_call x1, Pallas kernels, post(): pl.pallas_call(post_kernel, in_specs=[pl.BlockSpec(memory_space=pltpu.SME...  6.49 us
  transfers between devices with their start and end apart: 9, of which 2 were waited for; matrix products, arithmetic and copies ran while one was open for 0% of the time, Pallas kernels for 21%

profile of v2, /device:TPU:1, one launch (start us, length us, event | category | flops | bytes accessed | tf_op | source)
XLA Modules:
  0.0 164.7 jit_solution(1617992064849999974)
XLA Ops:
  0.6 0.0 copy-start
  0.6 3.8 %gate_products.1 = bf16[8,32,16,256]{3,2,1,0:T(8,128)(2,1)} custom-call(bf16[1,128,12288]{2,1,0:T(8,128)(2,1)} %proj_hbm.3, bf16[1,128,4096]{2,1,0:T(8,128)(2,1)} %grad_hbm.3), custom_call_target="tpu_custom_call" | custom-call | flops 1048576 | bytes 6291456 | tf_op jit(solution)/shard_map/gate_products/pallas_call | solution.py:87
  4.4 16.7 %all-to-all-start = ((bf16[256,16,256]{2,1,0:T(8,128)(2,1)}), bf16[256,16,256]{2,1,0:T(8,128)(2,1)}, u32[]{:S(2)}, u32[]{:S(2)}) async-start(bf16[256,16,256]{2,1,0:T(8,128)(2,1)} %bitcast.12), calls=%async_computation | async-start | bytes 4194304 | tf_op jit(solution)/shard_map/all_to_all | solution.py:499
  21.1 0.0 copy-done
  21.1 9.2 %toeplitz_tiles.1.tile_hbm = bf16[16,4,256,256]{3,2,1,0:T(8,128)(2,1)} custom-call(f32[16,4096]{1,0:T(8,128)S(1)} %constant_dynamic-slice_fusion.filter_ref), custom_call_target="tpu_custom_call" | custom-call | flops 8388608 | bytes 9437184 | tf_op jit(solution)/shard_map/toeplitz_tiles/pallas_call | solution.py:132
  30.3 43.2 %all-to-all-done = bf16[256,16,256]{2,1,0:T(8,128)(2,1)} async-done(((bf16[256,16,256]{2,1,0:T(8,128)(2,1)}), bf16[256,16,256]{2,1,0:T(8,128)(2,1)}, u32[]{:S(2)}, u32[]{:S(2)}) %all-to-all-start) | async-done | bytes 2097184 | tf_op jit(solution)/shard_map/all_to_all | solution.py:499
  73.6 15.5 %convolve.1 = bf16[4096,256]{1,0:T(8,128)(2,1)} custom-call(bf16[4096,256]{1,0:T(8,128)(2,1)} %bitcast.6.lanes_hbm.refs_0_, bf16[16,4,256,256]{3,2,1,0:T(8,128)(2,1)} %toeplitz_tiles.1.tile_hbm), custom_call_target="tpu_custom_call" | custom-call | flops 5368709120 | bytes 20971520 | tf_op jit(solution)/shard_map/convolve/pallas_call | solution.py:286
  89.1 7.4 %all-to-all-start.1 = ((bf16[256,16,256]{2,1,0:T(8,128)(2,1)}), bf16[256,16,256]{2,1,0:T(8,128)(2,1)}, u32[]{:S(2)}, u32[]{:S(2)}) async-start(bf16[256,16,256]{2,1,0:T(8,128)(2,1)} %bitcast.13), calls=%async_computation.1 | async-start | bytes 4194304 | tf_op jit(solution)/shard_map/all_to_all | solution.py:505
  96.6 18.3 %filter_gradient.1.refs_0_ = bf16[16,4096]{1,0:T(8,128)(2,1)S(1)} custom-call(bf16[4096,256]{1,0:T(8,128)(2,1)} %bitcast.6.lanes_hbm.refs_0_), custom_call_target="tpu_custom_call" | custom-call | flops 2415919104 | bytes 5242880 | tf_op jit(solution)/shard_map/filter_gradient/pallas_call | solution.py:361
  114.8 6.5 %collective-permute-start = (bf16[16,4096]{1,0:T(8,128)(2,1)S(1)}, bf16[16,4096]{1,0:T(8,128)(2,1)S(1)}, u32[]{:S(2)}, u32[]{:S(2)}) collective-permute-start(bf16[16,4096]{1,0:T(8,128)(2,1)S(1)} %filter_gradient.1.refs_0_), channel_id=1, source_target_pairs={{0,32},{32,0},{64,96},{96,64},{128,160},{160,128},{192,224},{224,1... | collective-permute-start | bytes 393224 | tf_op jit(solution)/shard_map/ppermute | solution.py:512
  121.3 1.2 collective-permute-start.1
  122.5 2.4 %collective-permute-start.2 = (bf16[16,4096]{1,0:T(8,128)(2,1)S(1)}, bf16[16,4096]{1,0:T(8,128)(2,1)S(1)}, u32[]{:S(2)}, u32[]{:S(2)}) collective-permute-start(bf16[16,4096]{1,0:T(8,128)(2,1)S(1)} %filter_gradient.1.refs_0_), channel_id=1, source_target_pairs={{0,128},{32,160},{64,192},{96,224},{128,0},{160,32},{192,64},{224,... | collective-permute-start | bytes 393224 | tf_op jit(solution)/shard_map/ppermute | solution.py:513
  124.9 1.2 collective-permute-start.3
  126.1 25.1 %collective-permute-done.refs_1_ = bf16[16,4096]{1,0:T(8,128)(2,1)S(1)} collective-permute-done((bf16[16,4096]{1,0:T(8,128)(2,1)S(1)}, bf16[16,4096]{1,0:T(8,128)(2,1)S(1)}, u32[]{:S(2)}, u32[]{:S(2)}) %collective-permute-start) | collective-permute-done | bytes 131104 | tf_op jit(solution)/shard_map/ppermute | solution.py:512
  151.2 0.0 all-to-all-done.1
  151.2 1.7 %collective-permute-start.4 = (bf16[16,4096]{1,0:T(8,128)(2,1)S(1)}, bf16[16,4096]{1,0:T(8,128)(2,1)S(1)}, u32[]{:S(2)}, u32[]{:S(2)}) collective-permute-start(bf16[16,4096]{1,0:T(8,128)(2,1)S(1)} %collective-permute-done.refs_1_), channel_id=1, source_target_pairs={{0,64},{32,96},{64,128},{96,160},{128,192},{160,224},{192,0},{224,... | collective-permute-start | bytes 393224 | tf_op jit(solution)/shard_map/ppermute | solution.py:516
  152.8 2.4 %collective-permute-start.5 = (bf16[16,4096]{1,0:T(8,128)(2,1)S(1)}, bf16[16,4096]{1,0:T(8,128)(2,1)S(1)}, u32[]{:S(2)}, u32[]{:S(2)}) collective-permute-start(bf16[16,4096]{1,0:T(8,128)(2,1)S(1)} %collective-permute-done.refs_1_), channel_id=1, source_target_pairs={{0,128},{32,160},{64,192},{96,224},{128,0},{160,32},{192,64},{224,... | collective-permute-start | bytes 393224 | tf_op jit(solution)/shard_map/ppermute | solution.py:516
  155.3 0.0 collective-permute-done.1.refs_2_
  155.3 1.2 collective-permute-start.6
  156.4 0.1 stack.35.rows_ref
  156.5 0.1 pad_add_fusion.refs_0_
  156.6 0.0 collective-permute-done.2.refs_3_
  156.6 0.0 collective-permute-done.3.refs_4_
  156.6 6.5 %gate_results.1 = (bf16[1,128,4096]{2,1,0:T(8,128)(2,1)}, bf16[1,128,12288]{2,1,0:T(8,128)(2,1)}, f32[128,4096]{1,0:T(8,128)}) custom-call(s32[5]{0:T(128)S(1)} %stack.35.rows_ref, bf16[8,32,16,256]{3,2,1,0:T(8,128)(2,1)} %bitcast.8.lanes_hbm, bf16[1,128,12288]{2,1,0:T(8,128)(2,1)} %proj_hbm.3, bf16[1,128,4096]{2,1,0:T(8,128)(2,1)} %grad_hbm.3, ...), custom_call_target="tpu_custom_call" | custom-call | flops 2097152 | bytes 14680064 | tf_op jit(solution)/shard_map/gate_results/pallas_call | solution.py:469
  163.1 0.0 collective-permute-done.4.refs_1_
  163.1 0.0 collective-permute-done.5.refs_2_
  163.1 0.0 collective-permute-done.6.refs_3_
  163.1 1.5 place_rows.1
  (1 shorter events, 0.0 us)
Async XLA Ops:
  0.6 20.5 %copy-start = (f32[128,4096]{1,0:T(8,128)S(1)}, f32[128,4096]{1,0:T(8,128)}, u32[]{:S(2)}) copy-start(f32[128,4096]{1,0:T(8,128)} %param.4) | copy-start | bytes 6291460
  4.4 69.2 %all-to-all-start = ((bf16[256,16,256]{2,1,0:T(8,128)(2,1)}), bf16[256,16,256]{2,1,0:T(8,128)(2,1)}, u32[]{:S(2)}, u32[]{:S(2)}) async-start(bf16[256,16,256]{2,1,0:T(8,128)(2,1)} %bitcast.12), calls=%async_computation | async-start | bytes 4194304 | tf_op jit(solution)/shard_map/all_to_all | solution.py:499
  89.1 62.0 %all-to-all-start.1 = ((bf16[256,16,256]{2,1,0:T(8,128)(2,1)}), bf16[256,16,256]{2,1,0:T(8,128)(2,1)}, u32[]{:S(2)}, u32[]{:S(2)}) async-start(bf16[256,16,256]{2,1,0:T(8,128)(2,1)} %bitcast.13), calls=%async_computation.1 | async-start | bytes 4194304 | tf_op jit(solution)/shard_map/all_to_all | solution.py:505
  114.8 36.3 %collective-permute-start = (bf16[16,4096]{1,0:T(8,128)(2,1)S(1)}, bf16[16,4096]{1,0:T(8,128)(2,1)S(1)}, u32[]{:S(2)}, u32[]{:S(2)}) collective-permute-start(bf16[16,4096]{1,0:T(8,128)(2,1)S(1)} %filter_gradient.1.refs_0_), channel_id=1, source_target_pairs={{0,32},{32,0},{64,96},{96,64},{128,160},{160,128},{192,224},{224,1... | collective-permute-start | bytes 393224 | tf_op jit(solution)/shard_map/ppermute | solution.py:512
  121.3 34.0 %collective-permute-start.1 = (bf16[16,4096]{1,0:T(8,128)(2,1)S(1)}, bf16[16,4096]{1,0:T(8,128)(2,1)S(1)}, u32[]{:S(2)}, u32[]{:S(2)}) collective-permute-start(bf16[16,4096]{1,0:T(8,128)(2,1)S(1)} %filter_gradient.1.refs_0_), channel_id=1, source_target_pairs={{0,64},{32,96},{64,128},{96,160},{128,192},{160,224},{192,0},{224,... | collective-permute-start | bytes 393224 | tf_op jit(solution)/shard_map/ppermute | solution.py:513
  122.5 34.1 %collective-permute-start.2 = (bf16[16,4096]{1,0:T(8,128)(2,1)S(1)}, bf16[16,4096]{1,0:T(8,128)(2,1)S(1)}, u32[]{:S(2)}, u32[]{:S(2)}) collective-permute-start(bf16[16,4096]{1,0:T(8,128)(2,1)S(1)} %filter_gradient.1.refs_0_), channel_id=1, source_target_pairs={{0,128},{32,160},{64,192},{96,224},{128,0},{160,32},{192,64},{224,... | collective-permute-start | bytes 393224 | tf_op jit(solution)/shard_map/ppermute | solution.py:513
  124.9 31.7 %collective-permute-start.3 = (bf16[16,4096]{1,0:T(8,128)(2,1)S(1)}, bf16[16,4096]{1,0:T(8,128)(2,1)S(1)}, u32[]{:S(2)}, u32[]{:S(2)}) collective-permute-start(bf16[16,4096]{1,0:T(8,128)(2,1)S(1)} %filter_gradient.1.refs_0_), channel_id=1, source_target_pairs={{0,192},{32,224},{64,0},{96,32},{128,64},{160,96},{192,128},{224,1... | collective-permute-start | bytes 393224 | tf_op jit(solution)/shard_map/ppermute | solution.py:513
  151.2 11.9 %collective-permute-start.4 = (bf16[16,4096]{1,0:T(8,128)(2,1)S(1)}, bf16[16,4096]{1,0:T(8,128)(2,1)S(1)}, u32[]{:S(2)}, u32[]{:S(2)}) collective-permute-start(bf16[16,4096]{1,0:T(8,128)(2,1)S(1)} %collective-permute-done.refs_1_), channel_id=1, source_target_pairs={{0,64},{32,96},{64,128},{96,160},{128,192},{160,224},{192,0},{224,... | collective-permute-start | bytes 393224 | tf_op jit(solution)/shard_map/ppermute | solution.py:516
  152.8 10.3 %collective-permute-start.5 = (bf16[16,4096]{1,0:T(8,128)(2,1)S(1)}, bf16[16,4096]{1,0:T(8,128)(2,1)S(1)}, u32[]{:S(2)}, u32[]{:S(2)}) collective-permute-start(bf16[16,4096]{1,0:T(8,128)(2,1)S(1)} %collective-permute-done.refs_1_), channel_id=1, source_target_pairs={{0,128},{32,160},{64,192},{96,224},{128,0},{160,32},{192,64},{224,... | collective-permute-start | bytes 393224 | tf_op jit(solution)/shard_map/ppermute | solution.py:516
  155.3 7.9 %collective-permute-start.6 = (bf16[16,4096]{1,0:T(8,128)(2,1)S(1)}, bf16[16,4096]{1,0:T(8,128)(2,1)S(1)}, u32[]{:S(2)}, u32[]{:S(2)}) collective-permute-start(bf16[16,4096]{1,0:T(8,128)(2,1)S(1)} %collective-permute-done.refs_1_), channel_id=1, source_target_pairs={{0,192},{32,224},{64,0},{96,32},{128,64},{160,96},{192,128},{224,1... | collective-permute-start | bytes 393224 | tf_op jit(solution)/shard_map/ppermute | solution.py:516

commit v3 on v2

--- a/solution.py
+++ b/solution.py
@@ -42,7 +42,7 @@
     return pl.CostEstimate(flops=flops, bytes_accessed=moved, transcendentals=0)
 
 
-CHUNKS = 8
+CHUNKS = 4
 PER = BLOCKS // CHUNKS
 WIDE = PER * LANES
 
@@ -394,31 +394,25 @@
         copy.wait()
 
 
-def place_rows(rows, pieces, whole):
+def place_rows(rows, pieces, held=()):
     n = len(pieces)
     return pl.pallas_call(
         lambda *refs: place_kernel(n, *refs),
-        in_specs=[pl.BlockSpec(memory_space=pltpu.SMEM)] + [RESIDENT] * n + [ANY],
+        in_specs=[pl.BlockSpec(memory_space=pltpu.SMEM)] + [RESIDENT] * n + [ANY] * len(held),
         out_specs=ANY,
         out_shape=pltpu.HBM((SEQS * CHANS, LENGTH), F32),
-        input_output_aliases={n + 1: 0},
+        input_output_aliases={n + 1: 0} if held else {},
         scratch_shapes=[pltpu.VMEM((n, CHANS, LENGTH), F32), pltpu.SemaphoreType.DMA((n,))],
         compiler_params=params(16),
         cost_estimate=cost(n * CHANS * LENGTH, n * 6 * CHANS * LENGTH),
-        name="place_rows",
-    )(jnp.stack(rows).astype(jnp.int32), *pieces, hbm(whole))
-
-
-AT_HAND = 5
-
-
-def post_kernel(rows_ref, lanes_hbm, proj_hbm, grad_hbm, *refs):
-    pieces = refs[:AT_HAND]
-    (
-        gated_hbm, out_hbm, filter_hbm,
-        lanes_ref, proj_ref, grad_ref, gated_ref, out_ref, wide_ref, in_sems, out_sems, row_sems,
-    ) = refs[AT_HAND:]
-
+        name="place_rows_%d" % n,
+    )(jnp.stack(rows).astype(jnp.int32), *pieces, *[hbm(x) for x in held])
+
+
+def post_kernel(
+    lanes_hbm, proj_hbm, grad_hbm, gated_hbm, out_hbm,
+    lanes_ref, proj_ref, grad_ref, gated_ref, out_ref, in_sems, out_sems,
+):
     def copies_in(i):
         some = pl.ds(i * PER, PER)
         found = [pltpu.make_async_copy(lanes_hbm.at[:, some], lanes_ref.at[:, some], in_sems.at[i, 4])]
@@ -442,7 +436,6 @@
     for i in range(CHUNKS):
         for copy in copies_in(i):
             copy.start()
-    copies = place_pieces(rows_ref, pieces, filter_hbm, wide_ref, row_sems)
     for i in range(CHUNKS):
         for copy in copies_in(i):
             copy.wait()
@@ -461,19 +454,16 @@
     for i in range(CHUNKS):
         for copy in copies_out(i):
             copy.wait()
-    for copy in copies:
-        copy.wait()
-
-
-def post(lanes, proj, cotangent, rows, pieces):
+
+
+def post(lanes, proj, cotangent):
     return pl.pallas_call(
         post_kernel,
-        in_specs=[pl.BlockSpec(memory_space=pltpu.SMEM), ANY, ANY, ANY] + [RESIDENT] * AT_HAND,
-        out_specs=[ANY, ANY, ANY],
+        in_specs=[ANY, ANY, ANY],
+        out_specs=[ANY, ANY],
         out_shape=[
             pltpu.HBM((1, LANES, LENGTH), BF16),
             pltpu.HBM((1, LANES, 3 * LENGTH), BF16),
-            pltpu.HBM((SEQS * CHANS, LENGTH), F32),
         ],
         scratch_shapes=[
             pltpu.VMEM((SEQS, BLOCKS, CHANS, 2 * LANES), BF16),
@@ -481,15 +471,13 @@
             pltpu.VMEM((LANES, LENGTH), BF16),
             pltpu.VMEM((LANES, LENGTH), BF16),
             pltpu.VMEM((LANES, 3 * LENGTH), BF16),
-            pltpu.VMEM((AT_HAND, CHANS, LENGTH), F32),
             pltpu.SemaphoreType.DMA((CHUNKS, 5)),
             pltpu.SemaphoreType.DMA((CHUNKS, 4)),
-            pltpu.SemaphoreType.DMA((AT_HAND,)),
         ],
         compiler_params=params(32),
         cost_estimate=cost(4 * LANES * LENGTH, 14 * MIB),
         name="gate_results",
-    )(jnp.stack(rows).astype(jnp.int32), hbm(lanes), hbm(proj), hbm(cotangent), *pieces)
+    )(hbm(lanes), hbm(proj), hbm(cotangent))
 
 
 def body(proj, filters, cotangent):
@@ -511,17 +499,11 @@
     before = [(place + 8 - 2 * k) % 8 for k in range(1, 4)]
     other = lax.ppermute(own, "dp", [(i, i ^ 1) for i in range(8)])
     first = [lax.ppermute(own, "dp", pairs) for pairs in along_x]
-    rows = [place, place ^ 1] + before
-    back, other = lax.optimization_barrier((back, other))
+    gated, grad_proj = post(back.reshape(SEQS, BLOCKS, CHANS, 2 * LANES), proj, cotangent)
+    gated, own, other, *first = lax.optimization_barrier((gated, own, other, *first))
     second = [lax.ppermute(other, "dp", pairs) for pairs in along_x]
-    gated, grad_proj, filter_grad = post(
-        back.reshape(SEQS, BLOCKS, CHANS, 2 * LANES),
-        proj,
-        cotangent,
-        [r * CHANS for r in rows],
-        [own, other] + first,
-    )
-    filter_grad = place_rows([(r ^ 1) * CHANS for r in before], second, filter_grad)
+    filter_grad = place_rows([r * CHANS for r in [place, place ^ 1] + before], [own, other] + first)
+    filter_grad = place_rows([(r ^ 1) * CHANS for r in before], second, [filter_grad])
     return (gated, grad_proj, filter_grad)
 
 

time: 165 us -> 164 us (level); the launches traced: 165 us -> 161 us
  waiting for transfers between devices: 68.4 us -> 66.5 us
    ppermute x1, waiting for transfers between devices: 25.1 us -> 0.01 us  [body(): other = lax.ppermute(own, 'dp', [(i, i ^ 1) for i in range(8)])]
    all_to_all x1, waiting for transfers between devices: 0.01 us -> 21.6 us  [body(): lax.all_to_all(results.reshape(ROWS, CHANS, 2 * LANES), ('dp', 'ctx'), sp...]
  transfers between devices with their start and end apart: 9 -> 9, of which waited for: 2 -> 4; matrix products, arithmetic and copies ran while one was open for 0% -> 0% of each run, Pallas kernels for 21% -> 21%
where the time goes in v3:
time: 164 us; the launch traced here: 161 us
  waiting for transfers between devices  66.5 us (41%)
  Pallas kernels  54.5 us (33%)
  starting transfers between devices  39.3 us (24%)
    all_to_all x1, waiting for transfers between devices, body(): lax.all_to_all(send.reshape(ROWS, CHANS, 2 * LANES), ('dp', 'ctx'), split...  43.2 us
    all_to_all x1, waiting for transfers between devices, body(): lax.all_to_all(results.reshape(ROWS, CHANS, 2 * LANES), ('dp', 'ctx'), sp...  21.6 us
    pallas_call x1, Pallas kernels, filter_gradient(): pl.pallas_call(lambda *refs: filter_kernel(scale, *refs), grid=(CHANS,),...  18.3 us
    all_to_all x1, starting transfers between devices, body(): lax.all_to_all(send.reshape(ROWS, CHANS, 2 * LANES), ('dp', 'ctx'), split...  16.7 us
    pallas_call x1, Pallas kernels, convolve(): pl.pallas_call(conv_kernel, in_specs=[ANY, ANY], out_specs=ANY, out_shape...  15.5 us
    pallas_call x1, Pallas kernels, toeplitz_tiles(): pl.pallas_call(tile_kernel, grid=(CHANS,), in_specs=[pl.BlockSpec((CHANS,...  9.22 us
    all_to_all x1, starting transfers between devices, body(): lax.all_to_all(results.reshape(ROWS, CHANS, 2 * LANES), ('dp', 'ctx'), sp...  7.43 us
    ppermute x1, starting transfers between devices, body(): other = lax.ppermute(own, 'dp', [(i, i ^ 1) for i in range(8)])  6.45 us
  transfers between devices with their start and end apart: 9, of which 4 were waited for; matrix products, arithmetic and copies ran while one was open for 0% of the time, Pallas kernels for 21%

profile of v3, /device:TPU:1, one launch (start us, length us, event | category | flops | bytes accessed | tf_op | source)
XLA Modules:
  0.0 161.3 jit_solution(8781165154300212979)
XLA Ops:
  0.6 0.0 copy-start
  0.6 3.5 %gate_products.1 = bf16[8,32,16,256]{3,2,1,0:T(8,128)(2,1)} custom-call(bf16[1,128,12288]{2,1,0:T(8,128)(2,1)} %proj_hbm.3, bf16[1,128,4096]{2,1,0:T(8,128)(2,1)} %grad_hbm.3), custom_call_target="tpu_custom_call" | custom-call | flops 1048576 | bytes 6291456 | tf_op jit(solution)/shard_map/gate_products/pallas_call | solution.py:87
  4.1 16.7 %all-to-all-start = ((bf16[256,16,256]{2,1,0:T(8,128)(2,1)}), bf16[256,16,256]{2,1,0:T(8,128)(2,1)}, u32[]{:S(2)}, u32[]{:S(2)}) async-start(bf16[256,16,256]{2,1,0:T(8,128)(2,1)} %bitcast.12), calls=%async_computation | async-start | bytes 4194304 | tf_op jit(solution)/shard_map/all_to_all | solution.py:487
  20.8 0.0 copy-done
  20.9 9.2 %toeplitz_tiles.1.tile_hbm = bf16[16,4,256,256]{3,2,1,0:T(8,128)(2,1)} custom-call(f32[16,4096]{1,0:T(8,128)S(1)} %constant_dynamic-slice_fusion.filter_ref), custom_call_target="tpu_custom_call" | custom-call | flops 8388608 | bytes 9437184 | tf_op jit(solution)/shard_map/toeplitz_tiles/pallas_call | solution.py:132
  30.1 43.2 %all-to-all-done = bf16[256,16,256]{2,1,0:T(8,128)(2,1)} async-done(((bf16[256,16,256]{2,1,0:T(8,128)(2,1)}), bf16[256,16,256]{2,1,0:T(8,128)(2,1)}, u32[]{:S(2)}, u32[]{:S(2)}) %all-to-all-start) | async-done | bytes 2097184 | tf_op jit(solution)/shard_map/all_to_all | solution.py:487
  73.3 15.5 %convolve.1 = bf16[4096,256]{1,0:T(8,128)(2,1)} custom-call(bf16[4096,256]{1,0:T(8,128)(2,1)} %bitcast.1.lanes_hbm.refs_0_, bf16[16,4,256,256]{3,2,1,0:T(8,128)(2,1)} %toeplitz_tiles.1.tile_hbm), custom_call_target="tpu_custom_call" | custom-call | flops 5368709120 | bytes 20971520 | tf_op jit(solution)/shard_map/convolve/pallas_call | solution.py:286
  88.9 7.4 %all-to-all-start.1 = ((bf16[256,16,256]{2,1,0:T(8,128)(2,1)}), bf16[256,16,256]{2,1,0:T(8,128)(2,1)}, u32[]{:S(2)}, u32[]{:S(2)}) async-start(bf16[256,16,256]{2,1,0:T(8,128)(2,1)} %bitcast.13), calls=%async_computation.1 | async-start | bytes 4194304 | tf_op jit(solution)/shard_map/all_to_all | solution.py:493
  96.3 18.3 %filter_gradient.1.refs_1_ = bf16[16,4096]{1,0:T(8,128)(2,1)S(1)} custom-call(bf16[4096,256]{1,0:T(8,128)(2,1)} %bitcast.1.lanes_hbm.refs_0_), custom_call_target="tpu_custom_call" | custom-call | flops 2415919104 | bytes 5242880 | tf_op jit(solution)/shard_map/filter_gradient/pallas_call | solution.py:361
  114.6 6.5 %collective-permute-start = (bf16[16,4096]{1,0:T(8,128)(2,1)S(1)}, bf16[16,4096]{1,0:T(8,128)(2,1)S(1)}, u32[]{:S(2)}, u32[]{:S(2)}) collective-permute-start(bf16[16,4096]{1,0:T(8,128)(2,1)S(1)} %filter_gradient.1.refs_1_), channel_id=1, source_target_pairs={{0,32},{32,0},{64,96},{96,64},{128,160},{160,128},{192,224},{224,1... | collective-permute-start | bytes 393224 | tf_op jit(solution)/shard_map/ppermute | solution.py:500
  121.0 1.2 collective-permute-start.1
  122.2 2.4 %collective-permute-start.2 = (bf16[16,4096]{1,0:T(8,128)(2,1)S(1)}, bf16[16,4096]{1,0:T(8,128)(2,1)S(1)}, u32[]{:S(2)}, u32[]{:S(2)}) collective-permute-start(bf16[16,4096]{1,0:T(8,128)(2,1)S(1)} %filter_gradient.1.refs_1_), channel_id=1, source_target_pairs={{0,128},{32,160},{64,192},{96,224},{128,0},{160,32},{192,64},{224,... | collective-permute-start | bytes 393224 | tf_op jit(solution)/shard_map/ppermute | solution.py:501
  124.6 1.2 collective-permute-start.3
  125.8 21.6 %all-to-all-done.1 = bf16[256,16,256]{2,1,0:T(8,128)(2,1)} async-done(((bf16[256,16,256]{2,1,0:T(8,128)(2,1)}), bf16[256,16,256]{2,1,0:T(8,128)(2,1)}, u32[]{:S(2)}, u32[]{:S(2)}) %all-to-all-start.1) | async-done | bytes 2097184 | tf_op jit(solution)/shard_map/all_to_all | solution.py:493
  147.4 4.9 %gate_results.1 = (bf16[1,128,4096]{2,1,0:T(8,128)(2,1)}, bf16[1,128,12288]{2,1,0:T(8,128)(2,1)}) custom-call(bf16[8,32,16,256]{3,2,1,0:T(8,128)(2,1)} %bitcast.3.lanes_hbm, bf16[1,128,12288]{2,1,0:T(8,128)(2,1)} %proj_hbm.3, bf16[1,128,4096]{2,1,0:T(8,128)(2,1)} %grad_hbm.3), custom_call_target="tpu_custom_call" | custom-call | flops 2097152 | bytes 14680064 | tf_op jit(solution)/shard_map/gate_results/pallas_call | solution.py:460
  152.3 0.0 collective-permute-done.refs_2_
  152.3 0.0 collective-permute-done.1.refs_3_
  152.3 0.0 collective-permute-done.2.refs_4_
  152.3 0.0 collective-permute-done.3.refs_5_
  152.3 0.4 collective-permute-start.4
  152.7 2.4 %collective-permute-start.5 = (bf16[16,4096]{1,0:T(8,128)(2,1)S(1)}, bf16[16,4096]{1,0:T(8,128)(2,1)S(1)}, u32[]{:S(2)}, u32[]{:S(2)}) collective-permute-start(bf16[16,4096]{1,0:T(8,128)(2,1)S(1)} %collective-permute-done.refs_2_), channel_id=1, source_target_pairs={{0,128},{32,160},{64,192},{96,224},{128,0},{160,32},{192,64},{224,... | collective-permute-start | bytes 393224 | tf_op jit(solution)/shard_map/ppermute | solution.py:504
  155.1 1.2 collective-permute-start.6
  156.2 0.1 stack.39.refs_0_
  156.3 0.1 pad_add_fusion.refs_0_
  156.4 1.6 %place_rows_5.1.refs_4_ = f32[128,4096]{1,0:T(8,128)} custom-call(s32[5]{0:T(128)S(1)} %stack.39.refs_0_, bf16[16,4096]{1,0:T(8,128)(2,1)S(1)} %filter_gradient.1.refs_1_, bf16[16,4096]{1,0:T(8,128)(2,1)S(1)} %collective-permute-done.refs_2_, bf16[16,4096]{1,0:T(8,128)(2,1)S(1)} %collective-permute-done.1.refs_3_, ...), custom_call_target="tpu_custom_call" | custom-call | flops 327680 | bytes 1966080 | tf_op jit(solution)/shard_map/place_rows_5/pallas_call | solution.py:399
  158.1 0.0 collective-permute-done.4.refs_1_
  158.1 1.0 collective-permute-done.5.refs_2_
  159.1 0.6 collective-permute-done.6.refs_3_
  159.7 1.5 place_rows_3.1
  (1 shorter events, 0.0 us)
Async XLA Ops:
  0.6 20.2 %copy-start = (f32[128,4096]{1,0:T(8,128)S(1)}, f32[128,4096]{1,0:T(8,128)}, u32[]{:S(2)}) copy-start(f32[128,4096]{1,0:T(8,128)} %param.4) | copy-start | bytes 6291460
  4.1 69.2 %all-to-all-start = ((bf16[256,16,256]{2,1,0:T(8,128)(2,1)}), bf16[256,16,256]{2,1,0:T(8,128)(2,1)}, u32[]{:S(2)}, u32[]{:S(2)}) async-start(bf16[256,16,256]{2,1,0:T(8,128)(2,1)} %bitcast.12), calls=%async_computation | async-start | bytes 4194304 | tf_op jit(solution)/shard_map/all_to_all | solution.py:487
  88.9 58.6 %all-to-all-start.1 = ((bf16[256,16,256]{2,1,0:T(8,128)(2,1)}), bf16[256,16,256]{2,1,0:T(8,128)(2,1)}, u32[]{:S(2)}, u32[]{:S(2)}) async-start(bf16[256,16,256]{2,1,0:T(8,128)(2,1)} %bitcast.13), calls=%async_computation.1 | async-start | bytes 4194304 | tf_op jit(solution)/shard_map/all_to_all | solution.py:493
  114.6 37.7 %collective-permute-start = (bf16[16,4096]{1,0:T(8,128)(2,1)S(1)}, bf16[16,4096]{1,0:T(8,128)(2,1)S(1)}, u32[]{:S(2)}, u32[]{:S(2)}) collective-permute-start(bf16[16,4096]{1,0:T(8,128)(2,1)S(1)} %filter_gradient.1.refs_1_), channel_id=1, source_target_pairs={{0,32},{32,0},{64,96},{96,64},{128,160},{160,128},{192,224},{224,1... | collective-permute-start | bytes 393224 | tf_op jit(solution)/shard_map/ppermute | solution.py:500
  121.0 31.3 %collective-permute-start.1 = (bf16[16,4096]{1,0:T(8,128)(2,1)S(1)}, bf16[16,4096]{1,0:T(8,128)(2,1)S(1)}, u32[]{:S(2)}, u32[]{:S(2)}) collective-permute-start(bf16[16,4096]{1,0:T(8,128)(2,1)S(1)} %filter_gradient.1.refs_1_), channel_id=1, source_target_pairs={{0,64},{32,96},{64,128},{96,160},{128,192},{160,224},{192,0},{224,... | collective-permute-start | bytes 393224 | tf_op jit(solution)/shard_map/ppermute | solution.py:501
  122.2 30.1 %collective-permute-start.2 = (bf16[16,4096]{1,0:T(8,128)(2,1)S(1)}, bf16[16,4096]{1,0:T(8,128)(2,1)S(1)}, u32[]{:S(2)}, u32[]{:S(2)}) collective-permute-start(bf16[16,4096]{1,0:T(8,128)(2,1)S(1)} %filter_gradient.1.refs_1_), channel_id=1, source_target_pairs={{0,128},{32,160},{64,192},{96,224},{128,0},{160,32},{192,64},{224,... | collective-permute-start | bytes 393224 | tf_op jit(solution)/shard_map/ppermute | solution.py:501
  124.6 27.7 %collective-permute-start.3 = (bf16[16,4096]{1,0:T(8,128)(2,1)S(1)}, bf16[16,4096]{1,0:T(8,128)(2,1)S(1)}, u32[]{:S(2)}, u32[]{:S(2)}) collective-permute-start(bf16[16,4096]{1,0:T(8,128)(2,1)S(1)} %filter_gradient.1.refs_1_), channel_id=1, source_target_pairs={{0,192},{32,224},{64,0},{96,32},{128,64},{160,96},{192,128},{224,1... | collective-permute-start | bytes 393224 | tf_op jit(solution)/shard_map/ppermute | solution.py:501
  152.3 5.7 %collective-permute-start.4 = (bf16[16,4096]{1,0:T(8,128)(2,1)S(1)}, bf16[16,4096]{1,0:T(8,128)(2,1)S(1)}, u32[]{:S(2)}, u32[]{:S(2)}) collective-permute-start(bf16[16,4096]{1,0:T(8,128)(2,1)S(1)} %collective-permute-done.refs_2_), channel_id=1, source_target_pairs={{0,64},{32,96},{64,128},{96,160},{128,192},{160,224},{192,0},{224,... | collective-permute-start | bytes 393224 | tf_op jit(solution)/shard_map/ppermute | solution.py:504
  152.7 6.4 %collective-permute-start.5 = (bf16[16,4096]{1,0:T(8,128)(2,1)S(1)}, bf16[16,4096]{1,0:T(8,128)(2,1)S(1)}, u32[]{:S(2)}, u32[]{:S(2)}) collective-permute-start(bf16[16,4096]{1,0:T(8,128)(2,1)S(1)} %collective-permute-done.refs_2_), channel_id=1, source_target_pairs={{0,128},{32,160},{64,192},{96,224},{128,0},{160,32},{192,64},{224,... | collective-permute-start | bytes 393224 | tf_op jit(solution)/shard_map/ppermute | solution.py:504
  155.1 4.6 %collective-permute-start.6 = (bf16[16,4096]{1,0:T(8,128)(2,1)S(1)}, bf16[16,4096]{1,0:T(8,128)(2,1)S(1)}, u32[]{:S(2)}, u32[]{:S(2)}) collective-permute-start(bf16[16,4096]{1,0:T(8,128)(2,1)S(1)} %collective-permute-done.refs_2_), channel_id=1, source_target_pairs={{0,192},{32,224},{64,0},{96,32},{128,64},{160,96},{192,128},{224,1... | collective-permute-start | bytes 393224 | tf_op jit(solution)/shard_map/ppermute | solution.py:504

commit v4 on v3

--- a/solution.py
+++ b/solution.py
@@ -61,7 +61,7 @@
 
     def copy_out(i):
         some = pl.ds(i * PER, PER)
-        return pltpu.make_async_copy(send_ref.at[:, some], send_hbm.at[:, some], out_sems.at[i])
+        return pltpu.make_async_copy(send_ref.at[some], send_hbm.at[some], out_sems.at[i])
 
     for i in range(CHUNKS):
         for copy in copies_in(i):
@@ -75,15 +75,15 @@
                 proj_ref[:, part * LENGTH + first : part * LENGTH + first + LANES].astype(F32) for part in range(3)
             )
             grad = grad_ref[:, first : first + LANES].astype(F32) * query
-            send_ref[:, q, :, 0:LANES] = (key * value).T.astype(BF16).reshape(SEQS, CHANS, LANES)
-            send_ref[:, q, :, LANES:] = grad.T.astype(BF16).reshape(SEQS, CHANS, LANES)
+            send_ref[q, :, :, 0:LANES] = (key * value).T.astype(BF16).reshape(SEQS, CHANS, LANES)
+            send_ref[q, :, :, LANES:] = grad.T.astype(BF16).reshape(SEQS, CHANS, LANES)
         copy_out(i).start()
     for i in range(CHUNKS):
         copy_out(i).wait()
 
 
 def pre(proj, cotangent):
-    shape = (SEQS, BLOCKS, CHANS, 2 * LANES)
+    shape = (BLOCKS, SEQS, CHANS, 2 * LANES)
     return pl.pallas_call(
         pre_kernel,
         in_specs=[ANY, ANY],
@@ -175,7 +175,7 @@
         return pltpu.roll(x, HALF, 1)
 
     def rows_of(t):
-        return [wide_ref[pl.ds(r * CHANS + t, SEQS, stride=BLOCKS * CHANS), :] for r in range(BLOCKS)]
+        return [wide_ref[pl.ds(r * SEQS * CHANS + t, SEQS, stride=CHANS), :] for r in range(BLOCKS)]
 
     def gather_mixed(ref, t):
         own = rows_of(t)
@@ -213,7 +213,7 @@
             here = acc_ref[first : first + SEQS, :]
             before = acc_ref[first - SEQS : first, :] if r else none
             after = acc_ref[first + SEQS : first + tile, :]
-            done_ref[pl.ds(r * CHANS + t, SEQS, stride=BLOCKS * CHANS), :] = here + turn(
+            done_ref[pl.ds(r * SEQS * CHANS + t, SEQS, stride=CHANS), :] = here + turn(
                 jnp.where(left, after, before)
             )
 
@@ -236,7 +236,7 @@
                 odd_far = acc_ref[far + SEQS : far + tile, :]
             else:
                 even_far = odd_far = none
-            done_ref[pl.ds(r * CHANS + t, SEQS, stride=BLOCKS * CHANS), :] = jnp.where(left, even, odd_far) + turn(
+            done_ref[pl.ds(r * SEQS * CHANS + t, SEQS, stride=CHANS), :] = jnp.where(left, even, odd_far) + turn(
                 jnp.where(left, odd, even_far)
             )
 
@@ -317,7 +317,7 @@
         grad_ref[...] = lanes_ref[:, LANES:].astype(F32)
 
     def rows_of(ref):
-        return [ref[pl.ds(r * CHANS + t, SEQS, stride=BLOCKS * CHANS), :] for r in range(BLOCKS)]
+        return [ref[pl.ds(r * SEQS * CHANS + t, SEQS, stride=CHANS), :] for r in range(BLOCKS)]
 
     none = jnp.zeros((SEQS, LANES), F32)
     own = rows_of(mixed_ref)
@@ -415,7 +415,7 @@
 ):
     def copies_in(i):
         some = pl.ds(i * PER, PER)
-        found = [pltpu.make_async_copy(lanes_hbm.at[:, some], lanes_ref.at[:, some], in_sems.at[i, 4])]
+        found = [pltpu.make_async_copy(lanes_hbm.at[some], lanes_ref.at[some], in_sems.at[i, 4])]
         for part in range(3):
             cols = pl.ds(part * LENGTH + i * WIDE, WIDE)
             found.append(
@@ -440,7 +440,7 @@
         for copy in copies_in(i):
             copy.wait()
         for q in range(i * PER, (i + 1) * PER):
-            both = lanes_ref[:, q].reshape(LANES, 2 * LANES).astype(F32)
+            both = lanes_ref[q].reshape(LANES, 2 * LANES).astype(F32)
             conv = both[:, :LANES].T
             back = both[:, LANES:].T
             first = q * LANES
@@ -466,7 +466,7 @@
             pltpu.HBM((1, LANES, 3 * LENGTH), BF16),
         ],
         scratch_shapes=[
-            pltpu.VMEM((SEQS, BLOCKS, CHANS, 2 * LANES), BF16),
+            pltpu.VMEM((BLOCKS, SEQS, CHANS, 2 * LANES), BF16),
             pltpu.VMEM((LANES, 3 * LENGTH), BF16),
             pltpu.VMEM((LANES, LENGTH), BF16),
             pltpu.VMEM((LANES, LENGTH), BF16),
@@ -485,21 +485,21 @@
     scale = 1.0 / math.sqrt(SEQS * LENGTH)
     send = pre(proj, cotangent)
     lanes = lax.all_to_all(
-        send.reshape(ROWS, CHANS, 2 * LANES), ("dp", "ctx"), split_axis=0, concat_axis=0, tiled=True
+        send.reshape(ROWS, CHANS, 2 * LANES), ("ctx", "dp"), split_axis=0, concat_axis=0, tiled=True
     )
     tiles = toeplitz_tiles(lax.dynamic_slice(filters, (place * CHANS, 0), (CHANS, LENGTH)))
     lanes = lanes.reshape(ROWS * CHANS, 2 * LANES)
     results = convolve(lanes, tiles)
     back = lax.all_to_all(
-        results.reshape(ROWS, CHANS, 2 * LANES), ("dp", "ctx"), split_axis=0, concat_axis=0, tiled=True
+        results.reshape(ROWS, CHANS, 2 * LANES), ("ctx", "dp"), split_axis=0, concat_axis=0, tiled=True
     )
 
     own = filter_gradient(lanes, scale)
-    along_x = [[(i, (i + 2 * k) % 8) for i in range(8)] for k in range(1, 4)]
-    before = [(place + 8 - 2 * k) % 8 for k in range(1, 4)]
+    along_x = [[(i, (i + 2 * k) % 8) for i in range(8)] for k in (2, 1, 3)]
+    before = [(place + 8 - 2 * k) % 8 for k in (2, 1, 3)]
     other = lax.ppermute(own, "dp", [(i, i ^ 1) for i in range(8)])
     first = [lax.ppermute(own, "dp", pairs) for pairs in along_x]
-    gated, grad_proj = post(back.reshape(SEQS, BLOCKS, CHANS, 2 * LANES), proj, cotangent)
+    gated, grad_proj = post(back.reshape(BLOCKS, SEQS, CHANS, 2 * LANES), proj, cotangent)
     gated, own, other, *first = lax.optimization_barrier((gated, own, other, *first))
     second = [lax.ppermute(other, "dp", pairs) for pairs in along_x]
     filter_grad = place_rows([r * CHANS for r in [place, place ^ 1] + before], [own, other] + first)

time: 164 us -> 165 us (level)
  the two profiles are of different devices: /device:TPU:1 before, /device:TPU:105 now
where the time goes in v4:
time: 165 us; the launch traced here: 164 us
  waiting for transfers between devices  72.8 us (44%)
  Pallas kernels  53.3 us (32%)
  starting transfers between devices  37.2 us (23%)
    all_to_all x1, waiting for transfers between devices, body(): lax.all_to_all(send.reshape(ROWS, CHANS, 2 * LANES), ('ctx', 'dp'), split...  40.4 us
    all_to_all x1, waiting for transfers between devices, body(): lax.all_to_all(results.reshape(ROWS, CHANS, 2 * LANES), ('ctx', 'dp'), sp...  27.8 us
    pallas_call x1, Pallas kernels, filter_gradient(): pl.pallas_call(lambda *refs: filter_kernel(scale, *refs), grid=(CHANS,),...  18 us
    all_to_all x1, starting transfers between devices, body(): lax.all_to_all(send.reshape(ROWS, CHANS, 2 * LANES), ('ctx', 'dp'), split...  15.3 us
    pallas_call x1, Pallas kernels, convolve(): pl.pallas_call(conv_kernel, in_specs=[ANY, ANY], out_specs=ANY, out_shape...  14.6 us
    all_to_all x1, starting transfers between devices, body(): lax.all_to_all(results.reshape(ROWS, CHANS, 2 * LANES), ('ctx', 'dp'), sp...  10.1 us
    pallas_call x1, Pallas kernels, toeplitz_tiles(): pl.pallas_call(tile_kernel, grid=(CHANS,), in_specs=[pl.BlockSpec((CHANS,...  9.22 us
    ppermute x3, starting transfers between devices, body(): first = [lax.ppermute(own, 'dp', pairs) for pairs in along_x]  5.4 us
  transfers between devices with their start and end apart: 9, of which 4 were waited for; matrix products, arithmetic and copies ran while one was open for 0% of the time, Pallas kernels for 21%

profile of v4, /device:TPU:105, one launch (start us, length us, event | category | flops | bytes accessed | tf_op | source)
XLA Modules:
  0.0 164.4 jit_solution(11118254110921757935)
XLA Ops:
  0.6 0.0 copy-start
  0.6 3.5 %gate_products.1 = bf16[32,8,16,256]{3,2,1,0:T(8,128)(2,1)} custom-call(bf16[1,128,12288]{2,1,0:T(8,128)(2,1)} %proj_hbm.3, bf16[1,128,4096]{2,1,0:T(8,128)(2,1)} %grad_hbm.3), custom_call_target="tpu_custom_call" | custom-call | flops 1048576 | bytes 6291456 | tf_op jit(solution)/shard_map/gate_products/pallas_call | solution.py:87
  4.1 15.3 %all-to-all-start = ((bf16[256,16,256]{2,1,0:T(8,128)(2,1)}), bf16[256,16,256]{2,1,0:T(8,128)(2,1)}, u32[]{:S(2)}, u32[]{:S(2)}) async-start(bf16[256,16,256]{2,1,0:T(8,128)(2,1)} %bitcast.12), calls=%async_computation | async-start | bytes 4194304 | tf_op jit(solution)/shard_map/all_to_all | solution.py:487
  19.4 0.0 copy-done
  19.5 9.2 %toeplitz_tiles.1.tile_hbm = bf16[16,4,256,256]{3,2,1,0:T(8,128)(2,1)} custom-call(f32[16,4096]{1,0:T(8,128)S(1)} %constant_dynamic-slice_fusion.filter_ref), custom_call_target="tpu_custom_call" | custom-call | flops 8388608 | bytes 9437184 | tf_op jit(solution)/shard_map/toeplitz_tiles/pallas_call | solution.py:132
  28.7 40.4 %all-to-all-done = bf16[256,16,256]{2,1,0:T(8,128)(2,1)} async-done(((bf16[256,16,256]{2,1,0:T(8,128)(2,1)}), bf16[256,16,256]{2,1,0:T(8,128)(2,1)}, u32[]{:S(2)}, u32[]{:S(2)}) %all-to-all-start) | async-done | bytes 2097184 | tf_op jit(solution)/shard_map/all_to_all | solution.py:487
  69.1 14.6 %convolve.1 = bf16[4096,256]{1,0:T(8,128)(2,1)} custom-call(bf16[4096,256]{1,0:T(8,128)(2,1)} %bitcast.1.lanes_hbm.refs_0_, bf16[16,4,256,256]{3,2,1,0:T(8,128)(2,1)} %toeplitz_tiles.1.tile_hbm), custom_call_target="tpu_custom_call" | custom-call | flops 5368709120 | bytes 20971520 | tf_op jit(solution)/shard_map/convolve/pallas_call | solution.py:286
  83.7 10.1 %all-to-all-start.1 = ((bf16[256,16,256]{2,1,0:T(8,128)(2,1)}), bf16[256,16,256]{2,1,0:T(8,128)(2,1)}, u32[]{:S(2)}, u32[]{:S(2)}) async-start(bf16[256,16,256]{2,1,0:T(8,128)(2,1)} %bitcast.13), calls=%async_computation.1 | async-start | bytes 4194304 | tf_op jit(solution)/shard_map/all_to_all | solution.py:493
  93.9 18.0 %filter_gradient.1.refs_1_ = bf16[16,4096]{1,0:T(8,128)(2,1)S(1)} custom-call(bf16[4096,256]{1,0:T(8,128)(2,1)} %bitcast.1.lanes_hbm.refs_0_), custom_call_target="tpu_custom_call" | custom-call | flops 2415919104 | bytes 5242880 | tf_op jit(solution)/shard_map/filter_gradient/pallas_call | solution.py:361
  111.9 3.6 %collective-permute-start = (bf16[16,4096]{1,0:T(8,128)(2,1)S(1)}, bf16[16,4096]{1,0:T(8,128)(2,1)S(1)}, u32[]{:S(2)}, u32[]{:S(2)}) collective-permute-start(bf16[16,4096]{1,0:T(8,128)(2,1)S(1)} %filter_gradient.1.refs_1_), channel_id=1, source_target_pairs={{0,32},{32,0},{64,96},{96,64},{128,160},{160,128},{192,224},{224,1... | collective-permute-start | bytes 393224 | tf_op jit(solution)/shard_map/ppermute | solution.py:500
  115.5 2.7 %collective-permute-start.1 = (bf16[16,4096]{1,0:T(8,128)(2,1)S(1)}, bf16[16,4096]{1,0:T(8,128)(2,1)S(1)}, u32[]{:S(2)}, u32[]{:S(2)}) collective-permute-start(bf16[16,4096]{1,0:T(8,128)(2,1)S(1)} %filter_gradient.1.refs_1_), channel_id=1, source_target_pairs={{0,128},{32,160},{64,192},{96,224},{128,0},{160,32},{192,64},{224,... | collective-permute-start | bytes 393224 | tf_op jit(solution)/shard_map/ppermute | solution.py:501
  118.2 0.3 collective-permute-start.2
  118.5 2.4 %collective-permute-start.3 = (bf16[16,4096]{1,0:T(8,128)(2,1)S(1)}, bf16[16,4096]{1,0:T(8,128)(2,1)S(1)}, u32[]{:S(2)}, u32[]{:S(2)}) collective-permute-start(bf16[16,4096]{1,0:T(8,128)(2,1)S(1)} %filter_gradient.1.refs_1_), channel_id=1, source_target_pairs={{0,192},{32,224},{64,0},{96,32},{128,64},{160,96},{192,128},{224,1... | collective-permute-start | bytes 393224 | tf_op jit(solution)/shard_map/ppermute | solution.py:501
  120.9 27.8 %all-to-all-done.1 = bf16[256,16,256]{2,1,0:T(8,128)(2,1)} async-done(((bf16[256,16,256]{2,1,0:T(8,128)(2,1)}), bf16[256,16,256]{2,1,0:T(8,128)(2,1)}, u32[]{:S(2)}, u32[]{:S(2)}) %all-to-all-start.1) | async-done | bytes 2097184 | tf_op jit(solution)/shard_map/all_to_all | solution.py:493
  148.7 4.9 %gate_results.1 = (bf16[1,128,4096]{2,1,0:T(8,128)(2,1)}, bf16[1,128,12288]{2,1,0:T(8,128)(2,1)}) custom-call(bf16[32,8,16,256]{3,2,1,0:T(8,128)(2,1)} %bitcast.3.lanes_hbm, bf16[1,128,12288]{2,1,0:T(8,128)(2,1)} %proj_hbm.3, bf16[1,128,4096]{2,1,0:T(8,128)(2,1)} %grad_hbm.3), custom_call_target="tpu_custom_call" | custom-call | flops 2097152 | bytes 14680064 | tf_op jit(solution)/shard_map/gate_results/pallas_call | solution.py:460
  153.5 0.0 collective-permute-done.refs_2_
  153.5 0.0 collective-permute-done.1.refs_3_
  153.5 0.0 collective-permute-done.2.refs_4_
  153.6 0.0 collective-permute-done.3.refs_5_
  153.6 0.1 collective-permute-start.4
  153.7 0.5 collective-permute-start.5
  154.2 2.2 %collective-permute-start.6 = (bf16[16,4096]{1,0:T(8,128)(2,1)S(1)}, bf16[16,4096]{1,0:T(8,128)(2,1)S(1)}, u32[]{:S(2)}, u32[]{:S(2)}) collective-permute-start(bf16[16,4096]{1,0:T(8,128)(2,1)S(1)} %collective-permute-done.refs_2_), channel_id=1, source_target_pairs={{0,192},{32,224},{64,0},{96,32},{128,64},{160,96},{192,128},{224,1... | collective-permute-start | bytes 393224 | tf_op jit(solution)/shard_map/ppermute | solution.py:504
  156.4 0.1 stack.39.refs_0_
  156.5 0.1 pad_add_fusion.refs_0_
  156.6 1.6 %place_rows_5.1.refs_4_ = f32[128,4096]{1,0:T(8,128)} custom-call(s32[5]{0:T(128)S(1)} %stack.39.refs_0_, bf16[16,4096]{1,0:T(8,128)(2,1)S(1)} %filter_gradient.1.refs_1_, bf16[16,4096]{1,0:T(8,128)(2,1)S(1)} %collective-permute-done.refs_2_, bf16[16,4096]{1,0:T(8,128)(2,1)S(1)} %collective-permute-done.1.refs_3_, ...), custom_call_target="tpu_custom_call" | custom-call | flops 327680 | bytes 1966080 | tf_op jit(solution)/shard_map/place_rows_5/pallas_call | solution.py:399
  158.2 2.1 %collective-permute-done.4.refs_1_ = bf16[16,4096]{1,0:T(8,128)(2,1)S(1)} collective-permute-done((bf16[16,4096]{1,0:T(8,128)(2,1)S(1)}, bf16[16,4096]{1,0:T(8,128)(2,1)S(1)}, u32[]{:S(2)}, u32[]{:S(2)}) %collective-permute-start.4) | collective-permute-done | bytes 131104 | tf_op jit(solution)/shard_map/ppermute | solution.py:504
  160.4 2.5 %collective-permute-done.5.refs_2_ = bf16[16,4096]{1,0:T(8,128)(2,1)S(1)} collective-permute-done((bf16[16,4096]{1,0:T(8,128)(2,1)S(1)}, bf16[16,4096]{1,0:T(8,128)(2,1)S(1)}, u32[]{:S(2)}, u32[]{:S(2)}) %collective-permute-start.5) | collective-permute-done | bytes 131104 | tf_op jit(solution)/shard_map/ppermute | solution.py:504
  162.8 0.0 collective-permute-done.6.refs_3_
  162.8 1.5 place_rows_3.1
  (1 shorter events, 0.0 us)
Async XLA Ops:
  0.6 18.8 %copy-start = (f32[128,4096]{1,0:T(8,128)S(1)}, f32[128,4096]{1,0:T(8,128)}, u32[]{:S(2)}) copy-start(f32[128,4096]{1,0:T(8,128)} %param.4) | copy-start | bytes 6291460
  4.1 65.0 %all-to-all-start = ((bf16[256,16,256]{2,1,0:T(8,128)(2,1)}), bf16[256,16,256]{2,1,0:T(8,128)(2,1)}, u32[]{:S(2)}, u32[]{:S(2)}) async-start(bf16[256,16,256]{2,1,0:T(8,128)(2,1)} %bitcast.12), calls=%async_computation | async-start | bytes 4194304 | tf_op jit(solution)/shard_map/all_to_all | solution.py:487
  83.7 64.9 %all-to-all-start.1 = ((bf16[256,16,256]{2,1,0:T(8,128)(2,1)}), bf16[256,16,256]{2,1,0:T(8,128)(2,1)}, u32[]{:S(2)}, u32[]{:S(2)}) async-start(bf16[256,16,256]{2,1,0:T(8,128)(2,1)} %bitcast.13), calls=%async_computation.1 | async-start | bytes 4194304 | tf_op jit(solution)/shard_map/all_to_all | solution.py:493
  111.9 41.6 %collective-permute-start = (bf16[16,4096]{1,0:T(8,128)(2,1)S(1)}, bf16[16,4096]{1,0:T(8,128)(2,1)S(1)}, u32[]{:S(2)}, u32[]{:S(2)}) collective-permute-start(bf16[16,4096]{1,0:T(8,128)(2,1)S(1)} %filter_gradient.1.refs_1_), channel_id=1, source_target_pairs={{0,32},{32,0},{64,96},{96,64},{128,160},{160,128},{192,224},{224,1... | collective-permute-start | bytes 393224 | tf_op jit(solution)/shard_map/ppermute | solution.py:500
  115.5 38.1 %collective-permute-start.1 = (bf16[16,4096]{1,0:T(8,128)(2,1)S(1)}, bf16[16,4096]{1,0:T(8,128)(2,1)S(1)}, u32[]{:S(2)}, u32[]{:S(2)}) collective-permute-start(bf16[16,4096]{1,0:T(8,128)(2,1)S(1)} %filter_gradient.1.refs_1_), channel_id=1, source_target_pairs={{0,128},{32,160},{64,192},{96,224},{128,0},{160,32},{192,64},{224,... | collective-permute-start | bytes 393224 | tf_op jit(solution)/shard_map/ppermute | solution.py:501
  118.2 35.3 %collective-permute-start.2 = (bf16[16,4096]{1,0:T(8,128)(2,1)S(1)}, bf16[16,4096]{1,0:T(8,128)(2,1)S(1)}, u32[]{:S(2)}, u32[]{:S(2)}) collective-permute-start(bf16[16,4096]{1,0:T(8,128)(2,1)S(1)} %filter_gradient.1.refs_1_), channel_id=1, source_target_pairs={{0,64},{32,96},{64,128},{96,160},{128,192},{160,224},{192,0},{224,... | collective-permute-start | bytes 393224 | tf_op jit(solution)/shard_map/ppermute | solution.py:501
  118.5 35.0 %collective-permute-start.3 = (bf16[16,4096]{1,0:T(8,128)(2,1)S(1)}, bf16[16,4096]{1,0:T(8,128)(2,1)S(1)}, u32[]{:S(2)}, u32[]{:S(2)}) collective-permute-start(bf16[16,4096]{1,0:T(8,128)(2,1)S(1)} %filter_gradient.1.refs_1_), channel_id=1, source_target_pairs={{0,192},{32,224},{64,0},{96,32},{128,64},{160,96},{192,128},{224,1... | collective-permute-start | bytes 393224 | tf_op jit(solution)/shard_map/ppermute | solution.py:501
  153.6 6.8 %collective-permute-start.4 = (bf16[16,4096]{1,0:T(8,128)(2,1)S(1)}, bf16[16,4096]{1,0:T(8,128)(2,1)S(1)}, u32[]{:S(2)}, u32[]{:S(2)}) collective-permute-start(bf16[16,4096]{1,0:T(8,128)(2,1)S(1)} %collective-permute-done.refs_2_), channel_id=1, source_target_pairs={{0,128},{32,160},{64,192},{96,224},{128,0},{160,32},{192,64},{224,... | collective-permute-start | bytes 393224 | tf_op jit(solution)/shard_map/ppermute | solution.py:504
  153.7 9.2 %collective-permute-start.5 = (bf16[16,4096]{1,0:T(8,128)(2,1)S(1)}, bf16[16,4096]{1,0:T(8,128)(2,1)S(1)}, u32[]{:S(2)}, u32[]{:S(2)}) collective-permute-start(bf16[16,4096]{1,0:T(8,128)(2,1)S(1)} %collective-permute-done.refs_2_), channel_id=1, source_target_pairs={{0,64},{32,96},{64,128},{96,160},{128,192},{160,224},{192,0},{224,... | collective-permute-start | bytes 393224 | tf_op jit(solution)/shard_map/ppermute | solution.py:504
  154.2 8.6 %collective-permute-start.6 = (bf16[16,4096]{1,0:T(8,128)(2,1)S(1)}, bf16[16,4096]{1,0:T(8,128)(2,1)S(1)}, u32[]{:S(2)}, u32[]{:S(2)}) collective-permute-start(bf16[16,4096]{1,0:T(8,128)(2,1)S(1)} %collective-permute-done.refs_2_), channel_id=1, source_target_pairs={{0,192},{32,224},{64,0},{96,32},{128,64},{160,96},{192,128},{224,1... | collective-permute-start | bytes 393224 | tf_op jit(solution)/shard_map/ppermute | solution.py:504

commit v5 on v3

--- a/solution.py
+++ b/solution.py
@@ -61,7 +61,7 @@
 
     def copy_out(i):
         some = pl.ds(i * PER, PER)
-        return pltpu.make_async_copy(send_ref.at[:, some], send_hbm.at[:, some], out_sems.at[i])
+        return pltpu.make_async_copy(send_ref.at[some], send_hbm.at[some], out_sems.at[i])
 
     for i in range(CHUNKS):
         for copy in copies_in(i):
@@ -75,15 +75,15 @@
                 proj_ref[:, part * LENGTH + first : part * LENGTH + first + LANES].astype(F32) for part in range(3)
             )
             grad = grad_ref[:, first : first + LANES].astype(F32) * query
-            send_ref[:, q, :, 0:LANES] = (key * value).T.astype(BF16).reshape(SEQS, CHANS, LANES)
-            send_ref[:, q, :, LANES:] = grad.T.astype(BF16).reshape(SEQS, CHANS, LANES)
+            send_ref[q, :, :, 0:LANES] = (key * value).T.astype(BF16).reshape(SEQS, CHANS, LANES)
+            send_ref[q, :, :, LANES:] = grad.T.astype(BF16).reshape(SEQS, CHANS, LANES)
         copy_out(i).start()
     for i in range(CHUNKS):
         copy_out(i).wait()
 
 
 def pre(proj, cotangent):
-    shape = (SEQS, BLOCKS, CHANS, 2 * LANES)
+    shape = (BLOCKS, SEQS, CHANS, 2 * LANES)
     return pl.pallas_call(
         pre_kernel,
         in_specs=[ANY, ANY],
@@ -175,7 +175,7 @@
         return pltpu.roll(x, HALF, 1)
 
     def rows_of(t):
-        return [wide_ref[pl.ds(r * CHANS + t, SEQS, stride=BLOCKS * CHANS), :] for r in range(BLOCKS)]
+        return [wide_ref[pl.ds(r * SEQS * CHANS + t, SEQS, stride=CHANS), :] for r in range(BLOCKS)]
 
     def gather_mixed(ref, t):
         own = rows_of(t)
@@ -317,7 +317,7 @@
         grad_ref[...] = lanes_ref[:, LANES:].astype(F32)
 
     def rows_of(ref):
-        return [ref[pl.ds(r * CHANS + t, SEQS, stride=BLOCKS * CHANS), :] for r in range(BLOCKS)]
+        return [ref[pl.ds(r * SEQS * CHANS + t, SEQS, stride=CHANS), :] for r in range(BLOCKS)]
 
     none = jnp.zeros((SEQS, LANES), F32)
     own = rows_of(mixed_ref)
@@ -485,7 +485,7 @@
     scale = 1.0 / math.sqrt(SEQS * LENGTH)
     send = pre(proj, cotangent)
     lanes = lax.all_to_all(
-        send.reshape(ROWS, CHANS, 2 * LANES), ("dp", "ctx"), split_axis=0, concat_axis=0, tiled=True
+        send.reshape(ROWS, CHANS, 2 * LANES), ("ctx", "dp"), split_axis=0, concat_axis=0, tiled=True
     )
     tiles = toeplitz_tiles(lax.dynamic_slice(filters, (place * CHANS, 0), (CHANS, LENGTH)))
     lanes = lanes.reshape(ROWS * CHANS, 2 * LANES)

time: 164 us -> 163 us (level)
  no operation moved by 1% of the time
where the time goes in v5:
time: 163 us; the launch traced here: 160 us
  waiting for transfers between devices  65.7 us (40%)
  Pallas kernels  53.6 us (33%)
  starting transfers between devices  40.1 us (25%)
    all_to_all x1, waiting for transfers between devices, body(): lax.all_to_all(send.reshape(ROWS, CHANS, 2 * LANES), ('ctx', 'dp'), split...  42.2 us
    all_to_all x1, waiting for transfers between devices, body(): lax.all_to_all(results.reshape(ROWS, CHANS, 2 * LANES), ('dp', 'ctx'), sp...  21.8 us
    pallas_call x1, Pallas kernels, filter_gradient(): pl.pallas_call(lambda *refs: filter_kernel(scale, *refs), grid=(CHANS,),...  18 us
    all_to_all x1, starting transfers between devices, body(): lax.all_to_all(send.reshape(ROWS, CHANS, 2 * LANES), ('ctx', 'dp'), split...  16.7 us
    pallas_call x1, Pallas kernels, convolve(): pl.pallas_call(conv_kernel, in_specs=[ANY, ANY], out_specs=ANY, out_shape...  14.9 us
    pallas_call x1, Pallas kernels, toeplitz_tiles(): pl.pallas_call(tile_kernel, grid=(CHANS,), in_specs=[pl.BlockSpec((CHANS,...  9.22 us
    all_to_all x1, starting transfers between devices, body(): lax.all_to_all(results.reshape(ROWS, CHANS, 2 * LANES), ('dp', 'ctx'), sp...  8.27 us
    ppermute x1, starting transfers between devices, body(): other = lax.ppermute(own, 'dp', [(i, i ^ 1) for i in range(8)])  6.41 us
  transfers between devices with their start and end apart: 9, of which 4 were waited for; matrix products, arithmetic and copies ran while one was open for 0% of the time, Pallas kernels for 21%

profile of v5, /device:TPU:1, one launch (start us, length us, event | category | flops | bytes accessed | tf_op | source)
XLA Modules:
  0.0 160.4 jit_solution(6335462850547389637)
XLA Ops:
  0.6 0.0 copy-start
  0.6 3.5 %gate_products.1 = bf16[32,8,16,256]{3,2,1,0:T(8,128)(2,1)} custom-call(bf16[1,128,12288]{2,1,0:T(8,128)(2,1)} %proj_hbm.3, bf16[1,128,4096]{2,1,0:T(8,128)(2,1)} %grad_hbm.3), custom_call_target="tpu_custom_call" | custom-call | flops 1048576 | bytes 6291456 | tf_op jit(solution)/shard_map/gate_products/pallas_call | solution.py:87
  4.1 16.7 %all-to-all-start = ((bf16[256,16,256]{2,1,0:T(8,128)(2,1)}), bf16[256,16,256]{2,1,0:T(8,128)(2,1)}, u32[]{:S(2)}, u32[]{:S(2)}) async-start(bf16[256,16,256]{2,1,0:T(8,128)(2,1)} %bitcast.12), calls=%async_computation | async-start | bytes 4194304 | tf_op jit(solution)/shard_map/all_to_all | solution.py:487
  20.8 0.0 copy-done
  20.9 9.2 %toeplitz_tiles.1.tile_hbm = bf16[16,4,256,256]{3,2,1,0:T(8,128)(2,1)} custom-call(f32[16,4096]{1,0:T(8,128)S(1)} %constant_dynamic-slice_fusion.filter_ref), custom_call_target="tpu_custom_call" | custom-call | flops 8388608 | bytes 9437184 | tf_op jit(solution)/shard_map/toeplitz_tiles/pallas_call | solution.py:132
  30.1 42.2 %all-to-all-done = bf16[256,16,256]{2,1,0:T(8,128)(2,1)} async-done(((bf16[256,16,256]{2,1,0:T(8,128)(2,1)}), bf16[256,16,256]{2,1,0:T(8,128)(2,1)}, u32[]{:S(2)}, u32[]{:S(2)}) %all-to-all-start) | async-done | bytes 2097184 | tf_op jit(solution)/shard_map/all_to_all | solution.py:487
  72.3 14.9 %convolve.1 = bf16[4096,256]{1,0:T(8,128)(2,1)} custom-call(bf16[4096,256]{1,0:T(8,128)(2,1)} %bitcast.1.lanes_hbm.refs_0_, bf16[16,4,256,256]{3,2,1,0:T(8,128)(2,1)} %toeplitz_tiles.1.tile_hbm), custom_call_target="tpu_custom_call" | custom-call | flops 5368709120 | bytes 20971520 | tf_op jit(solution)/shard_map/convolve/pallas_call | solution.py:286
  87.2 8.3 %all-to-all-start.1 = ((bf16[256,16,256]{2,1,0:T(8,128)(2,1)}), bf16[256,16,256]{2,1,0:T(8,128)(2,1)}, u32[]{:S(2)}, u32[]{:S(2)}) async-start(bf16[256,16,256]{2,1,0:T(8,128)(2,1)} %bitcast.13), calls=%async_computation.1 | async-start | bytes 4194304 | tf_op jit(solution)/shard_map/all_to_all | solution.py:493
  95.4 18.0 %filter_gradient.1.refs_1_ = bf16[16,4096]{1,0:T(8,128)(2,1)S(1)} custom-call(bf16[4096,256]{1,0:T(8,128)(2,1)} %bitcast.1.lanes_hbm.refs_0_), custom_call_target="tpu_custom_call" | custom-call | flops 2415919104 | bytes 5242880 | tf_op jit(solution)/shard_map/filter_gradient/pallas_call | solution.py:361
  113.5 6.4 %collective-permute-start = (bf16[16,4096]{1,0:T(8,128)(2,1)S(1)}, bf16[16,4096]{1,0:T(8,128)(2,1)S(1)}, u32[]{:S(2)}, u32[]{:S(2)}) collective-permute-start(bf16[16,4096]{1,0:T(8,128)(2,1)S(1)} %filter_gradient.1.refs_1_), channel_id=1, source_target_pairs={{0,32},{32,0},{64,96},{96,64},{128,160},{160,128},{192,224},{224,1... | collective-permute-start | bytes 393224 | tf_op jit(solution)/shard_map/ppermute | solution.py:500
  119.9 1.2 collective-permute-start.1
  121.1 2.4 %collective-permute-start.2 = (bf16[16,4096]{1,0:T(8,128)(2,1)S(1)}, bf16[16,4096]{1,0:T(8,128)(2,1)S(1)}, u32[]{:S(2)}, u32[]{:S(2)}) collective-permute-start(bf16[16,4096]{1,0:T(8,128)(2,1)S(1)} %filter_gradient.1.refs_1_), channel_id=1, source_target_pairs={{0,128},{32,160},{64,192},{96,224},{128,0},{160,32},{192,64},{224,... | collective-permute-start | bytes 393224 | tf_op jit(solution)/shard_map/ppermute | solution.py:501
  123.5 1.2 collective-permute-start.3
  124.7 21.8 %all-to-all-done.1 = bf16[256,16,256]{2,1,0:T(8,128)(2,1)} async-done(((bf16[256,16,256]{2,1,0:T(8,128)(2,1)}), bf16[256,16,256]{2,1,0:T(8,128)(2,1)}, u32[]{:S(2)}, u32[]{:S(2)}) %all-to-all-start.1) | async-done | bytes 2097184 | tf_op jit(solution)/shard_map/all_to_all | solution.py:493
  146.5 4.9 %gate_results.1 = (bf16[1,128,4096]{2,1,0:T(8,128)(2,1)}, bf16[1,128,12288]{2,1,0:T(8,128)(2,1)}) custom-call(bf16[8,32,16,256]{3,2,1,0:T(8,128)(2,1)} %bitcast.3.lanes_hbm, bf16[1,128,12288]{2,1,0:T(8,128)(2,1)} %proj_hbm.3, bf16[1,128,4096]{2,1,0:T(8,128)(2,1)} %grad_hbm.3), custom_call_target="tpu_custom_call" | custom-call | flops 2097152 | bytes 14680064 | tf_op jit(solution)/shard_map/gate_results/pallas_call | solution.py:460
  151.4 0.0 collective-permute-done.refs_2_
  151.4 0.0 collective-permute-done.1.refs_3_
  151.4 0.0 collective-permute-done.2.refs_4_
  151.4 0.0 collective-permute-done.3.refs_5_
  151.4 0.4 collective-permute-start.4
  151.8 2.4 %collective-permute-start.5 = (bf16[16,4096]{1,0:T(8,128)(2,1)S(1)}, bf16[16,4096]{1,0:T(8,128)(2,1)S(1)}, u32[]{:S(2)}, u32[]{:S(2)}) collective-permute-start(bf16[16,4096]{1,0:T(8,128)(2,1)S(1)} %collective-permute-done.refs_2_), channel_id=1, source_target_pairs={{0,128},{32,160},{64,192},{96,224},{128,0},{160,32},{192,64},{224,... | collective-permute-start | bytes 393224 | tf_op jit(solution)/shard_map/ppermute | solution.py:504
  154.2 1.2 collective-permute-start.6
  155.3 0.1 stack.39.refs_0_
  155.4 0.1 pad_add_fusion.refs_0_
  155.5 1.6 %place_rows_5.1.refs_4_ = f32[128,4096]{1,0:T(8,128)} custom-call(s32[5]{0:T(128)S(1)} %stack.39.refs_0_, bf16[16,4096]{1,0:T(8,128)(2,1)S(1)} %filter_gradient.1.refs_1_, bf16[16,4096]{1,0:T(8,128)(2,1)S(1)} %collective-permute-done.refs_2_, bf16[16,4096]{1,0:T(8,128)(2,1)S(1)} %collective-permute-done.1.refs_3_, ...), custom_call_target="tpu_custom_call" | custom-call | flops 327680 | bytes 1966080 | tf_op jit(solution)/shard_map/place_rows_5/pallas_call | solution.py:399
  157.2 0.0 collective-permute-done.4.refs_1_
  157.2 1.0 collective-permute-done.5.refs_2_
  158.2 0.6 collective-permute-done.6.refs_3_
  158.8 1.5 place_rows_3.1
  (1 shorter events, 0.0 us)
Async XLA Ops:
  0.6 20.2 %copy-start = (f32[128,4096]{1,0:T(8,128)S(1)}, f32[128,4096]{1,0:T(8,128)}, u32[]{:S(2)}) copy-start(f32[128,4096]{1,0:T(8,128)} %param.4) | copy-start | bytes 6291460
  4.1 68.1 %all-to-all-start = ((bf16[256,16,256]{2,1,0:T(8,128)(2,1)}), bf16[256,16,256]{2,1,0:T(8,128)(2,1)}, u32[]{:S(2)}, u32[]{:S(2)}) async-start(bf16[256,16,256]{2,1,0:T(8,128)(2,1)} %bitcast.12), calls=%async_computation | async-start | bytes 4194304 | tf_op jit(solution)/shard_map/all_to_all | solution.py:487
  87.2 59.3 %all-to-all-start.1 = ((bf16[256,16,256]{2,1,0:T(8,128)(2,1)}), bf16[256,16,256]{2,1,0:T(8,128)(2,1)}, u32[]{:S(2)}, u32[]{:S(2)}) async-start(bf16[256,16,256]{2,1,0:T(8,128)(2,1)} %bitcast.13), calls=%async_computation.1 | async-start | bytes 4194304 | tf_op jit(solution)/shard_map/all_to_all | solution.py:493
  113.5 37.9 %collective-permute-start = (bf16[16,4096]{1,0:T(8,128)(2,1)S(1)}, bf16[16,4096]{1,0:T(8,128)(2,1)S(1)}, u32[]{:S(2)}, u32[]{:S(2)}) collective-permute-start(bf16[16,4096]{1,0:T(8,128)(2,1)S(1)} %filter_gradient.1.refs_1_), channel_id=1, source_target_pairs={{0,32},{32,0},{64,96},{96,64},{128,160},{160,128},{192,224},{224,1... | collective-permute-start | bytes 393224 | tf_op jit(solution)/shard_map/ppermute | solution.py:500
  119.9 31.5 %collective-permute-start.1 = (bf16[16,4096]{1,0:T(8,128)(2,1)S(1)}, bf16[16,4096]{1,0:T(8,128)(2,1)S(1)}, u32[]{:S(2)}, u32[]{:S(2)}) collective-permute-start(bf16[16,4096]{1,0:T(8,128)(2,1)S(1)} %filter_gradient.1.refs_1_), channel_id=1, source_target_pairs={{0,64},{32,96},{64,128},{96,160},{128,192},{160,224},{192,0},{224,... | collective-permute-start | bytes 393224 | tf_op jit(solution)/shard_map/ppermute | solution.py:501
  121.1 30.3 %collective-permute-start.2 = (bf16[16,4096]{1,0:T(8,128)(2,1)S(1)}, bf16[16,4096]{1,0:T(8,128)(2,1)S(1)}, u32[]{:S(2)}, u32[]{:S(2)}) collective-permute-start(bf16[16,4096]{1,0:T(8,128)(2,1)S(1)} %filter_gradient.1.refs_1_), channel_id=1, source_target_pairs={{0,128},{32,160},{64,192},{96,224},{128,0},{160,32},{192,64},{224,... | collective-permute-start | bytes 393224 | tf_op jit(solution)/shard_map/ppermute | solution.py:501
  123.5 27.9 %collective-permute-start.3 = (bf16[16,4096]{1,0:T(8,128)(2,1)S(1)}, bf16[16,4096]{1,0:T(8,128)(2,1)S(1)}, u32[]{:S(2)}, u32[]{:S(2)}) collective-permute-start(bf16[16,4096]{1,0:T(8,128)(2,1)S(1)} %filter_gradient.1.refs_1_), channel_id=1, source_target_pairs={{0,192},{32,224},{64,0},{96,32},{128,64},{160,96},{192,128},{224,1... | collective-permute-start | bytes 393224 | tf_op jit(solution)/shard_map/ppermute | solution.py:501
  151.4 5.7 %collective-permute-start.4 = (bf16[16,4096]{1,0:T(8,128)(2,1)S(1)}, bf16[16,4096]{1,0:T(8,128)(2,1)S(1)}, u32[]{:S(2)}, u32[]{:S(2)}) collective-permute-start(bf16[16,4096]{1,0:T(8,128)(2,1)S(1)} %collective-permute-done.refs_2_), channel_id=1, source_target_pairs={{0,64},{32,96},{64,128},{96,160},{128,192},{160,224},{192,0},{224,... | collective-permute-start | bytes 393224 | tf_op jit(solution)/shard_map/ppermute | solution.py:504
  151.8 6.4 %collective-permute-start.5 = (bf16[16,4096]{1,0:T(8,128)(2,1)S(1)}, bf16[16,4096]{1,0:T(8,128)(2,1)S(1)}, u32[]{:S(2)}, u32[]{:S(2)}) collective-permute-start(bf16[16,4096]{1,0:T(8,128)(2,1)S(1)} %collective-permute-done.refs_2_), channel_id=1, source_target_pairs={{0,128},{32,160},{64,192},{96,224},{128,0},{160,32},{192,64},{224,... | collective-permute-start | bytes 393224 | tf_op jit(solution)/shard_map/ppermute | solution.py:504
  154.2 4.6 %collective-permute-start.6 = (bf16[16,4096]{1,0:T(8,128)(2,1)S(1)}, bf16[16,4096]{1,0:T(8,128)(2,1)S(1)}, u32[]{:S(2)}, u32[]{:S(2)}) collective-permute-start(bf16[16,4096]{1,0:T(8,128)(2,1)S(1)} %collective-permute-done.refs_2_), channel_id=1, source_target_pairs={{0,192},{32,224},{64,0},{96,32},{128,64},{160,96},{192,128},{224,1... | collective-permute-start | bytes 393224 | tf_op jit(solution)/shard_map/ppermute | solution.py:504

commit v6 on v5

--- a/solution.py
+++ b/solution.py
@@ -270,7 +270,12 @@
             product(odd_ref, 2 * i + 1, odd_acc)
             return carry
 
-        lax.fori_loop(0, PAIRS, step, 0)
+        def steps(i, carry, step=step):
+            for k in range(4):
+                step(4 * i + k, carry)
+            return carry
+
+        lax.fori_loop(0, PAIRS // 4, steps, 0)
         for c in range(QUARTERS):
             some = pl.ds(c * quarter, quarter)
             send_ref[some, pl.ds(h * LANES, LANES)] = done_ref[some, :].astype(BF16)
@@ -378,35 +383,35 @@
     )(lanes)
 
 
-def place_pieces(rows_ref, pieces, out_hbm, wide_ref, sems):
+def place_kernel(owners, *refs):
+    n = len(owners)
+    pieces, (out_hbm, wide_ref, sems) = refs[:n], refs[-3:]
+    place = lax.axis_index("dp")
+    along, upper = lax.div(place, 2), lax.rem(place, 2)
     copies = []
-    for k, piece in enumerate(pieces):
-        wide_ref[k] = piece[...].astype(F32)
-        first = pl.multiple_of(rows_ref[k], CHANS)
+    for k, (back, other) in enumerate(owners):
+        owner = 2 * lax.rem(along + 4 - back, 4) + (1 - upper if other else upper)
+        wide_ref[k] = pieces[k][...].astype(F32)
+        first = pl.multiple_of(owner * CHANS, CHANS)
         copies.append(pltpu.make_async_copy(wide_ref.at[k], out_hbm.at[pl.ds(first, CHANS), :], sems.at[k]))
         copies[-1].start()
-    return copies
-
-
-def place_kernel(n, rows_ref, *refs):
-    pieces, (out_hbm, wide_ref, sems) = refs[:n], refs[-3:]
-    for copy in place_pieces(rows_ref, pieces, out_hbm, wide_ref, sems):
+    for copy in copies:
         copy.wait()
 
 
-def place_rows(rows, pieces, held=()):
-    n = len(pieces)
+def place_rows(owners, pieces, held=()):
+    n = len(owners)
     return pl.pallas_call(
-        lambda *refs: place_kernel(n, *refs),
-        in_specs=[pl.BlockSpec(memory_space=pltpu.SMEM)] + [RESIDENT] * n + [ANY] * len(held),
+        lambda *refs: place_kernel(owners, *refs),
+        in_specs=[RESIDENT] * n + [ANY] * len(held),
         out_specs=ANY,
         out_shape=pltpu.HBM((SEQS * CHANS, LENGTH), F32),
-        input_output_aliases={n + 1: 0} if held else {},
+        input_output_aliases={n: 0} if held else {},
         scratch_shapes=[pltpu.VMEM((n, CHANS, LENGTH), F32), pltpu.SemaphoreType.DMA((n,))],
         compiler_params=params(16),
         cost_estimate=cost(n * CHANS * LENGTH, n * 6 * CHANS * LENGTH),
         name="place_rows_%d" % n,
-    )(jnp.stack(rows).astype(jnp.int32), *pieces, *[hbm(x) for x in held])
+    )(*pieces, *[hbm(x) for x in held])
 
 
 def post_kernel(
@@ -496,14 +501,13 @@
 
     own = filter_gradient(lanes, scale)
     along_x = [[(i, (i + 2 * k) % 8) for i in range(8)] for k in range(1, 4)]
-    before = [(place + 8 - 2 * k) % 8 for k in range(1, 4)]
     other = lax.ppermute(own, "dp", [(i, i ^ 1) for i in range(8)])
     first = [lax.ppermute(own, "dp", pairs) for pairs in along_x]
     gated, grad_proj = post(back.reshape(SEQS, BLOCKS, CHANS, 2 * LANES), proj, cotangent)
     gated, own, other, *first = lax.optimization_barrier((gated, own, other, *first))
     second = [lax.ppermute(other, "dp", pairs) for pairs in along_x]
-    filter_grad = place_rows([r * CHANS for r in [place, place ^ 1] + before], [own, other] + first)
-    filter_grad = place_rows([(r ^ 1) * CHANS for r in before], second, [filter_grad])
+    filter_grad = place_rows([(0, False), (0, True)] + [(k, False) for k in range(1, 4)], [own, other] + first)
+    filter_grad = place_rows([(k, True) for k in range(1, 4)], second, [filter_grad])
     return (gated, grad_proj, filter_grad)
 
 

time: 163 us -> 162 us (level)
  transfers between devices with their start and end apart: 9 -> 9, of which waited for: 4 -> 5; matrix products, arithmetic and copies ran while one was open for 0% -> 0% of each run, Pallas kernels for 21% -> 21%
where the time goes in v6:
time: 162 us; the launch traced here: 159 us
  waiting for transfers between devices  66.4 us (41%)
  Pallas kernels  52 us (32%)
  starting transfers between devices  40.1 us (25%)
    all_to_all x1, waiting for transfers between devices, body(): lax.all_to_all(send.reshape(ROWS, CHANS, 2 * LANES), ('ctx', 'dp'), split...  42.2 us
    all_to_all x1, waiting for transfers between devices, body(): lax.all_to_all(results.reshape(ROWS, CHANS, 2 * LANES), ('dp', 'ctx'), sp...  21.8 us
    pallas_call x1, Pallas kernels, filter_gradient(): pl.pallas_call(lambda *refs: filter_kernel(scale, *refs), grid=(CHANS,),...  18 us
    all_to_all x1, starting transfers between devices, body(): lax.all_to_all(send.reshape(ROWS, CHANS, 2 * LANES), ('ctx', 'dp'), split...  16.7 us
    pallas_call x1, Pallas kernels, convolve(): pl.pallas_call(conv_kernel, in_specs=[ANY, ANY], out_specs=ANY, out_shape...  14.4 us
    pallas_call x1, Pallas kernels, toeplitz_tiles(): pl.pallas_call(tile_kernel, grid=(CHANS,), in_specs=[pl.BlockSpec((CHANS,...  9.22 us
    all_to_all x1, starting transfers between devices, body(): lax.all_to_all(results.reshape(ROWS, CHANS, 2 * LANES), ('dp', 'ctx'), sp...  8.29 us
    ppermute x1, starting transfers between devices, body(): other = lax.ppermute(own, 'dp', [(i, i ^ 1) for i in range(8)])  6.39 us
  transfers between devices with their start and end apart: 9, of which 5 were waited for; matrix products, arithmetic and copies ran while one was open for 0% of the time, Pallas kernels for 21%

profile of v6, /device:TPU:1, one launch (start us, length us, event | category | flops | bytes accessed | tf_op | source)
XLA Modules:
  0.0 159.4 jit_solution(6555992833190784576)
XLA Ops:
  0.6 0.0 copy-start
  0.6 3.5 %gate_products.1 = bf16[32,8,16,256]{3,2,1,0:T(8,128)(2,1)} custom-call(bf16[1,128,12288]{2,1,0:T(8,128)(2,1)} %proj_hbm.3, bf16[1,128,4096]{2,1,0:T(8,128)(2,1)} %grad_hbm.3), custom_call_target="tpu_custom_call" | custom-call | flops 1048576 | bytes 6291456 | tf_op jit(solution)/shard_map/gate_products/pallas_call | solution.py:87
  4.1 16.7 %all-to-all-start = ((bf16[256,16,256]{2,1,0:T(8,128)(2,1)}), bf16[256,16,256]{2,1,0:T(8,128)(2,1)}, u32[]{:S(2)}, u32[]{:S(2)}) async-start(bf16[256,16,256]{2,1,0:T(8,128)(2,1)} %bitcast.4), calls=%async_computation | async-start | bytes 4194304 | tf_op jit(solution)/shard_map/all_to_all | solution.py:492
  20.8 0.0 copy-done
  20.9 9.2 %toeplitz_tiles.1.tile_hbm = bf16[16,4,256,256]{3,2,1,0:T(8,128)(2,1)} custom-call(f32[16,4096]{1,0:T(8,128)S(1)} %constant_dynamic-slice_fusion.filter_ref), custom_call_target="tpu_custom_call" | custom-call | flops 8388608 | bytes 9437184 | tf_op jit(solution)/shard_map/toeplitz_tiles/pallas_call | solution.py:132
  30.1 42.2 %all-to-all-done = bf16[256,16,256]{2,1,0:T(8,128)(2,1)} async-done(((bf16[256,16,256]{2,1,0:T(8,128)(2,1)}), bf16[256,16,256]{2,1,0:T(8,128)(2,1)}, u32[]{:S(2)}, u32[]{:S(2)}) %all-to-all-start) | async-done | bytes 2097184 | tf_op jit(solution)/shard_map/all_to_all | solution.py:492
  72.3 14.4 %convolve.1 = bf16[4096,256]{1,0:T(8,128)(2,1)} custom-call(bf16[4096,256]{1,0:T(8,128)(2,1)} %bitcast.1.lanes_hbm.refs_0_, bf16[16,4,256,256]{3,2,1,0:T(8,128)(2,1)} %toeplitz_tiles.1.tile_hbm), custom_call_target="tpu_custom_call" | custom-call | flops 5368709120 | bytes 20971520 | tf_op jit(solution)/shard_map/convolve/pallas_call | solution.py:291
  86.6 8.3 %all-to-all-start.1 = ((bf16[256,16,256]{2,1,0:T(8,128)(2,1)}), bf16[256,16,256]{2,1,0:T(8,128)(2,1)}, u32[]{:S(2)}, u32[]{:S(2)}) async-start(bf16[256,16,256]{2,1,0:T(8,128)(2,1)} %bitcast.5), calls=%async_computation.1 | async-start | bytes 4194304 | tf_op jit(solution)/shard_map/all_to_all | solution.py:498
  94.9 18.0 %filter_gradient.1.refs_0_ = bf16[16,4096]{1,0:T(8,128)(2,1)S(1)} custom-call(bf16[4096,256]{1,0:T(8,128)(2,1)} %bitcast.1.lanes_hbm.refs_0_), custom_call_target="tpu_custom_call" | custom-call | flops 2415919104 | bytes 5242880 | tf_op jit(solution)/shard_map/filter_gradient/pallas_call | solution.py:366
  113.0 6.4 %collective-permute-start = (bf16[16,4096]{1,0:T(8,128)(2,1)S(1)}, bf16[16,4096]{1,0:T(8,128)(2,1)S(1)}, u32[]{:S(2)}, u32[]{:S(2)}) collective-permute-start(bf16[16,4096]{1,0:T(8,128)(2,1)S(1)} %filter_gradient.1.refs_0_), channel_id=1, source_target_pairs={{0,32},{32,0},{64,96},{96,64},{128,160},{160,128},{192,224},{224,1... | collective-permute-start | bytes 393224 | tf_op jit(solution)/shard_map/ppermute | solution.py:504
  119.4 1.2 collective-permute-start.1
  120.6 2.4 %collective-permute-start.2 = (bf16[16,4096]{1,0:T(8,128)(2,1)S(1)}, bf16[16,4096]{1,0:T(8,128)(2,1)S(1)}, u32[]{:S(2)}, u32[]{:S(2)}) collective-permute-start(bf16[16,4096]{1,0:T(8,128)(2,1)S(1)} %filter_gradient.1.refs_0_), channel_id=1, source_target_pairs={{0,128},{32,160},{64,192},{96,224},{128,0},{160,32},{192,64},{224,... | collective-permute-start | bytes 393224 | tf_op jit(solution)/shard_map/ppermute | solution.py:505
  123.0 1.2 collective-permute-start.3
  124.2 21.8 %all-to-all-done.1 = bf16[256,16,256]{2,1,0:T(8,128)(2,1)} async-done(((bf16[256,16,256]{2,1,0:T(8,128)(2,1)}), bf16[256,16,256]{2,1,0:T(8,128)(2,1)}, u32[]{:S(2)}, u32[]{:S(2)}) %all-to-all-start.1) | async-done | bytes 2097184 | tf_op jit(solution)/shard_map/all_to_all | solution.py:498
  146.0 4.9 %gate_results.1 = (bf16[1,128,4096]{2,1,0:T(8,128)(2,1)}, bf16[1,128,12288]{2,1,0:T(8,128)(2,1)}) custom-call(bf16[8,32,16,256]{3,2,1,0:T(8,128)(2,1)} %bitcast.3.lanes_hbm, bf16[1,128,12288]{2,1,0:T(8,128)(2,1)} %proj_hbm.3, bf16[1,128,4096]{2,1,0:T(8,128)(2,1)} %grad_hbm.3), custom_call_target="tpu_custom_call" | custom-call | flops 2097152 | bytes 14680064 | tf_op jit(solution)/shard_map/gate_results/pallas_call | solution.py:465
  150.8 0.0 collective-permute-done.refs_1_
  150.9 0.0 collective-permute-done.1.refs_2_
  150.9 0.0 collective-permute-done.2.refs_3_
  150.9 0.0 collective-permute-done.3.refs_4_
  150.9 0.4 collective-permute-start.4
  151.3 2.4 %collective-permute-start.5 = (bf16[16,4096]{1,0:T(8,128)(2,1)S(1)}, bf16[16,4096]{1,0:T(8,128)(2,1)S(1)}, u32[]{:S(2)}, u32[]{:S(2)}) collective-permute-start(bf16[16,4096]{1,0:T(8,128)(2,1)S(1)} %collective-permute-done.refs_1_), channel_id=1, source_target_pairs={{0,128},{32,160},{64,192},{96,224},{128,0},{160,32},{192,64},{224,... | collective-permute-start | bytes 393224 | tf_op jit(solution)/shard_map/ppermute | solution.py:508
  153.6 1.2 collective-permute-start.6
  154.8 1.1 place_rows_5.1.refs_3_
  155.9 0.1 collective-permute-done.4.refs_0_
  156.0 1.6 %collective-permute-done.5.refs_1_ = bf16[16,4096]{1,0:T(8,128)(2,1)S(1)} collective-permute-done((bf16[16,4096]{1,0:T(8,128)(2,1)S(1)}, bf16[16,4096]{1,0:T(8,128)(2,1)S(1)}, u32[]{:S(2)}, u32[]{:S(2)}) %collective-permute-start.5) | collective-permute-done | bytes 131104 | tf_op jit(solution)/shard_map/ppermute | solution.py:508
  157.6 0.6 collective-permute-done.6.refs_2_
  158.3 0.9 place_rows_3.1
  (1 shorter events, 0.0 us)
Async XLA Ops:
  0.6 20.2 %copy-start = (f32[128,4096]{1,0:T(8,128)S(1)}, f32[128,4096]{1,0:T(8,128)}, u32[]{:S(2)}) copy-start(f32[128,4096]{1,0:T(8,128)} %param.4) | copy-start | bytes 6291460
  4.1 68.1 %all-to-all-start = ((bf16[256,16,256]{2,1,0:T(8,128)(2,1)}), bf16[256,16,256]{2,1,0:T(8,128)(2,1)}, u32[]{:S(2)}, u32[]{:S(2)}) async-start(bf16[256,16,256]{2,1,0:T(8,128)(2,1)} %bitcast.4), calls=%async_computation | async-start | bytes 4194304 | tf_op jit(solution)/shard_map/all_to_all | solution.py:492
  86.6 59.3 %all-to-all-start.1 = ((bf16[256,16,256]{2,1,0:T(8,128)(2,1)}), bf16[256,16,256]{2,1,0:T(8,128)(2,1)}, u32[]{:S(2)}, u32[]{:S(2)}) async-start(bf16[256,16,256]{2,1,0:T(8,128)(2,1)} %bitcast.5), calls=%async_computation.1 | async-start | bytes 4194304 | tf_op jit(solution)/shard_map/all_to_all | solution.py:498
  113.0 37.9 %collective-permute-start = (bf16[16,4096]{1,0:T(8,128)(2,1)S(1)}, bf16[16,4096]{1,0:T(8,128)(2,1)S(1)}, u32[]{:S(2)}, u32[]{:S(2)}) collective-permute-start(bf16[16,4096]{1,0:T(8,128)(2,1)S(1)} %filter_gradient.1.refs_0_), channel_id=1, source_target_pairs={{0,32},{32,0},{64,96},{96,64},{128,160},{160,128},{192,224},{224,1... | collective-permute-start | bytes 393224 | tf_op jit(solution)/shard_map/ppermute | solution.py:504
  119.4 31.5 %collective-permute-start.1 = (bf16[16,4096]{1,0:T(8,128)(2,1)S(1)}, bf16[16,4096]{1,0:T(8,128)(2,1)S(1)}, u32[]{:S(2)}, u32[]{:S(2)}) collective-permute-start(bf16[16,4096]{1,0:T(8,128)(2,1)S(1)} %filter_gradient.1.refs_0_), channel_id=1, source_target_pairs={{0,64},{32,96},{64,128},{96,160},{128,192},{160,224},{192,0},{224,... | collective-permute-start | bytes 393224 | tf_op jit(solution)/shard_map/ppermute | solution.py:505
  120.6 30.3 %collective-permute-start.2 = (bf16[16,4096]{1,0:T(8,128)(2,1)S(1)}, bf16[16,4096]{1,0:T(8,128)(2,1)S(1)}, u32[]{:S(2)}, u32[]{:S(2)}) collective-permute-start(bf16[16,4096]{1,0:T(8,128)(2,1)S(1)} %filter_gradient.1.refs_0_), channel_id=1, source_target_pairs={{0,128},{32,160},{64,192},{96,224},{128,0},{160,32},{192,64},{224,... | collective-permute-start | bytes 393224 | tf_op jit(solution)/shard_map/ppermute | solution.py:505
  123.0 27.9 %collective-permute-start.3 = (bf16[16,4096]{1,0:T(8,128)(2,1)S(1)}, bf16[16,4096]{1,0:T(8,128)(2,1)S(1)}, u32[]{:S(2)}, u32[]{:S(2)}) collective-permute-start(bf16[16,4096]{1,0:T(8,128)(2,1)S(1)} %filter_gradient.1.refs_0_), channel_id=1, source_target_pairs={{0,192},{32,224},{64,0},{96,32},{128,64},{160,96},{192,128},{224,1... | collective-permute-start | bytes 393224 | tf_op jit(solution)/shard_map/ppermute | solution.py:505
  150.9 5.1 %collective-permute-start.4 = (bf16[16,4096]{1,0:T(8,128)(2,1)S(1)}, bf16[16,4096]{1,0:T(8,128)(2,1)S(1)}, u32[]{:S(2)}, u32[]{:S(2)}) collective-permute-start(bf16[16,4096]{1,0:T(8,128)(2,1)S(1)} %collective-permute-done.refs_1_), channel_id=1, source_target_pairs={{0,64},{32,96},{64,128},{96,160},{128,192},{160,224},{192,0},{224,... | collective-permute-start | bytes 393224 | tf_op jit(solution)/shard_map/ppermute | solution.py:508
  151.3 6.4 %collective-permute-start.5 = (bf16[16,4096]{1,0:T(8,128)(2,1)S(1)}, bf16[16,4096]{1,0:T(8,128)(2,1)S(1)}, u32[]{:S(2)}, u32[]{:S(2)}) collective-permute-start(bf16[16,4096]{1,0:T(8,128)(2,1)S(1)} %collective-permute-done.refs_1_), channel_id=1, source_target_pairs={{0,128},{32,160},{64,192},{96,224},{128,0},{160,32},{192,64},{224,... | collective-permute-start | bytes 393224 | tf_op jit(solution)/shard_map/ppermute | solution.py:508
  153.6 4.6 %collective-permute-start.6 = (bf16[16,4096]{1,0:T(8,128)(2,1)S(1)}, bf16[16,4096]{1,0:T(8,128)(2,1)S(1)}, u32[]{:S(2)}, u32[]{:S(2)}) collective-permute-start(bf16[16,4096]{1,0:T(8,128)(2,1)S(1)} %collective-permute-done.refs_1_), channel_id=1, source_target_pairs={{0,192},{32,224},{64,0},{96,32},{128,64},{160,96},{192,128},{224,1... | collective-permute-start | bytes 393224 | tf_op jit(solution)/shard_map/ppermute | solution.py:508

commit v7 on v6

--- a/solution.py
+++ b/solution.py
@@ -271,11 +271,11 @@
             return carry
 
         def steps(i, carry, step=step):
-            for k in range(4):
-                step(4 * i + k, carry)
+            for k in range(8):
+                step(8 * i + k, carry)
             return carry
 
-        lax.fori_loop(0, PAIRS // 4, steps, 0)
+        lax.fori_loop(0, PAIRS // 8, steps, 0)
         for c in range(QUARTERS):
             some = pl.ds(c * quarter, quarter)
             send_ref[some, pl.ds(h * LANES, LANES)] = done_ref[some, :].astype(BF16)

time: 162 us -> 162 us (level)
  no operation moved by 1% of the time
where the time goes in v7:
time: 162 us; the launch traced here: 159 us
  waiting for transfers between devices  66.4 us (41%)
  Pallas kernels  51.8 us (32%)
  starting transfers between devices  40.3 us (25%)
    all_to_all x1, waiting for transfers between devices, body(): lax.all_to_all(send.reshape(ROWS, CHANS, 2 * LANES), ('ctx', 'dp'), split...  42.2 us
    all_to_all x1, waiting for transfers between devices, body(): lax.all_to_all(results.reshape(ROWS, CHANS, 2 * LANES), ('dp', 'ctx'), sp...  21.8 us
    pallas_call x1, Pallas kernels, filter_gradient(): pl.pallas_call(lambda *refs: filter_kernel(scale, *refs), grid=(CHANS,),...  18 us
    all_to_all x1, starting transfers between devices, body(): lax.all_to_all(send.reshape(ROWS, CHANS, 2 * LANES), ('ctx', 'dp'), split...  16.7 us
    pallas_call x1, Pallas kernels, convolve(): pl.pallas_call(conv_kernel, in_specs=[ANY, ANY], out_specs=ANY, out_shape...  14.2 us
    pallas_call x1, Pallas kernels, toeplitz_tiles(): pl.pallas_call(tile_kernel, grid=(CHANS,), in_specs=[pl.BlockSpec((CHANS,...  9.22 us
    all_to_all x1, starting transfers between devices, body(): lax.all_to_all(results.reshape(ROWS, CHANS, 2 * LANES), ('dp', 'ctx'), sp...  8.45 us
    ppermute x1, starting transfers between devices, body(): other = lax.ppermute(own, 'dp', [(i, i ^ 1) for i in range(8)])  6.45 us
  transfers between devices with their start and end apart: 9, of which 5 were waited for; matrix products, arithmetic and copies ran while one was open for 0% of the time, Pallas kernels for 21%

profile of v7, /device:TPU:1, one launch (start us, length us, event | category | flops | bytes accessed | tf_op | source)
XLA Modules:
  0.0 159.4 jit_solution(2709159850273983115)
XLA Ops:
  0.6 0.0 copy-start
  0.6 3.5 %gate_products.1 = bf16[32,8,16,256]{3,2,1,0:T(8,128)(2,1)} custom-call(bf16[1,128,12288]{2,1,0:T(8,128)(2,1)} %proj_hbm.3, bf16[1,128,4096]{2,1,0:T(8,128)(2,1)} %grad_hbm.3), custom_call_target="tpu_custom_call" | custom-call | flops 1048576 | bytes 6291456 | tf_op jit(solution)/shard_map/gate_products/pallas_call | solution.py:87
  4.1 16.7 %all-to-all-start = ((bf16[256,16,256]{2,1,0:T(8,128)(2,1)}), bf16[256,16,256]{2,1,0:T(8,128)(2,1)}, u32[]{:S(2)}, u32[]{:S(2)}) async-start(bf16[256,16,256]{2,1,0:T(8,128)(2,1)} %bitcast.4), calls=%async_computation | async-start | bytes 4194304 | tf_op jit(solution)/shard_map/all_to_all | solution.py:492
  20.8 0.0 copy-done
  20.9 9.2 %toeplitz_tiles.1.tile_hbm = bf16[16,4,256,256]{3,2,1,0:T(8,128)(2,1)} custom-call(f32[16,4096]{1,0:T(8,128)S(1)} %constant_dynamic-slice_fusion.filter_ref), custom_call_target="tpu_custom_call" | custom-call | flops 8388608 | bytes 9437184 | tf_op jit(solution)/shard_map/toeplitz_tiles/pallas_call | solution.py:132
  30.1 42.2 %all-to-all-done = bf16[256,16,256]{2,1,0:T(8,128)(2,1)} async-done(((bf16[256,16,256]{2,1,0:T(8,128)(2,1)}), bf16[256,16,256]{2,1,0:T(8,128)(2,1)}, u32[]{:S(2)}, u32[]{:S(2)}) %all-to-all-start) | async-done | bytes 2097184 | tf_op jit(solution)/shard_map/all_to_all | solution.py:492
  72.3 14.2 %convolve.1 = bf16[4096,256]{1,0:T(8,128)(2,1)} custom-call(bf16[4096,256]{1,0:T(8,128)(2,1)} %bitcast.1.lanes_hbm.refs_0_, bf16[16,4,256,256]{3,2,1,0:T(8,128)(2,1)} %toeplitz_tiles.1.tile_hbm), custom_call_target="tpu_custom_call" | custom-call | flops 5368709120 | bytes 20971520 | tf_op jit(solution)/shard_map/convolve/pallas_call | solution.py:291
  86.5 8.4 %all-to-all-start.1 = ((bf16[256,16,256]{2,1,0:T(8,128)(2,1)}), bf16[256,16,256]{2,1,0:T(8,128)(2,1)}, u32[]{:S(2)}, u32[]{:S(2)}) async-start(bf16[256,16,256]{2,1,0:T(8,128)(2,1)} %bitcast.5), calls=%async_computation.1 | async-start | bytes 4194304 | tf_op jit(solution)/shard_map/all_to_all | solution.py:498
  94.9 18.0 %filter_gradient.1.refs_0_ = bf16[16,4096]{1,0:T(8,128)(2,1)S(1)} custom-call(bf16[4096,256]{1,0:T(8,128)(2,1)} %bitcast.1.lanes_hbm.refs_0_), custom_call_target="tpu_custom_call" | custom-call | flops 2415919104 | bytes 5242880 | tf_op jit(solution)/shard_map/filter_gradient/pallas_call | solution.py:366
  112.9 6.5 %collective-permute-start = (bf16[16,4096]{1,0:T(8,128)(2,1)S(1)}, bf16[16,4096]{1,0:T(8,128)(2,1)S(1)}, u32[]{:S(2)}, u32[]{:S(2)}) collective-permute-start(bf16[16,4096]{1,0:T(8,128)(2,1)S(1)} %filter_gradient.1.refs_0_), channel_id=1, source_target_pairs={{0,32},{32,0},{64,96},{96,64},{128,160},{160,128},{192,224},{224,1... | collective-permute-start | bytes 393224 | tf_op jit(solution)/shard_map/ppermute | solution.py:504
  119.4 1.2 collective-permute-start.1
  120.6 2.4 %collective-permute-start.2 = (bf16[16,4096]{1,0:T(8,128)(2,1)S(1)}, bf16[16,4096]{1,0:T(8,128)(2,1)S(1)}, u32[]{:S(2)}, u32[]{:S(2)}) collective-permute-start(bf16[16,4096]{1,0:T(8,128)(2,1)S(1)} %filter_gradient.1.refs_0_), channel_id=1, source_target_pairs={{0,128},{32,160},{64,192},{96,224},{128,0},{160,32},{192,64},{224,... | collective-permute-start | bytes 393224 | tf_op jit(solution)/shard_map/ppermute | solution.py:505
  123.0 1.2 collective-permute-start.3
  124.2 21.8 %all-to-all-done.1 = bf16[256,16,256]{2,1,0:T(8,128)(2,1)} async-done(((bf16[256,16,256]{2,1,0:T(8,128)(2,1)}), bf16[256,16,256]{2,1,0:T(8,128)(2,1)}, u32[]{:S(2)}, u32[]{:S(2)}) %all-to-all-start.1) | async-done | bytes 2097184 | tf_op jit(solution)/shard_map/all_to_all | solution.py:498
  146.0 4.9 %gate_results.1 = (bf16[1,128,4096]{2,1,0:T(8,128)(2,1)}, bf16[1,128,12288]{2,1,0:T(8,128)(2,1)}) custom-call(bf16[8,32,16,256]{3,2,1,0:T(8,128)(2,1)} %bitcast.3.lanes_hbm, bf16[1,128,12288]{2,1,0:T(8,128)(2,1)} %proj_hbm.3, bf16[1,128,4096]{2,1,0:T(8,128)(2,1)} %grad_hbm.3), custom_call_target="tpu_custom_call" | custom-call | flops 2097152 | bytes 14680064 | tf_op jit(solution)/shard_map/gate_results/pallas_call | solution.py:465
  150.9 0.0 collective-permute-done.refs_1_
  150.9 0.0 collective-permute-done.1.refs_2_
  150.9 0.0 collective-permute-done.2.refs_3_
  150.9 0.0 collective-permute-done.3.refs_4_
  150.9 0.4 collective-permute-start.4
  151.3 2.4 %collective-permute-start.5 = (bf16[16,4096]{1,0:T(8,128)(2,1)S(1)}, bf16[16,4096]{1,0:T(8,128)(2,1)S(1)}, u32[]{:S(2)}, u32[]{:S(2)}) collective-permute-start(bf16[16,4096]{1,0:T(8,128)(2,1)S(1)} %collective-permute-done.refs_1_), channel_id=1, source_target_pairs={{0,128},{32,160},{64,192},{96,224},{128,0},{160,32},{192,64},{224,... | collective-permute-start | bytes 393224 | tf_op jit(solution)/shard_map/ppermute | solution.py:508
  153.7 1.2 collective-permute-start.6
  154.9 1.1 place_rows_5.1.refs_3_
  156.0 0.1 collective-permute-done.4.refs_0_
  156.0 1.6 %collective-permute-done.5.refs_1_ = bf16[16,4096]{1,0:T(8,128)(2,1)S(1)} collective-permute-done((bf16[16,4096]{1,0:T(8,128)(2,1)S(1)}, bf16[16,4096]{1,0:T(8,128)(2,1)S(1)}, u32[]{:S(2)}, u32[]{:S(2)}) %collective-permute-start.5) | collective-permute-done | bytes 131104 | tf_op jit(solution)/shard_map/ppermute | solution.py:508
  157.7 0.6 collective-permute-done.6.refs_2_
  158.3 0.9 place_rows_3.1
  (1 shorter events, 0.0 us)
Async XLA Ops:
  0.6 20.2 %copy-start = (f32[128,4096]{1,0:T(8,128)S(1)}, f32[128,4096]{1,0:T(8,128)}, u32[]{:S(2)}) copy-start(f32[128,4096]{1,0:T(8,128)} %param.4) | copy-start | bytes 6291460
  4.1 68.1 %all-to-all-start = ((bf16[256,16,256]{2,1,0:T(8,128)(2,1)}), bf16[256,16,256]{2,1,0:T(8,128)(2,1)}, u32[]{:S(2)}, u32[]{:S(2)}) async-start(bf16[256,16,256]{2,1,0:T(8,128)(2,1)} %bitcast.4), calls=%async_computation | async-start | bytes 4194304 | tf_op jit(solution)/shard_map/all_to_all | solution.py:492
  86.5 59.6 %all-to-all-start.1 = ((bf16[256,16,256]{2,1,0:T(8,128)(2,1)}), bf16[256,16,256]{2,1,0:T(8,128)(2,1)}, u32[]{:S(2)}, u32[]{:S(2)}) async-start(bf16[256,16,256]{2,1,0:T(8,128)(2,1)} %bitcast.5), calls=%async_computation.1 | async-start | bytes 4194304 | tf_op jit(solution)/shard_map/all_to_all | solution.py:498
  112.9 37.9 %collective-permute-start = (bf16[16,4096]{1,0:T(8,128)(2,1)S(1)}, bf16[16,4096]{1,0:T(8,128)(2,1)S(1)}, u32[]{:S(2)}, u32[]{:S(2)}) collective-permute-start(bf16[16,4096]{1,0:T(8,128)(2,1)S(1)} %filter_gradient.1.refs_0_), channel_id=1, source_target_pairs={{0,32},{32,0},{64,96},{96,64},{128,160},{160,128},{192,224},{224,1... | collective-permute-start | bytes 393224 | tf_op jit(solution)/shard_map/ppermute | solution.py:504
  119.4 31.5 %collective-permute-start.1 = (bf16[16,4096]{1,0:T(8,128)(2,1)S(1)}, bf16[16,4096]{1,0:T(8,128)(2,1)S(1)}, u32[]{:S(2)}, u32[]{:S(2)}) collective-permute-start(bf16[16,4096]{1,0:T(8,128)(2,1)S(1)} %filter_gradient.1.refs_0_), channel_id=1, source_target_pairs={{0,64},{32,96},{64,128},{96,160},{128,192},{160,224},{192,0},{224,... | collective-permute-start | bytes 393224 | tf_op jit(solution)/shard_map/ppermute | solution.py:505
  120.6 30.3 %collective-permute-start.2 = (bf16[16,4096]{1,0:T(8,128)(2,1)S(1)}, bf16[16,4096]{1,0:T(8,128)(2,1)S(1)}, u32[]{:S(2)}, u32[]{:S(2)}) collective-permute-start(bf16[16,4096]{1,0:T(8,128)(2,1)S(1)} %filter_gradient.1.refs_0_), channel_id=1, source_target_pairs={{0,128},{32,160},{64,192},{96,224},{128,0},{160,32},{192,64},{224,... | collective-permute-start | bytes 393224 | tf_op jit(solution)/shard_map/ppermute | solution.py:505
  123.0 27.9 %collective-permute-start.3 = (bf16[16,4096]{1,0:T(8,128)(2,1)S(1)}, bf16[16,4096]{1,0:T(8,128)(2,1)S(1)}, u32[]{:S(2)}, u32[]{:S(2)}) collective-permute-start(bf16[16,4096]{1,0:T(8,128)(2,1)S(1)} %filter_gradient.1.refs_0_), channel_id=1, source_target_pairs={{0,192},{32,224},{64,0},{96,32},{128,64},{160,96},{192,128},{224,1... | collective-permute-start | bytes 393224 | tf_op jit(solution)/shard_map/ppermute | solution.py:505
  150.9 5.1 %collective-permute-start.4 = (bf16[16,4096]{1,0:T(8,128)(2,1)S(1)}, bf16[16,4096]{1,0:T(8,128)(2,1)S(1)}, u32[]{:S(2)}, u32[]{:S(2)}) collective-permute-start(bf16[16,4096]{1,0:T(8,128)(2,1)S(1)} %collective-permute-done.refs_1_), channel_id=1, source_target_pairs={{0,64},{32,96},{64,128},{96,160},{128,192},{160,224},{192,0},{224,... | collective-permute-start | bytes 393224 | tf_op jit(solution)/shard_map/ppermute | solution.py:508
  151.3 6.4 %collective-permute-start.5 = (bf16[16,4096]{1,0:T(8,128)(2,1)S(1)}, bf16[16,4096]{1,0:T(8,128)(2,1)S(1)}, u32[]{:S(2)}, u32[]{:S(2)}) collective-permute-start(bf16[16,4096]{1,0:T(8,128)(2,1)S(1)} %collective-permute-done.refs_1_), channel_id=1, source_target_pairs={{0,128},{32,160},{64,192},{96,224},{128,0},{160,32},{192,64},{224,... | collective-permute-start | bytes 393224 | tf_op jit(solution)/shard_map/ppermute | solution.py:508
  153.7 4.6 %collective-permute-start.6 = (bf16[16,4096]{1,0:T(8,128)(2,1)S(1)}, bf16[16,4096]{1,0:T(8,128)(2,1)S(1)}, u32[]{:S(2)}, u32[]{:S(2)}) collective-permute-start(bf16[16,4096]{1,0:T(8,128)(2,1)S(1)} %collective-permute-done.refs_1_), channel_id=1, source_target_pairs={{0,192},{32,224},{64,0},{96,32},{128,64},{160,96},{192,128},{224,1... | collective-permute-start | bytes 393224 | tf_op jit(solution)/shard_map/ppermute | solution.py:508
